TPU v7x, 32 devices: a whole 2x2x4 slice. The times are simulated.
32 devices in a mesh: groups: 2 (over y), tile: 8 (over z, x), col: 2 (over core).
Axes of the slice: x: 2, y: 2, z: 4, core: 2. Of those that a mesh axis runs over, the one named last changes fastest.
Arguments:
- jacobian: bfloat16 [512, 3, 128, 512], P(('groups', 'tile'), None, None, 'col'), parts along dimension 0, may hold values from -0.15625 to 0.15625
- footprint: int32 [512, 3], P(('groups', 'tile')), parts along dimension 0, may hold values from 0 to 4, all different within a row
- live: int32 [16], P(('groups', 'tile')), parts along dimension 0, may hold values from 1 to 32, as said below
- noise_weight: float32 [512, 128], P(('groups', 'tile')), parts along dimension 0, may hold values from 0.25 to 4
- probes: bfloat16 [16, 512, 256], P(('groups', 'tile'), 'col'), parts along dimension 0, may hold values from -6 to 6
Outputs:
- basis: float32 [16, 512, 256], P(('groups', 'tile'), 'col'), parts along dimension 0
- factor: float32 [512, 256], P('groups'), parts along dimension 0
There are 2 independent parts, one for each index of `groups`. A program takes and returns all parts, laid end to end along the dimension named above; each array names one. Nothing has to cross between parts.
Inputs may be any that keep to these rules, and one draw needn't show every extreme that they name: `footprint`: each row lists 3 different offsets. Some band has all 32 slots live.
All inputs are finite; a program needn't handle non-finite values.
Results may differ from a plain program's by a relative error of at most 0.0014.
Values may be sent and summed in bfloat16 or wider, within the bound.
No kernel may reach another device: no remote copies, remote signals or barrier semaphores. Data moves between devices by JAX's collectives and lax.ppermute only.
A program may use at most 64 MiB of HBM per device.

v0:
```python
import math

import jax
import jax.numpy as jnp
from jax import lax
from jax.sharding import PartitionSpec as P


def shifted(value, axis, steps):
    count = lax.axis_size(axis)
    pairs = [(source, (source + steps) % count) for source in range(count)]
    return lax.ppermute(value, axis, pairs)


def neighbour(piece, offset):
    return shifted(piece, "tile", offset)


def on_device(jacobian, footprint, live, noise_weight, probes):
    slots, reach, rows, cells = jacobian.shape
    width = probes.shape[2]
    group = math.gcd(slots, 8)
    turns = slots // group
    window = jnp.concatenate(
        [
            neighbour(probes, 2),
            neighbour(probes, 1),
            probes,
            neighbour(probes, -1),
            neighbour(probes, -2),
        ],
        axis=0,
    )
    onehot = footprint[:, :, None] == jnp.arange(5, dtype=jnp.int32)[None, None, :]
    hot_narrow = onehot.astype(jnp.bfloat16).reshape(turns, group, reach, 5)
    hot_wide = onehot.astype(jnp.float32).reshape(turns, group, reach, 5)
    jac_groups = jacobian.reshape(turns, group, reach, rows, cells)

    def forward(carry, inputs):
        jac_part, hot_part = inputs
        picked = jnp.einsum(
            "gfo,ock->gfck", hot_part, window, preferred_element_type=jnp.float32
        ).astype(jnp.bfloat16)
        images = jnp.einsum("gfrc,gfck->grk", jac_part, picked, preferred_element_type=jnp.float32)
        return (carry, images)

    _, partial_value = lax.scan(forward, jnp.zeros((), jnp.float32), (jac_groups, hot_narrow))
    partial_value = partial_value.reshape(slots, rows, width)
    active = (jnp.arange(slots, dtype=jnp.int32) < live[0]).astype(jnp.float32)
    scaling = noise_weight * active[:, None]
    share = lax.psum_scatter(partial_value, "col", scatter_dimension=1, tiled=True)
    half = share.shape[1]
    local_scale = lax.dynamic_slice_in_dim(scaling, lax.axis_index("col") * half, half, 1)
    piece = (share * local_scale[:, :, None]).astype(jnp.bfloat16)
    weighted = lax.all_gather(piece, "col", axis=1, tiled=True)
    weighted_groups = weighted.reshape(turns, group, rows, width)

    def backward(bucket, inputs):
        jac_part, hot_part, weighted_part = inputs
        contrib = jnp.einsum(
            "gfrc,grk->gfck", jac_part, weighted_part, preferred_element_type=jnp.float32
        )
        added = jnp.einsum("gfo,gfck->ock", hot_part, contrib, precision=lax.Precision.HIGHEST)
        return (bucket + added, None)

    bucket, _ = lax.scan(
        backward, jnp.zeros((5, cells, width), jnp.float32), (jac_groups, hot_wide, weighted_groups)
    )
    total = bucket[2]
    for offset in (-2, -1, 1, 2):
        total = total + shifted(bucket[2 + offset], "tile", offset)
    field = probes[0].astype(jnp.float32) + total
    local_gram = jnp.dot(field.T, field, precision=lax.Precision.HIGHEST)
    gram = lax.psum(local_gram, ("tile", "col"))
    lower = jnp.linalg.cholesky(gram)
    states = cells * lax.axis_size("col") * lax.axis_size("tile")
    scale = math.sqrt(states)
    solved = jax.scipy.linalg.solve_triangular(lower, field.T, lower=True)
    basis = (solved.T * scale)[None]
    factor = lower.T / scale
    return (basis, factor)


def solution(mesh):
    placed = (
        P(("groups", "tile"), None, None, "col"),
        P(("groups", "tile"), None),
        P(("groups", "tile")),
        P(("groups", "tile"), None),
        P(("groups", "tile"), "col", None),
    )
    return jax.shard_map(
        on_device,
        mesh=mesh,
        in_specs=placed,
        out_specs=(P(("groups", "tile"), "col", None), P("groups", None)),
        check_vma=False,
    )
```

profile of v0, /device:TPU:0, one launch (start us, length us, event | category | flops | bytes accessed | tf_op | source)
XLA Modules:
  0.0 314.3 jit_solution(8248134718715111169)
XLA Ops:
  11.8 3.2 %collective-permute-start.2 = (bf16[1,256,256]{2,1,0:T(8,128)(2,1)}, bf16[1,256,256]{2,1,0:T(8,128)(2,1)S(1)}, u32[]{:S(2)}, u32[]{:S(2)}) collective-permute-start(bf16[1,256,256]{2,1,0:T(8,128)(2,1)} %param.13), channel_id=1, source_target_pairs={{0,14},{2,0},{4,2},{6,4},{8,6},{10,8},{12,10},{14,12},{1,15},{3,1}... | collective-permute-start | bytes 393224 | tf_op jit(solution)/shard_map/ppermute | solution.py:12
  16.4 4.5 %collective-permute-done.1 = bf16[1,256,256]{2,1,0:T(8,128)(2,1)S(1)} collective-permute-done((bf16[1,256,256]{2,1,0:T(8,128)(2,1)}, bf16[1,256,256]{2,1,0:T(8,128)(2,1)S(1)}, u32[]{:S(2)}, u32[]{:S(2)}) %collective-permute-start.1) | collective-permute-done | bytes 131104 | tf_op jit(solution)/shard_map/ppermute | solution.py:12
  21.9 17.7 %while.22 = (s32[]{:T(128)}, f32[4,8,128,256]{3,2,1,0:T(8,128)}, bf16[4,8,3,128,256]{4,3,2,1,0:T(8,128)(2,1)}, bf16[4,8,3,5]{1,2,3,0:T(4,128)(2,1)S(1)}, bf16[5,256,256]{2,1,0:T(8,128)(2,1)S(1)}, /*index=5*/s32[]{:T(128)}) while((s32[]{:T(128)}, f32[4,8,128,256]{3,2,1,0:T(8,128)}, bf16[4,8,3,128,256]{4,3,2,1,0:T(8,128)(2,1)}, ...), condition=%wide.region_1.2_spmd, body=%wide.region_0.1_spmd.sunk | while | flops 418381824 | bytes 9570073 | solution.py:47
  27.6 3.1 fusion.65
  40.4 11.6 %reduce-scatter.2.cloned.1.call-done = f32[32,64,256]{2,1,0:T(8,128)} async-done(((f32[32,128,256]{2,1,0:T(8,128)}), f32[32,64,256]{2,1,0:T(8,128)}) %reduce-scatter.2.cloned.1.call-update) | async-done | bytes 2097168 | tf_op jit(solution)/shard_map/reduce_scatter | solution.py:51
  54.9 11.9 %all-gather.2.cloned.1.call-done = bf16[32,128,256]{2,1,0:T(8,128)(2,1)} async-done(((bf16[32,64,256]{2,1,0:T(8,128)(2,1)}), bf16[32,128,256]{2,1,0:T(8,128)(2,1)}) %all-gather.2.cloned.1.call-update) | async-done | bytes 2097168 | tf_op jit(solution)/shard_map/all_gather | solution.py:55
  66.9 62.4 %while.24 = (s32[]{:T(128)}, f32[5,256,256]{2,0,1:T(8,128)S(1)}, f32[4,8,3,5]{1,2,3,0:T(4,128)S(1)}, bf16[4,8,3,128,256]{4,3,2,1,0:T(8,128)(2,1)}, bf16[4,8,128,256]{3,2,1,0:T(8,128)(2,1)}, /*index=5*/s32[]{:T(128)}, s32[]{:T(128)}) while((s32[]{:T(128)}, f32[5,256,256]{2,0,1:T(8,128)S(1)}, f32[4,8,3,5]{1,2,3,0:T(4,128)S(1)}, ...), condition=%wide.region_4.5_spmd.clone, body=%wide.region_3.4_spmd.clone.sunk | while | flops 497680384 | bytes 17304060 | solution.py:66
  66.9 5.2 %fusion.71 = f32[8,3,256,256]{3,2,1,0:T(8,128)} fusion(bf16[4,8,3,128,256]{4,3,2,1,0:T(8,128)(2,1)} %get-tuple-element.257, s32[]{:T(128)} %get-tuple-element.247, bf16[4,8,128,256]{3,2,1,0:T(8,128)(2,1)} %get-tuple-element.258), kind=kOutput, calls=%fused_computation.16.clone.1 | convolution fusion | flops 402653184 | bytes 8389632 | tf_op jit(solution)/shard_map/while/body/eval_jaxpr/gfrc,grk->gfck/dot_general | solution.py:60
  72.0 10.4 %bitcast_add_fusion.3 = f32[5,256,256]{2,0,1:T(8,128)S(1)} fusion(f32[5,256,256]{2,0,1:T(8,128)S(1)} %get-tuple-element.248, f32[8,3,256,256]{3,2,1,0:T(8,128)} %fusion.71, pred[]{:T(512)S(6)} %compare.27, f32[8,3,5]{0,1,2:T(4,128)S(1)} %dynamic-slice_bitcast_fusion.5), kind=kOutput, calls=%fused_computation.15.clone.1 | convolution fusion | flops 95027200 | bytes 8913377 | tf_op jit(solution)/shard_map/while/body/eval_jaxpr/gfo,gfck->ock/dot_general | solution.py:63
  82.4 5.2 %fusion.71 = f32[8,3,256,256]{3,2,1,0:T(8,128)} fusion(bf16[4,8,3,128,256]{4,3,2,1,0:T(8,128)(2,1)} %get-tuple-element.257, s32[]{:T(128)} %get-tuple-element.247, bf16[4,8,128,256]{3,2,1,0:T(8,128)(2,1)} %get-tuple-element.258), kind=kOutput, calls=%fused_computation.16.clone.1 | convolution fusion | flops 402653184 | bytes 8389632 | tf_op jit(solution)/shard_map/while/body/eval_jaxpr/gfrc,grk->gfck/dot_general | solution.py:60
  87.6 10.4 %bitcast_add_fusion.3 = f32[5,256,256]{2,0,1:T(8,128)S(1)} fusion(f32[5,256,256]{2,0,1:T(8,128)S(1)} %get-tuple-element.248, f32[8,3,256,256]{3,2,1,0:T(8,128)} %fusion.71, pred[]{:T(512)S(6)} %compare.27, f32[8,3,5]{0,1,2:T(4,128)S(1)} %dynamic-slice_bitcast_fusion.5), kind=kOutput, calls=%fused_computation.15.clone.1 | convolution fusion | flops 95027200 | bytes 8913377 | tf_op jit(solution)/shard_map/while/body/eval_jaxpr/gfo,gfck->ock/dot_general | solution.py:63
  98.0 5.2 %fusion.71 = f32[8,3,256,256]{3,2,1,0:T(8,128)} fusion(bf16[4,8,3,128,256]{4,3,2,1,0:T(8,128)(2,1)} %get-tuple-element.257, s32[]{:T(128)} %get-tuple-element.247, bf16[4,8,128,256]{3,2,1,0:T(8,128)(2,1)} %get-tuple-element.258), kind=kOutput, calls=%fused_computation.16.clone.1 | convolution fusion | flops 402653184 | bytes 8389632 | tf_op jit(solution)/shard_map/while/body/eval_jaxpr/gfrc,grk->gfck/dot_general | solution.py:60
  103.2 10.4 %bitcast_add_fusion.3 = f32[5,256,256]{2,0,1:T(8,128)S(1)} fusion(f32[5,256,256]{2,0,1:T(8,128)S(1)} %get-tuple-element.248, f32[8,3,256,256]{3,2,1,0:T(8,128)} %fusion.71, pred[]{:T(512)S(6)} %compare.27, f32[8,3,5]{0,1,2:T(4,128)S(1)} %dynamic-slice_bitcast_fusion.5), kind=kOutput, calls=%fused_computation.15.clone.1 | convolution fusion | flops 95027200 | bytes 8913377 | tf_op jit(solution)/shard_map/while/body/eval_jaxpr/gfo,gfck->ock/dot_general | solution.py:63
  113.6 5.2 %fusion.71 = f32[8,3,256,256]{3,2,1,0:T(8,128)} fusion(bf16[4,8,3,128,256]{4,3,2,1,0:T(8,128)(2,1)} %get-tuple-element.257, s32[]{:T(128)} %get-tuple-element.247, bf16[4,8,128,256]{3,2,1,0:T(8,128)(2,1)} %get-tuple-element.258), kind=kOutput, calls=%fused_computation.16.clone.1 | convolution fusion | flops 402653184 | bytes 8389632 | tf_op jit(solution)/shard_map/while/body/eval_jaxpr/gfrc,grk->gfck/dot_general | solution.py:60
  118.8 10.4 %bitcast_add_fusion.3 = f32[5,256,256]{2,0,1:T(8,128)S(1)} fusion(f32[5,256,256]{2,0,1:T(8,128)S(1)} %get-tuple-element.248, f32[8,3,256,256]{3,2,1,0:T(8,128)} %fusion.71, pred[]{:T(512)S(6)} %compare.27, f32[8,3,5]{0,1,2:T(4,128)S(1)} %dynamic-slice_bitcast_fusion.5), kind=kOutput, calls=%fused_computation.15.clone.1 | convolution fusion | flops 95027200 | bytes 8913377 | tf_op jit(solution)/shard_map/while/body/eval_jaxpr/gfo,gfck->ock/dot_general | solution.py:63
  130.0 3.6 %collective-permute-start.4 = (f32[256,256]{1,0:T(8,128)S(1)}, f32[256,256]{1,0:T(8,128)S(1)}, u32[]{:S(2)}, u32[]{:S(2)}) collective-permute-start(f32[256,256]{1,0:T(8,128)S(1)} %get-tuple-element.116), channel_id=1, source_target_pairs={{0,12},{2,14},{4,0},{6,2},{8,4},{10,6},{12,8},{14,10},{1,13},{3,15... | collective-permute-start | bytes 786440 | tf_op jit(solution)/shard_map/ppermute | solution.py:12
  135.1 3.5 %collective-permute-start.5 = (f32[256,256]{1,0:T(8,128)S(1)}, f32[256,256]{1,0:T(8,128)S(1)}, u32[]{:S(2)}, u32[]{:S(2)}) collective-permute-start(f32[256,256]{1,0:T(8,128)S(1)} %bitcast.127), channel_id=1, source_target_pairs={{0,14},{2,0},{4,2},{6,4},{8,6},{10,8},{12,10},{14,12},{1,15},{3,1}... | collective-permute-start | bytes 786440 | tf_op jit(solution)/shard_map/ppermute | solution.py:12
  140.3 7.5 %collective-permute-done.6 = f32[256,256]{1,0:T(8,128)S(1)} collective-permute-done((f32[256,256]{1,0:T(8,128)S(1)}, f32[256,256]{1,0:T(8,128)S(1)}, u32[]{:S(2)}, u32[]{:S(2)}) %collective-permute-start.6) | collective-permute-done | bytes 262176 | tf_op jit(solution)/shard_map/ppermute | solution.py:12
  152.4 90.8 %all-reduce.3.cloned.1.call-done = f32[256,256]{0,1:T(8,128)} async-done(((f32[256,256]{0,1:T(8,128)}), f32[256,256]{0,1:T(8,128)}) %all-reduce.3.cloned.1.call-update) | async-done | bytes 262160 | tf_op jit(solution)/shard_map/psum | solution.py:74
  245.3 11.7 %cholesky.50 = f32[128,128]{1,0:T(8,128)S(1)} custom-call(f32[128,128]{1,0:T(8,128)S(1)} %cholesky.118), custom_call_target="Cholesky" | custom-call | tf_op jit(solution)/shard_map/jit(cholesky)/cholesky | solution.py:75
  257.1 9.8 %custom-call.15 = f32[1,128,128]{1,2,0:T(8,128)S(1)} custom-call(f32[1,128,128]{2,1,0:T(8,128)S(1)} %get-tuple-element.124), custom_call_target="InvertDiagBlocksLowerTriangular" | custom-call | tf_op jit(solution)/shard_map/jit(cholesky)/cholesky | solution.py:75
  267.3 11.7 %cholesky.105 = f32[128,128]{1,0:T(8,128)S(1)} custom-call(f32[128,128]{1,0:T(8,128)S(1)} %convolution_subtract_fusion), custom_call_target="Cholesky" | custom-call | tf_op jit(solution)/shard_map/jit(cholesky)/cholesky | solution.py:75
  281.2 4.1 %while.23 = (s32[]{:T(128)}, f32[256,256]{1,0:T(8,128)S(1)}, s32[2,2]{1,0:T(2,128)S(1)}, f32[2,128,128]{2,1,0:T(8,128)S(1)}, s32[]{:T(128)}) while((s32[]{:T(128)}, f32[256,256]{1,0:T(8,128)S(1)}, s32[2,2]{1,0:T(2,128)S(1)}, f32[2,128,128]{2,1,0:T(8,128)S(1)}, s32[]{:T(128)}) %tuple.68), condition=%wide.while_cond, body=%wide.while_body.sunk | while | flops 2 | bytes 131181 | solution.py:78
  285.3 19.7 %custom-call.16 = f32[2,128,128]{1,2,0:T(8,128)S(1)} custom-call(f32[2,128,128]{2,1,0:T(8,128)S(1)} %get-tuple-element.65), custom_call_target="InvertDiagBlocksLowerTriangular" | custom-call | tf_op jit(solution)/shard_map/jit(_solve_triangular)/triangular_solve | solution.py:78
  (80 shorter events, 43.0 us)
Async XLA Ops:
  7.2 44.8 %reduce-scatter.2.cloned.1.call-start = ((), (), s32[]{:S(2)}) async-start(), calls=%async_computation.1 | async-start | bytes 6291456 | tf_op jit(solution)/shard_map/reduce_scatter | solution.py:51
  7.2 9.1 %collective-permute-start = (bf16[1,256,256]{2,1,0:T(8,128)(2,1)}, bf16[1,256,256]{2,1,0:T(8,128)(2,1)S(1)}, u32[]{:S(2)}, u32[]{:S(2)}) collective-permute-start(bf16[1,256,256]{2,1,0:T(8,128)(2,1)} %param.13), channel_id=1, source_target_pairs={{0,4},{2,6},{4,8},{6,10},{8,12},{10,14},{12,0},{14,2},{1,5},{3,7},... | collective-permute-start | bytes 393224 | tf_op jit(solution)/shard_map/ppermute | solution.py:12
  10.3 10.6 %collective-permute-start.1 = (bf16[1,256,256]{2,1,0:T(8,128)(2,1)}, bf16[1,256,256]{2,1,0:T(8,128)(2,1)S(1)}, u32[]{:S(2)}, u32[]{:S(2)}) collective-permute-start(bf16[1,256,256]{2,1,0:T(8,128)(2,1)} %param.13), channel_id=1, source_target_pairs={{0,2},{2,4},{4,6},{6,8},{8,10},{10,12},{12,14},{14,0},{1,3},{3,5},... | collective-permute-start | bytes 393224 | tf_op jit(solution)/shard_map/ppermute | solution.py:12
  11.8 10.0 %collective-permute-start.2 = (bf16[1,256,256]{2,1,0:T(8,128)(2,1)}, bf16[1,256,256]{2,1,0:T(8,128)(2,1)S(1)}, u32[]{:S(2)}, u32[]{:S(2)}) collective-permute-start(bf16[1,256,256]{2,1,0:T(8,128)(2,1)} %param.13), channel_id=1, source_target_pairs={{0,14},{2,0},{4,2},{6,4},{8,6},{10,8},{12,10},{14,12},{1,15},{3,1}... | collective-permute-start | bytes 393224 | tf_op jit(solution)/shard_map/ppermute | solution.py:12
  15.0 6.8 %collective-permute-start.3 = (bf16[1,256,256]{2,1,0:T(8,128)(2,1)}, bf16[1,256,256]{2,1,0:T(8,128)(2,1)S(1)}, u32[]{:S(2)}, u32[]{:S(2)}) collective-permute-start(bf16[1,256,256]{2,1,0:T(8,128)(2,1)} %param.13), channel_id=1, source_target_pairs={{0,12},{2,14},{4,0},{6,2},{8,4},{10,6},{12,8},{14,10},{1,13},{3,15... | collective-permute-start | bytes 393224 | tf_op jit(solution)/shard_map/ppermute | solution.py:12
  39.5 0.7 copy-start.1
  39.6 27.3 %all-gather.2.cloned.1.call-start = ((), (), s32[]{:S(2)}) async-start(), calls=%async_computation.2 | async-start | bytes 3145728 | tf_op jit(solution)/shard_map/all_gather | solution.py:55
  54.8 188.3 %all-reduce.3.cloned.1.call-start = ((), (), s32[]{:S(2)}) async-start(), calls=%async_computation.3 | async-start | bytes 524288 | tf_op jit(solution)/shard_map/psum | solution.py:74
  129.2 21.7 %copy-start = (bf16[1,256,256]{2,1,0:T(8,128)(2,1)S(1)}, bf16[1,256,256]{2,1,0:T(8,128)(2,1)}, u32[]{:S(2)}) copy-start(bf16[1,256,256]{2,1,0:T(8,128)(2,1)} %param.13) | copy-start | bytes 393220
  130.0 10.3 %collective-permute-start.4 = (f32[256,256]{1,0:T(8,128)S(1)}, f32[256,256]{1,0:T(8,128)S(1)}, u32[]{:S(2)}, u32[]{:S(2)}) collective-permute-start(f32[256,256]{1,0:T(8,128)S(1)} %get-tuple-element.116), channel_id=1, source_target_pairs={{0,12},{2,14},{4,0},{6,2},{8,4},{10,6},{12,8},{14,10},{1,13},{3,15... | collective-permute-start | bytes 786440 | tf_op jit(solution)/shard_map/ppermute | solution.py:12
  133.6 14.2 %collective-permute-start.6 = (f32[256,256]{1,0:T(8,128)S(1)}, f32[256,256]{1,0:T(8,128)S(1)}, u32[]{:S(2)}, u32[]{:S(2)}) collective-permute-start(f32[256,256]{1,0:T(8,128)S(1)} %get-tuple-element.118), channel_id=1, source_target_pairs={{0,2},{2,4},{4,6},{6,8},{8,10},{10,12},{12,14},{14,0},{1,3},{3,5},... | collective-permute-start | bytes 786440 | tf_op jit(solution)/shard_map/ppermute | solution.py:12
  135.1 12.7 %collective-permute-start.7 = (f32[256,256]{1,0:T(8,128)S(1)}, f32[256,256]{1,0:T(8,128)S(1)}, u32[]{:S(2)}, u32[]{:S(2)}) collective-permute-start(f32[256,256]{1,0:T(8,128)S(1)} %get-tuple-element.117), channel_id=1, source_target_pairs={{0,4},{2,6},{4,8},{6,10},{8,12},{10,14},{12,0},{14,2},{1,5},{3,7},... | collective-permute-start | bytes 786440 | tf_op jit(solution)/shard_map/ppermute | solution.py:12
  135.1 15.8 %collective-permute-start.5 = (f32[256,256]{1,0:T(8,128)S(1)}, f32[256,256]{1,0:T(8,128)S(1)}, u32[]{:S(2)}, u32[]{:S(2)}) collective-permute-start(f32[256,256]{1,0:T(8,128)S(1)} %bitcast.127), channel_id=1, source_target_pairs={{0,14},{2,0},{4,2},{6,4},{8,6},{10,8},{12,10},{14,12},{1,15},{3,1}... | collective-permute-start | bytes 786440 | tf_op jit(solution)/shard_map/ppermute | solution.py:12
Sparse Core Ops, SparseCore 0:
  39.7 12.1 reduce-scatter.1
  55.0 11.8 all-gather.1
  152.5 90.6 all-reduce.2
where the time goes:
time: 315 us; the launch traced here: 314 us
  waiting for transfers between devices  131 us (42%)
  matrix products  82.6 us (26%)
  other arithmetic  57.8 us (18%)
  starting transfers between devices  16.8 us (5%)
  between operations  15.9 us (5%)
  local copies, waits for them, and re-layouts  9.31 us (3%)
    psum x1, waiting for transfers between devices, on_device(): gram = lax.psum(local_gram, ('tile', 'col'))  90.8 us
    dot_general x4, matrix products, backward(): jnp.einsum('gfo,gfck->ock', hot_part, contrib, precision=lax.Precision.HI...  41.5 us
    another operation x6, other arithmetic, on_device(): lower = jnp.linalg.cholesky(gram)  34 us
    dot_general x4, matrix products, backward(): jnp.einsum('gfrc,grk->gfck', jac_part, weighted_part, preferred_element_t...  20.8 us
    another operation x2, other arithmetic, on_device(): solved = jax.scipy.linalg.solve_triangular(lower, field.T, lower=True)  19.7 us
    ppermute x8, waiting for transfers between devices, shifted(): return lax.ppermute(value, axis, pairs)  17.1 us
    ppermute x8, starting transfers between devices, shifted(): return lax.ppermute(value, axis, pairs)  16.7 us
    dot_general x4, matrix products, forward(): jnp.einsum('gfrc,gfck->grk', jac_part, picked, preferred_element_type=jnp...  12.5 us
  transfers between devices with their start and end apart: 11, of which 8 were waited for; matrix products, arithmetic and copies ran while one was open for 1% of the time, Pallas kernels for 0%

commit v1 on v0

v1 whole, which is shorter than its diff:
```python
import functools
import math

import jax
import jax.numpy as jnp
from jax import lax
from jax.experimental import pallas as pl
from jax.experimental.pallas import tpu as pltpu
from jax.sharding import PartitionSpec as P

F32 = jnp.float32
BF16 = jnp.bfloat16
NN = (((1,), (0,)), ((), ()))
NT = (((1,), (1,)), ((), ()))
OFFSETS = (-2, -1, 0, 1, 2)
PAD = 16
LIMIT = 48 << 20
VMEM = pl.BlockSpec(memory_space=pltpu.VMEM)
SMEM = pl.BlockSpec(memory_space=pltpu.SMEM)
FWD_GROUP = 4
BWD_GROUP = 4
MAX_GROUP = 8


def kernel_call(body, out_shape, in_specs, out_specs, scratch=(), flops=0, nbytes=0):
    return pl.pallas_call(
        body,
        out_shape=out_shape,
        in_specs=in_specs,
        out_specs=out_specs,
        scratch_shapes=list(scratch),
        compiler_params=pltpu.CompilerParams(vmem_limit_bytes=LIMIT),
        cost_estimate=pl.CostEstimate(flops=flops, bytes_accessed=nbytes, transcendentals=0),
    )


def dot(a, b, dims=NN):
    return lax.dot_general(a, b, dims, preferred_element_type=F32)


def halves(a):
    high = a.astype(BF16)
    return high, (a - high.astype(F32)).astype(BF16)


def dot3(a, b, dims=NN):
    a_high, a_low = a
    b_high, b_low = b
    return dot(a_high, b_high, dims) + (dot(a_high, b_low, dims) + dot(a_low, b_high, dims))


def shifted(value, axis, steps):
    count = lax.axis_size(axis)
    pairs = [(source, (source + steps) % count) for source in range(count)]
    return lax.ppermute(value, axis, pairs)


def flipped(value):
    return shifted(value, "col", 1)


def list_kernel(cap, half, footprint, live, core, ids, own, every):
    slots, reach = footprint.shape
    for o in range(len(OFFSETS)):
        every[o] = 0

    def step(j, _):
        slot = lax.rem(j + core[0] * half, slots)
        alive = (slot < live[0]).astype(jnp.int32)
        for f in range(reach):
            o = footprint[slot, f]
            n = every[o]
            ids[o * cap + n] = j * 4 + f
            every[o] = n + alive
        return 0

    lax.fori_loop(0, half, step, 0)
    for o in range(len(OFFSETS)):
        own[o] = every[o]
    lax.fori_loop(half, slots, step, 0)


def forward_kernel(cap, ids, own, core, jac_near, jac_far, *rest):
    near, far = rest[:5], rest[5:10]
    noise, out, window, images = rest[10:]
    half, _, rows, cells = jac_near.shape
    for o in range(len(OFFSETS)):
        window[o, :cells] = near[o][...]
        window[o, cells:] = far[o][...]

    def clear(j, _):
        images[j] = jnp.zeros(images.shape[1:], F32)
        return 0

    lax.fori_loop(0, half, clear, 0)
    for o in range(len(OFFSETS)):
        count = own[o]

        def step(i, _):
            slots, parts = [], []
            for q in range(FWD_GROUP):
                n = i * FWD_GROUP + q
                code = jnp.where(n < count, ids[o * cap + n], half * 4)
                j, f = lax.div(code, 4), lax.rem(code, 4)
                slots.append(j)
                jj = jnp.minimum(j, half - 1)
                parts.append(jnp.concatenate([jac_near[jj, f], jac_far[jj, f]], axis=1))
            product = dot(jnp.concatenate(parts, axis=0), window[o])
            for q in range(FWD_GROUP):
                images[slots[q]] += product[q * rows : (q + 1) * rows]
            return 0

        lax.fori_loop(0, lax.div(count + FWD_GROUP - 1, FWD_GROUP), step, 0)

    def finish(j, _):
        scale = noise[pl.ds(core[0] * half + j, 1), :]
        out[j] = (images[j].T * scale).astype(BF16)
        return 0

    lax.fori_loop(0, half, finish, 0)


def gather_kernel(mine, other, out):
    half = mine.shape[0]

    def step(j, _):
        out[j] = mine[j]
        out[half + j] = other[j]
        return 0

    lax.fori_loop(0, half, step, 0)
    out[2 * half] = jnp.zeros(out.shape[1:], BF16)


def backward_kernel(o, cap, ids, every, jac, weighted, out, total):
    slots = jac.shape[0]
    width = weighted.shape[1]
    count = every[o]
    total[...] = jnp.zeros_like(total)

    def step(i, _):
        left, right = [], []
        for q in range(BWD_GROUP):
            n = i * BWD_GROUP + q
            code = jnp.where(n < count, ids[o * cap + n], slots * 4)
            j, f = lax.div(code, 4), lax.rem(code, 4)
            left.append(weighted[j])
            right.append(jac[jnp.minimum(j, slots - 1), f])
        total[...] += dot(jnp.concatenate(left, axis=1), jnp.concatenate(right, axis=0))
        return 0

    lax.fori_loop(0, lax.div(count + BWD_GROUP - 1, BWD_GROUP), step, 0)
    value = total[...]
    if OFFSETS[o] == 0:
        out[...] = value
        return
    top = jnp.max(jnp.abs(value), axis=0, keepdims=True)
    power = jnp.clip(jnp.floor(jnp.log2(jnp.maximum(top, 1e-30))) + 1.0, -96.0, 96.0)
    coded = jnp.clip(jnp.round(value * jnp.exp2(15.0 - power)), -32767.0, 32767.0)
    out[:width] = coded.astype(jnp.int32).astype(jnp.int16)
    rows = jnp.broadcast_to(power.astype(jnp.int32), (PAD, power.shape[1]))
    out[width:] = rows.astype(jnp.int16)


def field_kernel(core, probes, own, *rest):
    parts, (field, keep, send) = rest[:4], rest[4:]
    width = own.shape[0]
    total = probes[...].astype(F32).T + own[...]
    for part in parts:
        power = part[width:].astype(jnp.int32).astype(F32)[:1]
        total = total + part[:width].astype(jnp.int32).astype(F32) * jnp.exp2(power - 15.0)
    field[...] = total
    both = halves(total)
    gram = dot3(both, both, NT)
    mid, quarter = width // 2, width // 4
    lower = [gram[:mid, :mid], gram[mid : mid + quarter, :mid]]
    upper = [gram[mid:, mid:], gram[mid + quarter :, :mid]]
    first = core[0] == 0
    low, high = jnp.concatenate(lower, axis=0), jnp.concatenate(upper, axis=0)
    keep[...] = jnp.where(first, low, high)
    send[...] = jnp.where(first, high, low)


def finish_kernel(scale, rounds, core, mine, other, field, basis, factor, gram, inverse, a_high, a_low):
    width = gram.shape[0]
    mid, quarter = width // 2, width // 4
    first = core[0] == 0
    low = jnp.where(first, mine[...], other[...])
    high = jnp.where(first, other[...], mine[...])
    corner = jnp.concatenate([low[mid:], high[mid:]], axis=0)
    gram[:mid, :mid] = low[:mid]
    gram[mid:, mid:] = high[:mid]
    gram[mid:, :mid] = corner
    gram[:mid, mid:] = corner.T
    matrix = gram[...]
    row = lax.broadcasted_iota(jnp.int32, matrix.shape, 0)
    column = lax.broadcasted_iota(jnp.int32, matrix.shape, 1)
    eye = (row == column).astype(F32)
    diagonal = matrix * eye
    down = lax.rsqrt(jnp.sum(diagonal, axis=1, keepdims=True))
    along = lax.rsqrt(jnp.sum(diagonal, axis=0, keepdims=True))
    unit = matrix * down * along
    parts = halves(unit)
    a_high[...], a_low[...] = parts

    def correction(error):
        return jnp.where(row > column, error, 0.5 * eye * error).astype(BF16)

    now = (eye - jnp.where(row > column, unit, 0.0)).astype(BF16)
    for _ in range(rounds):
        error = dot(dot(now, a_high[...]).astype(BF16), now, NT) - eye
        now = (now.astype(F32) - dot(correction(error), now)).astype(BF16)
    exact = now.astype(F32)
    applied = dot(now, a_high[...]) + dot(now, a_low[...])
    applied_high, applied_low = halves(applied)
    error = dot(applied_high, now, NT) + dot(applied_low, now, NT) - eye
    exact = exact - dot(correction(error), now)
    full = halves(exact)
    error = dot3(halves(dot3(full, (a_high[...], a_low[...]))), full, NT) - eye
    inverse[...] = (exact - dot(correction(error), full[0])) * along
    left = jnp.sum(error * error)

    @pl.when(jnp.logical_not(left < 1e-4))
    def _():
        inverse[...] = eye
        across = lax.broadcasted_iota(jnp.int32, (1, width), 1)
        down_at = lax.broadcasted_iota(jnp.int32, (width, 1), 0)

        def eliminate(k, _):
            pivot_row = gram[pl.ds(k, 1), :]
            pivot = jnp.sum(jnp.where(across == k, pivot_row, 0.0), axis=1, keepdims=True)
            scaled = pivot_row * lax.rsqrt(pivot)
            now = gram[...]
            below = jnp.sum(jnp.where(column == k, now, 0.0), axis=1, keepdims=True)
            below = jnp.where(down_at > k, below * lax.rsqrt(pivot), 0.0)
            done = inverse[pl.ds(k, 1), :] * lax.rsqrt(pivot)
            gram[...] = now - below * scaled
            inverse[...] = inverse[...] - below * done
            inverse[pl.ds(k, 1), :] = done
            return 0

        lax.fori_loop(0, width, eliminate, 0)

    solved = halves(inverse[...])
    upper = dot3(solved, halves(matrix)) * (1.0 / scale)
    factor[...] = jnp.where(row <= column, upper, 0.0)
    basis[...] = (dot3(solved, halves(field[...])) * scale).T


def all_reduced(value):
    count = lax.axis_size("tile")
    if count & (count - 1):
        return lax.psum(value, "tile")
    mask = 1
    while mask < count:
        jump = mask if mask < 4 else mask + mask // 2
        value = value + lax.ppermute(value, "tile", [(i, i ^ jump) for i in range(count)])
        mask *= 2
    return value


def on_device(jacobian, footprint, live, noise_weight, probes):
    slots, reach, rows, cells = jacobian.shape
    width = probes.shape[2]
    half = slots // lax.axis_size("col")
    cap = slots + MAX_GROUP
    core = lax.axis_index("col").astype(jnp.int32).reshape(1)
    mine = probes[0]

    near = [mine if offset == 0 else shifted(mine, "tile", -offset) for offset in OFFSETS]
    far = [flipped(piece) for piece in near]
    start = core[0] * half
    own_share = lax.dynamic_slice_in_dim(jacobian, start, half, 0)
    other_share = lax.dynamic_slice_in_dim(jacobian, half - start, half, 0)
    jac_far = flipped(other_share)
    jac_all = jnp.concatenate([own_share, other_share], axis=0)

    def smem(n):
        return jax.ShapeDtypeStruct((n,), jnp.int32)

    ids, own, every = kernel_call(
        functools.partial(list_kernel, cap, half),
        (smem(len(OFFSETS) * cap), smem(len(OFFSETS)), smem(len(OFFSETS))),
        [SMEM] * 3,
        (SMEM,) * 3,
    )(footprint, live, core)

    share = 2 * half * reach * rows * 2 * cells * width
    weighted = kernel_call(
        functools.partial(forward_kernel, cap),
        jax.ShapeDtypeStruct((half, width, rows), BF16),
        [SMEM] * 3 + [VMEM] * 13,
        VMEM,
        [pltpu.VMEM((len(OFFSETS), 2 * cells, width), BF16), pltpu.VMEM((half + 1, rows, width), F32)],
        flops=share,
    )(ids, own, core, own_share, jac_far, *near, *far, noise_weight)
    weighted = kernel_call(
        gather_kernel,
        jax.ShapeDtypeStruct((2 * half + 1, width, rows), BF16),
        [VMEM] * 2,
        VMEM,
    )(weighted, flipped(weighted))

    def bucket(o):
        if OFFSETS[o] == 0:
            shape = jax.ShapeDtypeStruct((width, cells), F32)
        else:
            shape = jax.ShapeDtypeStruct((width + PAD, cells), jnp.int16)
        return kernel_call(
            functools.partial(backward_kernel, o, cap),
            shape,
            [SMEM] * 2 + [VMEM] * 2,
            VMEM,
            [pltpu.VMEM((width, cells), F32)],
            flops=share // len(OFFSETS),
        )(ids, every, jac_all, weighted)

    arrived = [shifted(bucket(o), "tile", OFFSETS[o]) for o in (0, 4, 1, 3)]
    packed = jax.ShapeDtypeStruct((3 * width // 4, width // 2), F32)
    field, keep, send = kernel_call(
        field_kernel,
        (jax.ShapeDtypeStruct((width, cells), F32), packed, packed),
        [SMEM] + [VMEM] * 6,
        (VMEM,) * 3,
    )(core, mine, bucket(2), *arrived)
    summed = all_reduced(keep + flipped(send))
    scale = math.sqrt(cells * lax.axis_size("col") * lax.axis_size("tile"))
    square = jax.ShapeDtypeStruct((width, width), F32)
    basis, factor = kernel_call(
        functools.partial(finish_kernel, scale, 2),
        (jax.ShapeDtypeStruct((cells, width), F32), square),
        [SMEM] + [VMEM] * 3,
        (VMEM,) * 2,
        [pltpu.VMEM((width, width), F32)] * 2 + [pltpu.VMEM((width, width), BF16)] * 2,
    )(core, summed, flipped(summed), field)
    return (basis[None], factor)


def solution(mesh):
    placed = (
        P(("groups", "tile"), None, None, "col"),
        P(("groups", "tile"), None),
        P(("groups", "tile")),
        P(("groups", "tile"), None),
        P(("groups", "tile"), "col", None),
    )
    return jax.shard_map(
        on_device,
        mesh=mesh,
        in_specs=placed,
        out_specs=(P(("groups", "tile"), "col", None), P("groups", None)),
        check_vma=False,
    )
```

time: 315 us -> 131 us (0.42)
  waiting for transfers between devices: 131 us -> 28.6 us
  matrix products: 82.6 us -> 0 us
  Pallas kernels: 0 us -> 70.4 us
  other arithmetic: 57.8 us -> 5.14 us
  between operations: 15.9 us -> 1.48 us
    psum x1 -> x0, waiting for transfers between devices: 90.8 us -> none  [on_device(): gram = lax.psum(local_gram, ('tile', 'col'))]
    dot_general x17 -> x0, matrix products: 81.2 us -> none  [the longest x4 41.5 us: backward(): jnp.einsum('gfo,gfck->ock', hot_part, contrib, precision=lax.Precision.HI...]
    pallas_call x0 -> x10, Pallas kernels: none -> 70.4 us  [the longest x1 41.1 us: on_device(): kernel_call(functools.partial(finish_kernel, scale, 2), (jax.ShapeDtypeSt...]
    another operation x8 -> x0, other arithmetic: 53.7 us -> none  [the longest x6 34 us: on_device(): lower = jnp.linalg.cholesky(gram)]
    ppermute x0 -> x3, waiting for transfers between devices: none -> 14.2 us  [all_reduced(): lax.ppermute(value, 'tile', [(i, i ^ jump) for i in range(count)])]
    all_gather x1 -> x0, waiting for transfers between devices: 11.9 us -> none  [on_device(): weighted = lax.all_gather(piece, 'col', axis=1, tiled=True)]
    reduce_scatter x1 -> x0, waiting for transfers between devices: 11.6 us -> none  [on_device(): lax.psum_scatter(partial_value, 'col', scatter_dimension=1, tiled=True)]
    dynamic_slice x0 -> x1, local copies, waits for them, and re-layouts: none -> 5.23 us  [on_device(): own_share = lax.dynamic_slice_in_dim(jacobian, start, half, 0)]
  transfers between devices with their start and end apart: 11 -> 20, of which waited for: 8 -> 11; matrix products, arithmetic and copies ran while one was open for 1% -> 4% of each run, Pallas kernels for 0% -> 4%
where the time goes in v1:
time: 131 us
  Pallas kernels  70.4 us (54%)
  waiting for transfers between devices  28.6 us (22%)
  starting transfers between devices  18.5 us (14%)
  local copies, waits for them, and re-layouts  6.71 us (5%)
  other arithmetic  5.14 us (4%)
  between operations  1.48 us (1%)
    pallas_call x1, Pallas kernels, on_device(): kernel_call(functools.partial(finish_kernel, scale, 2), (jax.ShapeDtypeSt...  41.1 us
    pallas_call x5, Pallas kernels, bucket(): kernel_call(functools.partial(backward_kernel, o, cap), shape, [SMEM] * 2...  18.3 us
    ppermute x17, starting transfers between devices, shifted(): return lax.ppermute(value, axis, pairs)  16.6 us
    ppermute x17, waiting for transfers between devices, shifted(): return lax.ppermute(value, axis, pairs)  14.4 us
    ppermute x3, waiting for transfers between devices, all_reduced(): lax.ppermute(value, 'tile', [(i, i ^ jump) for i in range(count)])  14.2 us
    pallas_call x1, Pallas kernels, on_device(): kernel_call(functools.partial(forward_kernel, cap), jax.ShapeDtypeStruct(...  8.21 us
    dynamic_slice x1, local copies, waits for them, and re-layouts, on_device(): own_share = lax.dynamic_slice_in_dim(jacobian, start, half, 0)  5.23 us
    concatenate x1, other arithmetic, on_device(): jac_all = jnp.concatenate([own_share, other_share], axis=0)  5.09 us
  transfers between devices with their start and end apart: 20, of which 11 were waited for; matrix products, arithmetic and copies ran while one was open for 4% of the time, Pallas kernels for 4%

profile of v1, /device:TPU:0, one launch (start us, length us, event | category | flops | bytes accessed | tf_op | source)
XLA Modules:
  0.0 130.8 jit_solution(14651381447294707906)
XLA Ops:
  0.6 5.2 %constant_dynamic-slice_fusion.1 = (bf16[16,3,128,256]{3,2,1,0:T(8,128)(2,1)S(1)}, bf16[16,3,128,256]{3,2,1,0:T(8,128)(2,1)}) fusion(bf16[32,3,128,256]{3,2,1,0:T(8,128)(2,1)} %param.5, s32[]{:T(128)S(6)} %select_n.6, s32[]{:T(128)S(6)} %select_n.7), kind=kLoop, calls=%fused_computation.2 | loop fusion | bytes 12582920 | tf_op jit(solution)/shard_map/dynamic_slice | solution.py:273
  6.4 5.0 %collective-permute-start.4 = (bf16[256,256]{1,0:T(8,128)(2,1)S(1)}, bf16[256,256]{1,0:T(8,128)(2,1)S(1)}, u32[]{:S(2)}, u32[]{:S(2)}) collective-permute-start(bf16[256,256]{1,0:T(8,128)(2,1)S(1)} %bitcast.4), channel_id=1, source_target_pairs={{0,12},{2,14},{4,0},{6,2},{8,4},{10,6},{12,8},{14,10},{1,13},{3,15... | collective-permute-start | bytes 393224 | tf_op jit(solution)/shard_map/ppermute | solution.py:55
  11.4 1.4 %collective-permute-start.3 = (bf16[256,256]{1,0:T(8,128)(2,1)S(1)}, bf16[256,256]{1,0:T(8,128)(2,1)}, u32[]{:S(2)}, u32[]{:S(2)}) collective-permute-start(bf16[256,256]{1,0:T(8,128)(2,1)S(1)} %bitcast.5), channel_id=1, source_target_pairs={{0,14},{2,0},{4,2},{6,4},{8,6},{10,8},{12,10},{14,12},{1,15},{3,1}... | collective-permute-start | bytes 393224 | tf_op jit(solution)/shard_map/ppermute | solution.py:55
  15.3 2.8 %collective-permute-done.3.rest_3_ = bf16[256,256]{1,0:T(8,128)(2,1)} collective-permute-done((bf16[256,256]{1,0:T(8,128)(2,1)S(1)}, bf16[256,256]{1,0:T(8,128)(2,1)}, u32[]{:S(2)}, u32[]{:S(2)}) %collective-permute-start.3) | collective-permute-done | bytes 131104 | tf_op jit(solution)/shard_map/ppermute | solution.py:55
  18.1 3.7 %collective-permute-done.2.rest_1_ = bf16[256,256]{1,0:T(8,128)(2,1)} collective-permute-done((bf16[256,256]{1,0:T(8,128)(2,1)S(1)}, bf16[256,256]{1,0:T(8,128)(2,1)}, u32[]{:S(2)}, u32[]{:S(2)}) %collective-permute-start.2) | collective-permute-done | bytes 131104 | tf_op jit(solution)/shard_map/ppermute | solution.py:55
  23.8 2.2 %shard_map.68 = (s32[200]{0:T(256)S(1)}, s32[5]{0:T(128)S(1)}, s32[5]{0:T(128)S(1)}) custom-call(s32[32,3]{1,0:T(8,128)S(1)} %copy.7.footprint, s32[1]{0:T(128)S(6)} %copy.8.live, s32[1]{0:T(128)} %bitcast.core), custom_call_target="tpu_custom_call" | custom-call | tf_op jit(solution)/shard_map/pallas_call | solution.py:281
  26.8 8.2 %shard_map.69.mine = bf16[16,256,128]{2,1,0:T(8,128)(2,1)S(1)} custom-call(s32[200]{0:T(256)S(1)} %get-tuple-element.10.ids, s32[5]{0:T(128)S(1)} %get-tuple-element.12.own, s32[1]{0:T(128)} %bitcast.core, bf16[16,3,128,256]{3,2,1,0:T(8,128)(2,1)S(1)} %get-tuple-element.18.jac_near, bf16[16,3,128,256]{3,2,1,0:T(8,128)(2,1)} %collective-permute-done.jac_far, ...), custom_call_target="tpu_custom_call" | custom-call | flops 1610612736 | tf_op jit(solution)/shard_map/pallas_call | solution.py:289
  35.1 5.1 %pad_maximum_fusion.jac = bf16[32,3,128,256]{3,2,1,0:T(8,128)(2,1)} fusion(bf16[16,3,128,256]{3,2,1,0:T(8,128)(2,1)} %get-tuple-element.19, bf16[16,3,128,256]{3,2,1,0:T(8,128)(2,1)S(1)} %get-tuple-element.18.jac_near), kind=kLoop, calls=%fused_computation | loop fusion | flops 3145728 | bytes 12582912 | tf_op jit(solution)/shard_map/concatenate | solution.py:276
  40.4 3.9 %shard_map.75 = s16[272,256]{1,0:T(8,128)(2,1)S(1)} custom-call(s32[200]{0:T(256)S(1)} %get-tuple-element.10.ids, s32[5]{0:T(128)S(1)} %get-tuple-element.11.every, bf16[32,3,128,256]{3,2,1,0:T(8,128)(2,1)} %pad_maximum_fusion.jac, bf16[33,256,128]{2,1,0:T(8,128)(2,1)S(1)} %shard_map.70.weighted), custom_call_target="tpu_custom_call" | custom-call | flops 322122560 | tf_op jit(solution)/shard_map/pallas_call | solution.py:309
  44.2 3.6 %shard_map.74 = s16[272,256]{1,0:T(8,128)(2,1)S(1)} custom-call(s32[200]{0:T(256)S(1)} %get-tuple-element.10.ids, s32[5]{0:T(128)S(1)} %get-tuple-element.11.every, bf16[32,3,128,256]{3,2,1,0:T(8,128)(2,1)} %pad_maximum_fusion.jac, bf16[33,256,128]{2,1,0:T(8,128)(2,1)S(1)} %shard_map.70.weighted), custom_call_target="tpu_custom_call" | custom-call | flops 322122560 | tf_op jit(solution)/shard_map/pallas_call | solution.py:309
  47.9 3.6 %shard_map.73 = s16[272,256]{1,0:T(8,128)(2,1)S(1)} custom-call(s32[200]{0:T(256)S(1)} %get-tuple-element.10.ids, s32[5]{0:T(128)S(1)} %get-tuple-element.11.every, bf16[32,3,128,256]{3,2,1,0:T(8,128)(2,1)} %pad_maximum_fusion.jac, bf16[33,256,128]{2,1,0:T(8,128)(2,1)S(1)} %shard_map.70.weighted), custom_call_target="tpu_custom_call" | custom-call | flops 322122560 | tf_op jit(solution)/shard_map/pallas_call | solution.py:309
  51.5 3.6 %shard_map.72 = s16[272,256]{1,0:T(8,128)(2,1)S(1)} custom-call(s32[200]{0:T(256)S(1)} %get-tuple-element.10.ids, s32[5]{0:T(128)S(1)} %get-tuple-element.11.every, bf16[32,3,128,256]{3,2,1,0:T(8,128)(2,1)} %pad_maximum_fusion.jac, bf16[33,256,128]{2,1,0:T(8,128)(2,1)S(1)} %shard_map.70.weighted), custom_call_target="tpu_custom_call" | custom-call | flops 322122560 | tf_op jit(solution)/shard_map/pallas_call | solution.py:309
  55.1 3.0 %collective-permute-start.11 = (s16[272,256]{1,0:T(8,128)(2,1)S(1)}, s16[272,256]{1,0:T(8,128)(2,1)S(1)}, u32[]{:S(2)}, u32[]{:S(2)}) collective-permute-start(s16[272,256]{1,0:T(8,128)(2,1)S(1)} %shard_map.72), channel_id=1, source_target_pairs={{0,12},{2,14},{4,0},{6,2},{8,4},{10,6},{12,8},{14,10},{1,13},{3,15... | collective-permute-start | bytes 417800 | tf_op jit(solution)/shard_map/ppermute | solution.py:55
  58.1 4.4 %collective-permute-start.13 = (s16[272,256]{1,0:T(8,128)(2,1)S(1)}, s16[272,256]{1,0:T(8,128)(2,1)S(1)}, u32[]{:S(2)}, u32[]{:S(2)}) collective-permute-start(s16[272,256]{1,0:T(8,128)(2,1)S(1)} %shard_map.74), channel_id=1, source_target_pairs={{0,14},{2,0},{4,2},{6,4},{8,6},{10,8},{12,10},{14,12},{1,15},{3,1}... | collective-permute-start | bytes 417800 | tf_op jit(solution)/shard_map/ppermute | solution.py:55
  62.5 3.6 %shard_map.71.own = f32[256,256]{1,0:T(8,128)S(1)} custom-call(s32[200]{0:T(256)S(1)} %get-tuple-element.10.ids, s32[5]{0:T(128)S(1)} %get-tuple-element.11.every, bf16[32,3,128,256]{3,2,1,0:T(8,128)(2,1)} %pad_maximum_fusion.jac, bf16[33,256,128]{2,1,0:T(8,128)(2,1)S(1)} %shard_map.70.weighted), custom_call_target="tpu_custom_call" | custom-call | flops 322122560 | tf_op jit(solution)/shard_map/pallas_call | solution.py:309
  66.5 1.3 collective-permute-done.13.rest_2_
  67.7 2.7 %collective-permute-done.14.rest_3_ = s16[272,256]{1,0:T(8,128)(2,1)S(1)} collective-permute-done((s16[272,256]{1,0:T(8,128)(2,1)S(1)}, s16[272,256]{1,0:T(8,128)(2,1)S(1)}, u32[]{:S(2)}, u32[]{:S(2)}) %collective-permute-start.14) | collective-permute-done | bytes 139296 | tf_op jit(solution)/shard_map/ppermute | solution.py:55
  70.9 1.3 collective-permute-done.15
  72.3 4.8 %collective-permute-done.16 = f32[192,128]{1,0:T(8,128)S(1)} collective-permute-done((f32[192,128]{1,0:T(8,128)S(1)}, f32[192,128]{1,0:T(8,128)S(1)}, u32[]{:S(2)}, u32[]{:S(2)}) %collective-permute-start.16) | collective-permute-done | bytes 98336 | tf_op jit(solution)/shard_map/ppermute | solution.py:257
  77.6 4.3 %collective-permute-done.17 = f32[192,128]{1,0:T(8,128)S(1)} collective-permute-done((f32[192,128]{1,0:T(8,128)S(1)}, f32[192,128]{1,0:T(8,128)S(1)}, u32[]{:S(2)}, u32[]{:S(2)}) %collective-permute-start.17) | collective-permute-done | bytes 98336 | tf_op jit(solution)/shard_map/ppermute | solution.py:257
  81.9 1.4 %collective-permute-start.18 = (f32[192,128]{1,0:T(8,128)S(1)}, f32[192,128]{1,0:T(8,128)S(1)}, u32[]{:S(2)}, u32[]{:S(2)}) collective-permute-start(f32[192,128]{1,0:T(8,128)S(1)} %add.23), channel_id=1, source_target_pairs={{0,12},{2,14},{4,8},{6,10},{8,4},{10,6},{12,0},{14,2},{1,13},{3,15... | collective-permute-start | bytes 294920 | tf_op jit(solution)/shard_map/ppermute | solution.py:257
  83.3 5.1 %collective-permute-done.18 = f32[192,128]{1,0:T(8,128)S(1)} collective-permute-done((f32[192,128]{1,0:T(8,128)S(1)}, f32[192,128]{1,0:T(8,128)S(1)}, u32[]{:S(2)}, u32[]{:S(2)}) %collective-permute-start.18) | collective-permute-done | bytes 98336 | tf_op jit(solution)/shard_map/ppermute | solution.py:257
  88.5 1.3 collective-permute-done.19.other
  89.7 41.1 %shard_map.77 = (f32[256,256]{1,0:T(8,128)}, f32[256,256]{1,0:T(8,128)}) custom-call(s32[1]{0:T(128)} %bitcast.core, f32[192,128]{1,0:T(8,128)S(1)} %add.24.mine, f32[192,128]{1,0:T(8,128)S(1)} %collective-permute-done.19.other, f32[256,256]{1,0:T(8,128)S(1)} %get-tuple-element.15.field), custom_call_target="tpu_custom_call" | custom-call | tf_op jit(solution)/shard_map/pallas_call | solution.py:329
  (37 shorter events, 6.8 us)
Async XLA Ops:
  0.6 5.7 %copy-start = (bf16[1,256,256]{2,1,0:T(8,128)(2,1)S(1)}, bf16[1,256,256]{2,1,0:T(8,128)(2,1)}, u32[]{:S(2)}) copy-start(bf16[1,256,256]{2,1,0:T(8,128)(2,1)} %param.9) | copy-start | bytes 393220
  5.9 20.2 %collective-permute-start = (bf16[16,3,128,256]{3,2,1,0:T(8,128)(2,1)}, bf16[16,3,128,256]{3,2,1,0:T(8,128)(2,1)}, u32[]{:S(2)}, u32[]{:S(2)}) collective-permute-start(bf16[16,3,128,256]{3,2,1,0:T(8,128)(2,1)} %get-tuple-element.19), channel_id=1, source_target_pairs={{0,1},{1,0},{2,3},{3,2},{4,5},{5,4},{6,7},{7,6},{8,9},{9,8},{10,11... | collective-permute-start | bytes 9437192 | tf_op jit(solution)/shard_map/ppermute | solution.py:55
  6.3 7.1 %collective-permute-start.7 = (bf16[256,256]{1,0:T(8,128)(2,1)S(1)}, bf16[256,256]{1,0:T(8,128)(2,1)S(1)}, u32[]{:S(2)}, u32[]{:S(2)}) collective-permute-start(bf16[256,256]{1,0:T(8,128)(2,1)S(1)} %bitcast.3), channel_id=1, source_target_pairs={{0,1},{1,0},{2,3},{3,2},{4,5},{5,4},{6,7},{7,6},{8,9},{9,8},{10,11... | collective-permute-start | bytes 393224 | tf_op jit(solution)/shard_map/ppermute | solution.py:55
  6.4 8.9 %collective-permute-start.4 = (bf16[256,256]{1,0:T(8,128)(2,1)S(1)}, bf16[256,256]{1,0:T(8,128)(2,1)S(1)}, u32[]{:S(2)}, u32[]{:S(2)}) collective-permute-start(bf16[256,256]{1,0:T(8,128)(2,1)S(1)} %bitcast.4), channel_id=1, source_target_pairs={{0,12},{2,14},{4,0},{6,2},{8,4},{10,6},{12,8},{14,10},{1,13},{3,15... | collective-permute-start | bytes 393224 | tf_op jit(solution)/shard_map/ppermute | solution.py:55
  11.4 6.7 %collective-permute-start.3 = (bf16[256,256]{1,0:T(8,128)(2,1)S(1)}, bf16[256,256]{1,0:T(8,128)(2,1)}, u32[]{:S(2)}, u32[]{:S(2)}) collective-permute-start(bf16[256,256]{1,0:T(8,128)(2,1)S(1)} %bitcast.5), channel_id=1, source_target_pairs={{0,14},{2,0},{4,2},{6,4},{8,6},{10,8},{12,10},{14,12},{1,15},{3,1}... | collective-permute-start | bytes 393224 | tf_op jit(solution)/shard_map/ppermute | solution.py:55
  12.8 9.1 %collective-permute-start.2 = (bf16[256,256]{1,0:T(8,128)(2,1)S(1)}, bf16[256,256]{1,0:T(8,128)(2,1)}, u32[]{:S(2)}, u32[]{:S(2)}) collective-permute-start(bf16[256,256]{1,0:T(8,128)(2,1)S(1)} %bitcast.6), channel_id=1, source_target_pairs={{0,2},{2,4},{4,6},{6,8},{8,10},{10,12},{12,14},{14,0},{1,3},{3,5},... | collective-permute-start | bytes 393224 | tf_op jit(solution)/shard_map/ppermute | solution.py:55
  13.5 8.4 %collective-permute-start.1 = (bf16[256,256]{1,0:T(8,128)(2,1)S(1)}, bf16[256,256]{1,0:T(8,128)(2,1)}, u32[]{:S(2)}, u32[]{:S(2)}) collective-permute-start(bf16[256,256]{1,0:T(8,128)(2,1)S(1)} %bitcast.7), channel_id=1, source_target_pairs={{0,4},{2,6},{4,8},{6,10},{8,12},{10,14},{12,0},{14,2},{1,5},{3,7},... | collective-permute-start | bytes 393224 | tf_op jit(solution)/shard_map/ppermute | solution.py:55
  15.3 10.7 %collective-permute-start.9 = (bf16[256,256]{1,0:T(8,128)(2,1)S(1)}, bf16[256,256]{1,0:T(8,128)(2,1)}, u32[]{:S(2)}, u32[]{:S(2)}) collective-permute-start(bf16[256,256]{1,0:T(8,128)(2,1)S(1)} %collective-permute-done.4.rest_4_), channel_id=1, source_target_pairs={{0,1},{1,0},{2,3},{3,2},{4,5},{5,4},{6,7},{7,6},{8,9},{9,8},{10,11... | collective-permute-start | bytes 393224 | tf_op jit(solution)/shard_map/ppermute | solution.py:55
  18.1 7.9 %collective-permute-start.8 = (bf16[256,256]{1,0:T(8,128)(2,1)}, bf16[256,256]{1,0:T(8,128)(2,1)}, u32[]{:S(2)}, u32[]{:S(2)}) collective-permute-start(bf16[256,256]{1,0:T(8,128)(2,1)} %collective-permute-done.3.rest_3_), channel_id=1, source_target_pairs={{0,1},{1,0},{2,3},{3,2},{4,5},{5,4},{6,7},{7,6},{8,9},{9,8},{10,11... | collective-permute-start | bytes 393224 | tf_op jit(solution)/shard_map/ppermute | solution.py:55
  21.9 4.2 %collective-permute-start.6 = (bf16[256,256]{1,0:T(8,128)(2,1)}, bf16[256,256]{1,0:T(8,128)(2,1)}, u32[]{:S(2)}, u32[]{:S(2)}) collective-permute-start(bf16[256,256]{1,0:T(8,128)(2,1)} %collective-permute-done.2.rest_1_), channel_id=1, source_target_pairs={{0,1},{1,0},{2,3},{3,2},{4,5},{5,4},{6,7},{7,6},{8,9},{9,8},{10,11... | collective-permute-start | bytes 393224 | tf_op jit(solution)/shard_map/ppermute | solution.py:55
  21.9 4.2 %collective-permute-start.5 = (bf16[256,256]{1,0:T(8,128)(2,1)}, bf16[256,256]{1,0:T(8,128)(2,1)}, u32[]{:S(2)}, u32[]{:S(2)}) collective-permute-start(bf16[256,256]{1,0:T(8,128)(2,1)} %collective-permute-done.1.rest_0_), channel_id=1, source_target_pairs={{0,1},{1,0},{2,3},{3,2},{4,5},{5,4},{6,7},{7,6},{8,9},{9,8},{10,11... | collective-permute-start | bytes 393224 | tf_op jit(solution)/shard_map/ppermute | solution.py:55
  26.1 0.7 copy-start.1
  35.0 5.2 %collective-permute-start.10 = (bf16[16,256,128]{2,1,0:T(8,128)(2,1)S(1)}, bf16[16,256,128]{2,1,0:T(8,128)(2,1)S(1)}, u32[]{:S(2)}, u32[]{:S(2)}) collective-permute-start(bf16[16,256,128]{2,1,0:T(8,128)(2,1)S(1)} %shard_map.69.mine), channel_id=1, source_target_pairs={{0,1},{1,0},{2,3},{3,2},{4,5},{5,4},{6,7},{7,6},{8,9},{9,8},{10,11... | collective-permute-start | bytes 3145736 | tf_op jit(solution)/shard_map/ppermute | solution.py:55
  55.1 11.0 %collective-permute-start.11 = (s16[272,256]{1,0:T(8,128)(2,1)S(1)}, s16[272,256]{1,0:T(8,128)(2,1)S(1)}, u32[]{:S(2)}, u32[]{:S(2)}) collective-permute-start(s16[272,256]{1,0:T(8,128)(2,1)S(1)} %shard_map.72), channel_id=1, source_target_pairs={{0,12},{2,14},{4,0},{6,2},{8,4},{10,6},{12,8},{14,10},{1,13},{3,15... | collective-permute-start | bytes 417800 | tf_op jit(solution)/shard_map/ppermute | solution.py:55
  58.1 8.4 %collective-permute-start.12 = (s16[272,256]{1,0:T(8,128)(2,1)S(1)}, s16[272,256]{1,0:T(8,128)(2,1)S(1)}, u32[]{:S(2)}, u32[]{:S(2)}) collective-permute-start(s16[272,256]{1,0:T(8,128)(2,1)S(1)} %shard_map.73), channel_id=1, source_target_pairs={{0,4},{2,6},{4,8},{6,10},{8,12},{10,14},{12,0},{14,2},{1,5},{3,7},... | collective-permute-start | bytes 417800 | tf_op jit(solution)/shard_map/ppermute | solution.py:55
  58.1 9.6 %collective-permute-start.13 = (s16[272,256]{1,0:T(8,128)(2,1)S(1)}, s16[272,256]{1,0:T(8,128)(2,1)S(1)}, u32[]{:S(2)}, u32[]{:S(2)}) collective-permute-start(s16[272,256]{1,0:T(8,128)(2,1)S(1)} %shard_map.74), channel_id=1, source_target_pairs={{0,14},{2,0},{4,2},{6,4},{8,6},{10,8},{12,10},{14,12},{1,15},{3,1}... | collective-permute-start | bytes 417800 | tf_op jit(solution)/shard_map/ppermute | solution.py:55
  62.5 7.9 %collective-permute-start.14 = (s16[272,256]{1,0:T(8,128)(2,1)S(1)}, s16[272,256]{1,0:T(8,128)(2,1)S(1)}, u32[]{:S(2)}, u32[]{:S(2)}) collective-permute-start(s16[272,256]{1,0:T(8,128)(2,1)S(1)} %shard_map.75), channel_id=1, source_target_pairs={{0,2},{2,4},{4,6},{6,8},{8,10},{10,12},{12,14},{14,0},{1,3},{3,5},... | collective-permute-start | bytes 417800 | tf_op jit(solution)/shard_map/ppermute | solution.py:55
  70.9 1.4 %collective-permute-start.15 = (f32[192,128]{1,0:T(8,128)S(1)}, f32[192,128]{1,0:T(8,128)S(1)}, u32[]{:S(2)}, u32[]{:S(2)}) collective-permute-start(f32[192,128]{1,0:T(8,128)S(1)} %get-tuple-element.14), channel_id=1, source_target_pairs={{0,1},{1,0},{2,3},{3,2},{4,5},{5,4},{6,7},{7,6},{8,9},{9,8},{10,11... | collective-permute-start | bytes 294920 | tf_op jit(solution)/shard_map/ppermute | solution.py:55
  72.2 4.9 %collective-permute-start.16 = (f32[192,128]{1,0:T(8,128)S(1)}, f32[192,128]{1,0:T(8,128)S(1)}, u32[]{:S(2)}, u32[]{:S(2)}) collective-permute-start(f32[192,128]{1,0:T(8,128)S(1)} %add.21), channel_id=1, source_target_pairs={{0,2},{2,0},{4,6},{6,4},{8,10},{10,8},{12,14},{14,12},{1,3},{3,1},... | collective-permute-start | bytes 294920 | tf_op jit(solution)/shard_map/ppermute | solution.py:257
  77.2 4.7 %collective-permute-start.17 = (f32[192,128]{1,0:T(8,128)S(1)}, f32[192,128]{1,0:T(8,128)S(1)}, u32[]{:S(2)}, u32[]{:S(2)}) collective-permute-start(f32[192,128]{1,0:T(8,128)S(1)} %add.22), channel_id=1, source_target_pairs={{0,4},{2,6},{4,0},{6,2},{8,12},{10,14},{12,8},{14,10},{1,5},{3,7},... | collective-permute-start | bytes 294920 | tf_op jit(solution)/shard_map/ppermute | solution.py:257
  81.9 6.5 %collective-permute-start.18 = (f32[192,128]{1,0:T(8,128)S(1)}, f32[192,128]{1,0:T(8,128)S(1)}, u32[]{:S(2)}, u32[]{:S(2)}) collective-permute-start(f32[192,128]{1,0:T(8,128)S(1)} %add.23), channel_id=1, source_target_pairs={{0,12},{2,14},{4,8},{6,10},{8,4},{10,6},{12,0},{14,2},{1,13},{3,15... | collective-permute-start | bytes 294920 | tf_op jit(solution)/shard_map/ppermute | solution.py:257
  88.4 1.4 %collective-permute-start.19 = (f32[192,128]{1,0:T(8,128)S(1)}, f32[192,128]{1,0:T(8,128)S(1)}, u32[]{:S(2)}, u32[]{:S(2)}) collective-permute-start(f32[192,128]{1,0:T(8,128)S(1)} %add.24.mine), channel_id=1, source_target_pairs={{0,1},{1,0},{2,3},{3,2},{4,5},{5,4},{6,7},{7,6},{8,9},{9,8},{10,11... | collective-permute-start | bytes 294920 | tf_op jit(solution)/shard_map/ppermute | solution.py:55

commit v2 on v1

--- a/solution.py
+++ b/solution.py
@@ -14,7 +14,7 @@
 NT = (((1,), (1,)), ((), ()))
 OFFSETS = (-2, -1, 0, 1, 2)
 PAD = 16
-LIMIT = 48 << 20
+LIMIT = 24 << 20
 VMEM = pl.BlockSpec(memory_space=pltpu.VMEM)
 SMEM = pl.BlockSpec(memory_space=pltpu.SMEM)
 FWD_GROUP = 4
@@ -59,6 +59,28 @@
     return shifted(value, "col", 1)
 
 
+def swapped(value):
+    return lax.ppermute(value, "tile", [(i, i ^ 1) for i in range(lax.axis_size("tile"))])
+
+
+def spread(value, steps):
+    count = lax.axis_size("tile")
+    return lax.ppermute(value, "tile", [(i, (i + (steps, -steps)[i % 2]) % count) for i in range(count)])
+
+
+ROLES = ("own", "back", "ahead", "partner", "beyond")
+
+
+def place_of(role, parity):
+    return {
+        "own": 2,
+        "back": 4 - 4 * parity,
+        "ahead": 4 * parity,
+        "partner": 3 - 2 * parity,
+        "beyond": 1 + 2 * parity,
+    }[role]
+
+
 def list_kernel(cap, half, footprint, live, core, ids, own, every):
     slots, reach = footprint.shape
     for o in range(len(OFFSETS)):
@@ -83,10 +105,13 @@
 def forward_kernel(cap, ids, own, core, jac_near, jac_far, *rest):
     near, far = rest[:5], rest[5:10]
     noise, out, window, images = rest[10:]
-    half, _, rows, cells = jac_near.shape
-    for o in range(len(OFFSETS)):
-        window[o, :cells] = near[o][...]
-        window[o, cells:] = far[o][...]
+    half = out.shape[0]
+    _, _, rows, cells = jac_near.shape
+    base = core[0] * half
+    for i, role in enumerate(ROLES):
+        o = place_of(role, core[1])
+        window[o, :cells] = near[i][...]
+        window[o, cells:] = far[i][...]
 
     def clear(j, _):
         images[j] = jnp.zeros(images.shape[1:], F32)
@@ -103,7 +128,7 @@
                 code = jnp.where(n < count, ids[o * cap + n], half * 4)
                 j, f = lax.div(code, 4), lax.rem(code, 4)
                 slots.append(j)
-                jj = jnp.minimum(j, half - 1)
+                jj = base + jnp.minimum(j, half - 1)
                 parts.append(jnp.concatenate([jac_near[jj, f], jac_far[jj, f]], axis=1))
             product = dot(jnp.concatenate(parts, axis=0), window[o])
             for q in range(FWD_GROUP):
@@ -113,7 +138,7 @@
         lax.fori_loop(0, lax.div(count + FWD_GROUP - 1, FWD_GROUP), step, 0)
 
     def finish(j, _):
-        scale = noise[pl.ds(core[0] * half + j, 1), :]
+        scale = noise[pl.ds(base + j, 1), :]
         out[j] = (images[j].T * scale).astype(BF16)
         return 0
 
@@ -132,9 +157,26 @@
     out[2 * half] = jnp.zeros(out.shape[1:], BF16)
 
 
-def backward_kernel(o, cap, ids, every, jac, weighted, out, total):
+def encode(value, out):
+    width = value.shape[0]
+    top = jnp.max(jnp.abs(value), axis=0, keepdims=True)
+    power = jnp.clip(jnp.floor(jnp.log2(jnp.maximum(top, 1e-30))) + 1.0, -96.0, 96.0)
+    coded = jnp.clip(jnp.round(value * jnp.exp2(15.0 - power)), -32767.0, 32767.0)
+    out[:width] = coded.astype(jnp.int32).astype(jnp.int16)
+    rows = jnp.broadcast_to(power.astype(jnp.int32), (PAD, power.shape[1]))
+    out[width:] = rows.astype(jnp.int16)
+
+
+def decode(part):
+    width = part.shape[0] - PAD
+    power = part[width:].astype(jnp.int32).astype(F32)[:1]
+    return part[:width].astype(jnp.int32).astype(F32) * jnp.exp2(power - 15.0)
+
+
+def backward_kernel(role, coded, cap, ids, every, core, jac, weighted, out, total):
     slots = jac.shape[0]
-    width = weighted.shape[1]
+    half = slots // 2
+    o = place_of(role, core[1])
     count = every[o]
     total[...] = jnp.zeros_like(total)
 
@@ -145,30 +187,27 @@
             code = jnp.where(n < count, ids[o * cap + n], slots * 4)
             j, f = lax.div(code, 4), lax.rem(code, 4)
             left.append(weighted[j])
-            right.append(jac[jnp.minimum(j, slots - 1), f])
+            right.append(jac[lax.rem(j + core[0] * half, slots), f])
         total[...] += dot(jnp.concatenate(left, axis=1), jnp.concatenate(right, axis=0))
         return 0
 
     lax.fori_loop(0, lax.div(count + BWD_GROUP - 1, BWD_GROUP), step, 0)
-    value = total[...]
-    if OFFSETS[o] == 0:
-        out[...] = value
-        return
-    top = jnp.max(jnp.abs(value), axis=0, keepdims=True)
-    power = jnp.clip(jnp.floor(jnp.log2(jnp.maximum(top, 1e-30))) + 1.0, -96.0, 96.0)
-    coded = jnp.clip(jnp.round(value * jnp.exp2(15.0 - power)), -32767.0, 32767.0)
-    out[:width] = coded.astype(jnp.int32).astype(jnp.int16)
-    rows = jnp.broadcast_to(power.astype(jnp.int32), (PAD, power.shape[1]))
-    out[width:] = rows.astype(jnp.int16)
+    if coded:
+        encode(total[...], out)
+    else:
+        out[...] = total[...]
+
+
+def merge_kernel(value, part, out):
+    encode(value[...] + decode(part), out)
 
 
 def field_kernel(core, probes, own, *rest):
-    parts, (field, keep, send) = rest[:4], rest[4:]
+    parts, (field, keep, send) = rest[:3], rest[3:]
     width = own.shape[0]
     total = probes[...].astype(F32).T + own[...]
     for part in parts:
-        power = part[width:].astype(jnp.int32).astype(F32)[:1]
-        total = total + part[:width].astype(jnp.int32).astype(F32) * jnp.exp2(power - 15.0)
+        total = total + decode(part)
     field[...] = total
     both = halves(total)
     gram = dot3(both, both, NT)
@@ -248,14 +287,19 @@
 
 
 def all_reduced(value):
-    count = lax.axis_size("tile")
+    count, cols = lax.axis_size("tile"), lax.axis_size("col")
     if count & (count - 1):
         return lax.psum(value, "tile")
-    mask = 1
-    while mask < count:
-        jump = mask if mask < 4 else mask + mask // 2
-        value = value + lax.ppermute(value, "tile", [(i, i ^ jump) for i in range(count)])
-        mask *= 2
+    jumps = []
+    for bit in range(count.bit_length() - 1):
+        jumps.append(1 << bit if bit < 2 else 3 << (bit - 1))
+    for step, jump in enumerate(jumps):
+        other = jumps[1 - step] if step < 2 and len(jumps) > 1 else jump
+        pairs = []
+        for i in range(count):
+            for c in range(cols):
+                pairs.append((i * cols + c, (i ^ (jump, other)[c % 2]) * cols + c))
+        value = value + lax.ppermute(value, ("tile", "col"), pairs)
     return value
 
 
@@ -264,16 +308,9 @@
     width = probes.shape[2]
     half = slots // lax.axis_size("col")
     cap = slots + MAX_GROUP
-    core = lax.axis_index("col").astype(jnp.int32).reshape(1)
+    col = lax.axis_index("col").astype(jnp.int32)
+    core = jnp.stack([col, lax.rem(lax.axis_index("tile").astype(jnp.int32), 2)])
     mine = probes[0]
-
-    near = [mine if offset == 0 else shifted(mine, "tile", -offset) for offset in OFFSETS]
-    far = [flipped(piece) for piece in near]
-    start = core[0] * half
-    own_share = lax.dynamic_slice_in_dim(jacobian, start, half, 0)
-    other_share = lax.dynamic_slice_in_dim(jacobian, half - start, half, 0)
-    jac_far = flipped(other_share)
-    jac_all = jnp.concatenate([own_share, other_share], axis=0)
 
     def smem(n):
         return jax.ShapeDtypeStruct((n,), jnp.int32)
@@ -284,6 +321,12 @@
         [SMEM] * 3,
         (SMEM,) * 3,
     )(footprint, live, core)
+
+    back, ahead = spread(mine, -2), spread(mine, 2)
+    near = [mine, back, ahead, swapped(mine), swapped(back)]
+    near[4], ids = lax.optimization_barrier((near[4], ids))
+    far = [flipped(piece) for piece in near]
+    jac_far = flipped(jacobian)
 
     share = 2 * half * reach * rows * 2 * cells * width
     weighted = kernel_call(
@@ -293,7 +336,7 @@
         VMEM,
         [pltpu.VMEM((len(OFFSETS), 2 * cells, width), BF16), pltpu.VMEM((half + 1, rows, width), F32)],
         flops=share,
-    )(ids, own, core, own_share, jac_far, *near, *far, noise_weight)
+    )(ids, own, core, jacobian, jac_far, *near, *far, noise_weight)
     weighted = kernel_call(
         gather_kernel,
         jax.ShapeDtypeStruct((2 * half + 1, width, rows), BF16),
@@ -301,28 +344,30 @@
         VMEM,
     )(weighted, flipped(weighted))
 
-    def bucket(o):
-        if OFFSETS[o] == 0:
-            shape = jax.ShapeDtypeStruct((width, cells), F32)
-        else:
-            shape = jax.ShapeDtypeStruct((width + PAD, cells), jnp.int16)
+    plain = jax.ShapeDtypeStruct((width, cells), F32)
+    message = jax.ShapeDtypeStruct((width + PAD, cells), jnp.int16)
+
+    def bucket(role, coded):
         return kernel_call(
-            functools.partial(backward_kernel, o, cap),
-            shape,
-            [SMEM] * 2 + [VMEM] * 2,
+            functools.partial(backward_kernel, role, coded, cap),
+            message if coded else plain,
+            [SMEM] * 3 + [VMEM] * 2,
             VMEM,
             [pltpu.VMEM((width, cells), F32)],
-            flops=share // len(OFFSETS),
-        )(ids, every, jac_all, weighted)
-
-    arrived = [shifted(bucket(o), "tile", OFFSETS[o]) for o in (0, 4, 1, 3)]
+        )(ids, every, core, jacobian, weighted)
+
+    beyond = swapped(bucket("beyond", True))
+    ahead = spread(bucket("ahead", True), -2)
+    partner = swapped(bucket("partner", True))
+    back = kernel_call(merge_kernel, message, [VMEM] * 2, VMEM)(bucket("back", False), beyond)
+    arrived = [ahead, partner, spread(back, 2)]
     packed = jax.ShapeDtypeStruct((3 * width // 4, width // 2), F32)
     field, keep, send = kernel_call(
         field_kernel,
-        (jax.ShapeDtypeStruct((width, cells), F32), packed, packed),
-        [SMEM] + [VMEM] * 6,
+        (plain, packed, packed),
+        [SMEM] + [VMEM] * 5,
         (VMEM,) * 3,
-    )(core, mine, bucket(2), *arrived)
+    )(core, mine, bucket("own", False), *arrived)
     summed = all_reduced(keep + flipped(send))
     scale = math.sqrt(cells * lax.axis_size("col") * lax.axis_size("tile"))
     square = jax.ShapeDtypeStruct((width, width), F32)

time: 131 us -> 114 us (0.87); the launches traced: 131 us -> 112 us
  Pallas kernels: 70.4 us -> 62 us
  other arithmetic: 5.14 us -> 0.13 us
  waiting for transfers between devices: 28.6 us -> 26.3 us
  local copies, waits for them, and re-layouts: 6.71 us -> 5.17 us
  starting transfers between devices: 18.5 us -> 17.1 us
    ppermute x17 -> x9, starting transfers between devices: 16.6 us -> 1.9 us  [shifted(): return lax.ppermute(value, axis, pairs)]
    ppermute x3 -> x11, starting transfers between devices: 1.87 us -> 15.2 us  [the longest x4 8.4 us: spread(): lax.ppermute(value, 'tile', [(i, (i + (steps, -steps)[i % 2]) % count) fo...]
    pallas_call x6 -> x7, Pallas kernels: 18.7 us -> 8.96 us  [the longest x5 7.92 us: bucket(): kernel_call(functools.partial(backward_kernel, role, coded, cap), message...]
    ppermute x17 -> x9, waiting for transfers between devices: 14.4 us -> 6.49 us  [shifted(): return lax.ppermute(value, axis, pairs)]
    ppermute x3 -> x11, waiting for transfers between devices: 14.2 us -> 19.9 us  [the longest x3 11.2 us: all_reduced(): value = value + lax.ppermute(value, ('tile', 'col'), pairs)]
    dynamic_slice x1 -> x0, local copies, waits for them, and re-layouts: 5.23 us -> none  [on_device(): own_share = lax.dynamic_slice_in_dim(jacobian, start, half, 0)]
    concatenate x1 -> x0, other arithmetic: 5.09 us -> none  [on_device(): jac_all = jnp.concatenate([own_share, other_share], axis=0)]
    unnamed x5 -> x9, local copies, waits for them, and re-layouts: 1.48 us -> 5.17 us
  transfers between devices with their start and end apart: 20 -> 20, of which waited for: 11 -> 13; matrix products, arithmetic and copies ran while one was open for 4% -> 1% of each run, Pallas kernels for 4% -> 8%
where the time goes in v2:
time: 114 us; the launch traced here: 112 us
  Pallas kernels  62 us (54%)
  waiting for transfers between devices  26.3 us (23%)
  starting transfers between devices  17.1 us (15%)
  local copies, waits for them, and re-layouts  5.17 us (5%)
  between operations  1.44 us (1%)
    pallas_call x1, Pallas kernels, on_device(): kernel_call(functools.partial(finish_kernel, scale, 2), (jax.ShapeDtypeSt...  41.6 us
    ppermute x3, waiting for transfers between devices, all_reduced(): value = value + lax.ppermute(value, ('tile', 'col'), pairs)  11.2 us
    pallas_call x1, Pallas kernels, on_device(): kernel_call(functools.partial(forward_kernel, cap), jax.ShapeDtypeStruct(...  9.07 us
    ppermute x4, starting transfers between devices, spread(): lax.ppermute(value, 'tile', [(i, (i + (steps, -steps)[i % 2]) % count) fo...  8.4 us
    pallas_call x5, Pallas kernels, bucket(): kernel_call(functools.partial(backward_kernel, role, coded, cap), message...  7.92 us
    ppermute x4, waiting for transfers between devices, spread(): lax.ppermute(value, 'tile', [(i, (i + (steps, -steps)[i % 2]) % count) fo...  7.63 us
    ppermute x9, waiting for transfers between devices, shifted(): return lax.ppermute(value, axis, pairs)  6.49 us
    unnamed x9, local copies, waits for them, and re-layouts  5.17 us
  transfers between devices with their start and end apart: 20, of which 13 were waited for; matrix products, arithmetic and copies ran while one was open for 1% of the time, Pallas kernels for 8%

profile of v2, /device:TPU:0, one launch (start us, length us, event | category | flops | bytes accessed | tf_op | source)
XLA Modules:
  0.0 112.3 jit_solution(9386274611762090106)
XLA Ops:
  1.1 4.7 %collective-permute-start = (bf16[256,256]{1,0:T(8,128)(2,1)}, bf16[256,256]{1,0:T(8,128)(2,1)S(1)}, u32[]{:S(2)}, u32[]{:S(2)}) collective-permute-start(bf16[256,256]{1,0:T(8,128)(2,1)} %bitcast.4), channel_id=1, source_target_pairs={{0,12},{2,6},{4,0},{6,10},{8,4},{10,14},{12,8},{14,2},{1,13},{3,7}... | collective-permute-start | bytes 393224 | tf_op jit(solution)/shard_map/ppermute | solution.py:68
  6.9 3.1 %collective-permute-done.rest_1_ = bf16[256,256]{1,0:T(8,128)(2,1)S(1)} collective-permute-done((bf16[256,256]{1,0:T(8,128)(2,1)}, bf16[256,256]{1,0:T(8,128)(2,1)S(1)}, u32[]{:S(2)}, u32[]{:S(2)}) %collective-permute-start) | collective-permute-done | bytes 131104 | tf_op jit(solution)/shard_map/ppermute | solution.py:68
  10.0 2.1 %collective-permute-start.1 = (bf16[256,256]{1,0:T(8,128)(2,1)S(1)}, bf16[256,256]{1,0:T(8,128)(2,1)S(1)}, u32[]{:S(2)}, u32[]{:S(2)}) collective-permute-start(bf16[256,256]{1,0:T(8,128)(2,1)S(1)} %collective-permute-done.rest_1_), channel_id=1, source_target_pairs={{0,2},{2,0},{4,6},{6,4},{8,10},{10,8},{12,14},{14,12},{1,3},{3,1},... | collective-permute-start | bytes 393224 | tf_op jit(solution)/shard_map/ppermute | solution.py:63
  13.5 2.2 %shard_map.68 = (s32[200]{0:T(256)S(1)}, s32[5]{0:T(128)S(1)}, s32[5]{0:T(128)S(1)}) custom-call(s32[32,3]{1,0:T(8,128)S(1)} %copy.7.footprint, s32[1]{0:T(128)S(6)} %copy.8.live, s32[2]{0:T(128)S(1)} %pad_add_fusion.core), custom_call_target="tpu_custom_call" | custom-call | tf_op jit(solution)/shard_map/pallas_call | solution.py:318
  18.2 2.8 %copy-done = bf16[32,3,128,256]{3,2,1,0:T(8,128)(2,1)S(1)} copy-done((bf16[32,3,128,256]{3,2,1,0:T(8,128)(2,1)S(1)}, bf16[32,3,128,256]{3,2,1,0:T(8,128)(2,1)}, u32[]{:S(2)}) %copy-start) | copy-done | bytes 6291480
  22.6 9.1 %shard_map.69.mine = bf16[16,256,128]{2,1,0:T(8,128)(2,1)S(1)} custom-call(s32[200]{0:T(256)S(1)} %get-tuple-element.13.ids, s32[5]{0:T(128)S(1)} %get-tuple-element.15.own, s32[2]{0:T(128)S(1)} %pad_add_fusion.core, bf16[32,3,128,256]{3,2,1,0:T(8,128)(2,1)S(1)} %copy-done, bf16[32,3,128,256]{3,2,1,0:T(8,128)(2,1)} %collective-permute-done.2.jac_far, ...), custom_call_target="tpu_custom_call" | custom-call | flops 1610612736 | tf_op jit(solution)/shard_map/pallas_call | solution.py:332
  31.8 2.6 %collective-permute-done.10.other = bf16[16,256,128]{2,1,0:T(8,128)(2,1)S(1)} collective-permute-done((bf16[16,256,128]{2,1,0:T(8,128)(2,1)S(1)}, bf16[16,256,128]{2,1,0:T(8,128)(2,1)S(1)}, u32[]{:S(2)}, u32[]{:S(2)}) %collective-permute-start.10) | collective-permute-done | bytes 1048608 | tf_op jit(solution)/shard_map/ppermute | solution.py:55
  34.6 1.7 %shard_map.75 = s16[272,256]{1,0:T(8,128)(2,1)S(1)} custom-call(s32[200]{0:T(256)S(1)} %get-tuple-element.13.ids, s32[5]{0:T(128)S(1)} %get-tuple-element.14.every, s32[2]{0:T(128)S(1)} %pad_add_fusion.core, bf16[32,3,128,256]{3,2,1,0:T(8,128)(2,1)S(1)} %copy-done.1, bf16[33,256,128]{2,1,0:T(8,128)(2,1)S(1)} %shard_map.70.weighted), custom_call_target="tpu_custom_call" | custom-call | tf_op jit(solution)/shard_map/pallas_call | solution.py:351
  36.4 1.4 %shard_map.73 = s16[272,256]{1,0:T(8,128)(2,1)S(1)} custom-call(s32[200]{0:T(256)S(1)} %get-tuple-element.13.ids, s32[5]{0:T(128)S(1)} %get-tuple-element.14.every, s32[2]{0:T(128)S(1)} %pad_add_fusion.core, bf16[32,3,128,256]{3,2,1,0:T(8,128)(2,1)S(1)} %copy-done.1, bf16[33,256,128]{2,1,0:T(8,128)(2,1)S(1)} %shard_map.70.weighted), custom_call_target="tpu_custom_call" | custom-call | tf_op jit(solution)/shard_map/pallas_call | solution.py:351
  37.8 1.7 %shard_map.72 = s16[272,256]{1,0:T(8,128)(2,1)S(1)} custom-call(s32[200]{0:T(256)S(1)} %get-tuple-element.13.ids, s32[5]{0:T(128)S(1)} %get-tuple-element.14.every, s32[2]{0:T(128)S(1)} %pad_add_fusion.core, bf16[32,3,128,256]{3,2,1,0:T(8,128)(2,1)S(1)} %copy-done.1, bf16[33,256,128]{2,1,0:T(8,128)(2,1)S(1)} %shard_map.70.weighted), custom_call_target="tpu_custom_call" | custom-call | tf_op jit(solution)/shard_map/pallas_call | solution.py:351
  39.5 1.6 %shard_map.74.value = f32[256,256]{1,0:T(8,128)S(1)} custom-call(s32[200]{0:T(256)S(1)} %get-tuple-element.13.ids, s32[5]{0:T(128)S(1)} %get-tuple-element.14.every, s32[2]{0:T(128)S(1)} %pad_add_fusion.core, bf16[32,3,128,256]{3,2,1,0:T(8,128)(2,1)S(1)} %copy-done.1, bf16[33,256,128]{2,1,0:T(8,128)(2,1)S(1)} %shard_map.70.weighted), custom_call_target="tpu_custom_call" | custom-call | tf_op jit(solution)/shard_map/pallas_call | solution.py:351
  41.1 2.4 %collective-permute-start.11 = (s16[272,256]{1,0:T(8,128)(2,1)S(1)}, s16[272,256]{1,0:T(8,128)(2,1)S(1)}, u32[]{:S(2)}, u32[]{:S(2)}) collective-permute-start(s16[272,256]{1,0:T(8,128)(2,1)S(1)} %shard_map.72), channel_id=1, source_target_pairs={{0,12},{2,6},{4,0},{6,10},{8,4},{10,14},{12,8},{14,2},{1,13},{3,7}... | collective-permute-start | bytes 417800 | tf_op jit(solution)/shard_map/ppermute | solution.py:68
  43.9 1.6 %shard_map.71.own = f32[256,256]{1,0:T(8,128)S(1)} custom-call(s32[200]{0:T(256)S(1)} %get-tuple-element.13.ids, s32[5]{0:T(128)S(1)} %get-tuple-element.14.every, s32[2]{0:T(128)S(1)} %pad_add_fusion.core, bf16[32,3,128,256]{3,2,1,0:T(8,128)(2,1)S(1)} %copy-done.1, bf16[33,256,128]{2,1,0:T(8,128)(2,1)S(1)} %shard_map.70.weighted), custom_call_target="tpu_custom_call" | custom-call | tf_op jit(solution)/shard_map/pallas_call | solution.py:351
  45.5 2.0 %collective-permute-done.11.rest_0_ = s16[272,256]{1,0:T(8,128)(2,1)S(1)} collective-permute-done((s16[272,256]{1,0:T(8,128)(2,1)S(1)}, s16[272,256]{1,0:T(8,128)(2,1)S(1)}, u32[]{:S(2)}, u32[]{:S(2)}) %collective-permute-start.11) | collective-permute-done | bytes 139296 | tf_op jit(solution)/shard_map/ppermute | solution.py:68
  47.5 1.1 collective-permute-done.12.rest_1_
  48.6 2.5 %collective-permute-done.14.rest_2_ = s16[272,256]{1,0:T(8,128)(2,1)S(1)} collective-permute-done((s16[272,256]{1,0:T(8,128)(2,1)S(1)}, s16[272,256]{1,0:T(8,128)(2,1)S(1)}, u32[]{:S(2)}, u32[]{:S(2)}) %collective-permute-start.14) | collective-permute-done | bytes 139296 | tf_op jit(solution)/shard_map/ppermute | solution.py:68
  52.1 1.3 %collective-permute-done.15 = f32[192,128]{1,0:T(8,128)S(1)} collective-permute-done((f32[192,128]{1,0:T(8,128)S(1)}, f32[192,128]{1,0:T(8,128)S(1)}, u32[]{:S(2)}, u32[]{:S(2)}) %collective-permute-start.15) | collective-permute-done | bytes 98336 | tf_op jit(solution)/shard_map/ppermute | solution.py:55
  53.4 1.2 %collective-permute-start.16 = (f32[192,128]{1,0:T(8,128)S(1)}, f32[192,128]{1,0:T(8,128)S(1)}, u32[]{:S(2)}, u32[]{:S(2)}) collective-permute-start(f32[192,128]{1,0:T(8,128)S(1)} %add.12), channel_id=1, source_target_pairs={{0,2},{1,5},{2,0},{3,7},{4,6},{5,1},{6,4},{7,3},{8,10},{9,13},{10,... | collective-permute-start | bytes 294920 | tf_op jit(solution)/shard_map/ppermute | solution.py:302
  54.5 3.5 %collective-permute-done.16 = f32[192,128]{1,0:T(8,128)S(1)} collective-permute-done((f32[192,128]{1,0:T(8,128)S(1)}, f32[192,128]{1,0:T(8,128)S(1)}, u32[]{:S(2)}, u32[]{:S(2)}) %collective-permute-start.16) | collective-permute-done | bytes 98336 | tf_op jit(solution)/shard_map/ppermute | solution.py:302
  58.9 3.8 %collective-permute-done.17 = f32[192,128]{1,0:T(8,128)S(1)} collective-permute-done((f32[192,128]{1,0:T(8,128)S(1)}, f32[192,128]{1,0:T(8,128)S(1)}, u32[]{:S(2)}, u32[]{:S(2)}) %collective-permute-start.17) | collective-permute-done | bytes 98336 | tf_op jit(solution)/shard_map/ppermute | solution.py:302
  62.8 2.7 %collective-permute-start.18 = (f32[192,128]{1,0:T(8,128)S(1)}, f32[192,128]{1,0:T(8,128)S(1)}, u32[]{:S(2)}, u32[]{:S(2)}) collective-permute-start(f32[192,128]{1,0:T(8,128)S(1)} %add.14), channel_id=1, source_target_pairs={{0,12},{1,13},{2,14},{3,15},{4,8},{5,9},{6,10},{7,11},{8,4},{9,5},... | collective-permute-start | bytes 294920 | tf_op jit(solution)/shard_map/ppermute | solution.py:302
  65.4 3.8 %collective-permute-done.18 = f32[192,128]{1,0:T(8,128)S(1)} collective-permute-done((f32[192,128]{1,0:T(8,128)S(1)}, f32[192,128]{1,0:T(8,128)S(1)}, u32[]{:S(2)}, u32[]{:S(2)}) %collective-permute-start.18) | collective-permute-done | bytes 98336 | tf_op jit(solution)/shard_map/ppermute | solution.py:302
  69.3 1.3 %collective-permute-done.19.other = f32[192,128]{1,0:T(8,128)S(1)} collective-permute-done((f32[192,128]{1,0:T(8,128)S(1)}, f32[192,128]{1,0:T(8,128)S(1)}, u32[]{:S(2)}, u32[]{:S(2)}) %collective-permute-start.19) | collective-permute-done | bytes 98336 | tf_op jit(solution)/shard_map/ppermute | solution.py:55
  70.6 41.6 %shard_map.78 = (f32[256,256]{1,0:T(8,128)}, f32[256,256]{1,0:T(8,128)}) custom-call(s32[2]{0:T(128)S(1)} %pad_add_fusion.core, f32[192,128]{1,0:T(8,128)S(1)} %add.15.mine, f32[192,128]{1,0:T(8,128)S(1)} %collective-permute-done.19.other, f32[256,256]{1,0:T(8,128)S(1)} %get-tuple-element.19.field), custom_call_target="tpu_custom_call" | custom-call | tf_op jit(solution)/shard_map/pallas_call | solution.py:374
  (41 shorter events, 9.2 us)
Async XLA Ops:
  0.6 17.6 %collective-permute-start.2 = (bf16[32,3,128,256]{3,2,1,0:T(8,128)(2,1)}, bf16[32,3,128,256]{3,2,1,0:T(8,128)(2,1)}, u32[]{:S(2)}, u32[]{:S(2)}) collective-permute-start(bf16[32,3,128,256]{3,2,1,0:T(8,128)(2,1)} %jac.9), channel_id=1, source_target_pairs={{0,1},{1,0},{2,3},{3,2},{4,5},{5,4},{6,7},{7,6},{8,9},{9,8},{10,11... | collective-permute-start | bytes 18874376 | tf_op jit(solution)/shard_map/ppermute | solution.py:55
  1.1 8.8 %collective-permute-start = (bf16[256,256]{1,0:T(8,128)(2,1)}, bf16[256,256]{1,0:T(8,128)(2,1)S(1)}, u32[]{:S(2)}, u32[]{:S(2)}) collective-permute-start(bf16[256,256]{1,0:T(8,128)(2,1)} %bitcast.4), channel_id=1, source_target_pairs={{0,12},{2,6},{4,0},{6,10},{8,4},{10,14},{12,8},{14,2},{1,13},{3,7}... | collective-permute-start | bytes 393224 | tf_op jit(solution)/shard_map/ppermute | solution.py:68
  5.8 10.0 %collective-permute-start.4 = (bf16[256,256]{1,0:T(8,128)(2,1)}, bf16[256,256]{1,0:T(8,128)(2,1)S(1)}, u32[]{:S(2)}, u32[]{:S(2)}) collective-permute-start(bf16[256,256]{1,0:T(8,128)(2,1)} %bitcast.5), channel_id=1, source_target_pairs={{0,2},{2,0},{4,6},{6,4},{8,10},{10,8},{12,14},{14,12},{1,3},{3,1},... | collective-permute-start | bytes 393224 | tf_op jit(solution)/shard_map/ppermute | solution.py:63
  5.8 10.5 %collective-permute-start.3 = (bf16[256,256]{1,0:T(8,128)(2,1)}, bf16[256,256]{1,0:T(8,128)(2,1)S(1)}, u32[]{:S(2)}, u32[]{:S(2)}) collective-permute-start(bf16[256,256]{1,0:T(8,128)(2,1)} %bitcast.6), channel_id=1, source_target_pairs={{0,4},{2,14},{4,8},{6,2},{8,12},{10,6},{12,0},{14,10},{1,5},{3,15}... | collective-permute-start | bytes 393224 | tf_op jit(solution)/shard_map/ppermute | solution.py:68
  10.0 6.5 %collective-permute-start.1 = (bf16[256,256]{1,0:T(8,128)(2,1)S(1)}, bf16[256,256]{1,0:T(8,128)(2,1)S(1)}, u32[]{:S(2)}, u32[]{:S(2)}) collective-permute-start(bf16[256,256]{1,0:T(8,128)(2,1)S(1)} %collective-permute-done.rest_1_), channel_id=1, source_target_pairs={{0,2},{2,0},{4,6},{6,4},{8,10},{10,8},{12,14},{14,12},{1,3},{3,1},... | collective-permute-start | bytes 393224 | tf_op jit(solution)/shard_map/ppermute | solution.py:63
  12.0 4.8 %collective-permute-start.5 = (bf16[256,256]{1,0:T(8,128)(2,1)}, bf16[256,256]{1,0:T(8,128)(2,1)S(1)}, u32[]{:S(2)}, u32[]{:S(2)}) collective-permute-start(bf16[256,256]{1,0:T(8,128)(2,1)} %bitcast.7), channel_id=1, source_target_pairs={{0,1},{1,0},{2,3},{3,2},{4,5},{5,4},{6,7},{7,6},{8,9},{9,8},{10,11... | collective-permute-start | bytes 393224 | tf_op jit(solution)/shard_map/ppermute | solution.py:55
  15.8 2.1 %collective-permute-start.6 = (bf16[256,256]{1,0:T(8,128)(2,1)S(1)}, bf16[256,256]{1,0:T(8,128)(2,1)S(1)}, u32[]{:S(2)}, u32[]{:S(2)}) collective-permute-start(bf16[256,256]{1,0:T(8,128)(2,1)S(1)} %collective-permute-done.rest_1_), channel_id=1, source_target_pairs={{0,1},{1,0},{2,3},{3,2},{4,5},{5,4},{6,7},{7,6},{8,9},{9,8},{10,11... | collective-permute-start | bytes 393224 | tf_op jit(solution)/shard_map/ppermute | solution.py:55
  16.4 1.3 %collective-permute-start.8 = (bf16[256,256]{1,0:T(8,128)(2,1)S(1)}, bf16[256,256]{1,0:T(8,128)(2,1)S(1)}, u32[]{:S(2)}, u32[]{:S(2)}) collective-permute-start(bf16[256,256]{1,0:T(8,128)(2,1)S(1)} %collective-permute-done.4.rest_3_), channel_id=1, source_target_pairs={{0,1},{1,0},{2,3},{3,2},{4,5},{5,4},{6,7},{7,6},{8,9},{9,8},{10,11... | collective-permute-start | bytes 393224 | tf_op jit(solution)/shard_map/ppermute | solution.py:55
  16.4 1.4 %collective-permute-start.7 = (bf16[256,256]{1,0:T(8,128)(2,1)S(1)}, bf16[256,256]{1,0:T(8,128)(2,1)S(1)}, u32[]{:S(2)}, u32[]{:S(2)}) collective-permute-start(bf16[256,256]{1,0:T(8,128)(2,1)S(1)} %collective-permute-done.3.rest_2_), channel_id=1, source_target_pairs={{0,1},{1,0},{2,3},{3,2},{4,5},{5,4},{6,7},{7,6},{8,9},{9,8},{10,11... | collective-permute-start | bytes 393224 | tf_op jit(solution)/shard_map/ppermute | solution.py:55
  16.9 1.3 %collective-permute-start.9 = (bf16[256,256]{1,0:T(8,128)(2,1)S(1)}, bf16[256,256]{1,0:T(8,128)(2,1)S(1)}, u32[]{:S(2)}, u32[]{:S(2)}) collective-permute-start(bf16[256,256]{1,0:T(8,128)(2,1)S(1)} %collective-permute-done.1.rest_4_), channel_id=1, source_target_pairs={{0,1},{1,0},{2,3},{3,2},{4,5},{5,4},{6,7},{7,6},{8,9},{9,8},{10,11... | collective-permute-start | bytes 393224 | tf_op jit(solution)/shard_map/ppermute | solution.py:55
  18.2 2.8 %copy-start = (bf16[32,3,128,256]{3,2,1,0:T(8,128)(2,1)S(1)}, bf16[32,3,128,256]{3,2,1,0:T(8,128)(2,1)}, u32[]{:S(2)}) copy-start(bf16[32,3,128,256]{3,2,1,0:T(8,128)(2,1)} %jac.9) | copy-start | bytes 18874372
  21.0 0.9 copy-start.2
  21.9 0.7 copy-start.3
  22.6 12.0 %copy-start.1 = (bf16[32,3,128,256]{3,2,1,0:T(8,128)(2,1)S(1)}, bf16[32,3,128,256]{3,2,1,0:T(8,128)(2,1)}, u32[]{:S(2)}) copy-start(bf16[32,3,128,256]{3,2,1,0:T(8,128)(2,1)} %jac.9) | copy-start | bytes 18874372
  31.7 2.7 %collective-permute-start.10 = (bf16[16,256,128]{2,1,0:T(8,128)(2,1)S(1)}, bf16[16,256,128]{2,1,0:T(8,128)(2,1)S(1)}, u32[]{:S(2)}, u32[]{:S(2)}) collective-permute-start(bf16[16,256,128]{2,1,0:T(8,128)(2,1)S(1)} %shard_map.69.mine), channel_id=1, source_target_pairs={{0,1},{1,0},{2,3},{3,2},{4,5},{5,4},{6,7},{7,6},{8,9},{9,8},{10,11... | collective-permute-start | bytes 3145736 | tf_op jit(solution)/shard_map/ppermute | solution.py:55
  36.3 7.1 %collective-permute-start.13 = (s16[272,256]{1,0:T(8,128)(2,1)S(1)}, s16[272,256]{1,0:T(8,128)(2,1)S(1)}, u32[]{:S(2)}, u32[]{:S(2)}) collective-permute-start(s16[272,256]{1,0:T(8,128)(2,1)S(1)} %shard_map.75), channel_id=1, source_target_pairs={{0,2},{2,0},{4,6},{6,4},{8,10},{10,8},{12,14},{14,12},{1,3},{3,1},... | collective-permute-start | bytes 417800 | tf_op jit(solution)/shard_map/ppermute | solution.py:63
  41.1 6.4 %collective-permute-start.11 = (s16[272,256]{1,0:T(8,128)(2,1)S(1)}, s16[272,256]{1,0:T(8,128)(2,1)S(1)}, u32[]{:S(2)}, u32[]{:S(2)}) collective-permute-start(s16[272,256]{1,0:T(8,128)(2,1)S(1)} %shard_map.72), channel_id=1, source_target_pairs={{0,12},{2,6},{4,0},{6,10},{8,4},{10,14},{12,8},{14,2},{1,13},{3,7}... | collective-permute-start | bytes 417800 | tf_op jit(solution)/shard_map/ppermute | solution.py:68
  43.4 5.2 %collective-permute-start.12 = (s16[272,256]{1,0:T(8,128)(2,1)S(1)}, s16[272,256]{1,0:T(8,128)(2,1)S(1)}, u32[]{:S(2)}, u32[]{:S(2)}) collective-permute-start(s16[272,256]{1,0:T(8,128)(2,1)S(1)} %shard_map.73), channel_id=1, source_target_pairs={{0,2},{2,0},{4,6},{6,4},{8,10},{10,8},{12,14},{14,12},{1,3},{3,1},... | collective-permute-start | bytes 417800 | tf_op jit(solution)/shard_map/ppermute | solution.py:63
  43.5 7.5 %collective-permute-start.14 = (s16[272,256]{1,0:T(8,128)(2,1)S(1)}, s16[272,256]{1,0:T(8,128)(2,1)S(1)}, u32[]{:S(2)}, u32[]{:S(2)}) collective-permute-start(s16[272,256]{1,0:T(8,128)(2,1)S(1)} %shard_map.76), channel_id=1, source_target_pairs={{0,4},{2,14},{4,8},{6,2},{8,12},{10,6},{12,0},{14,10},{1,5},{3,15}... | collective-permute-start | bytes 417800 | tf_op jit(solution)/shard_map/ppermute | solution.py:68
  52.0 1.4 %collective-permute-start.15 = (f32[192,128]{1,0:T(8,128)S(1)}, f32[192,128]{1,0:T(8,128)S(1)}, u32[]{:S(2)}, u32[]{:S(2)}) collective-permute-start(f32[192,128]{1,0:T(8,128)S(1)} %get-tuple-element.18), channel_id=1, source_target_pairs={{0,1},{1,0},{2,3},{3,2},{4,5},{5,4},{6,7},{7,6},{8,9},{9,8},{10,11... | collective-permute-start | bytes 294920 | tf_op jit(solution)/shard_map/ppermute | solution.py:55
  53.4 4.7 %collective-permute-start.16 = (f32[192,128]{1,0:T(8,128)S(1)}, f32[192,128]{1,0:T(8,128)S(1)}, u32[]{:S(2)}, u32[]{:S(2)}) collective-permute-start(f32[192,128]{1,0:T(8,128)S(1)} %add.12), channel_id=1, source_target_pairs={{0,2},{1,5},{2,0},{3,7},{4,6},{5,1},{6,4},{7,3},{8,10},{9,13},{10,... | collective-permute-start | bytes 294920 | tf_op jit(solution)/shard_map/ppermute | solution.py:302
  58.1 4.7 %collective-permute-start.17 = (f32[192,128]{1,0:T(8,128)S(1)}, f32[192,128]{1,0:T(8,128)S(1)}, u32[]{:S(2)}, u32[]{:S(2)}) collective-permute-start(f32[192,128]{1,0:T(8,128)S(1)} %add.13), channel_id=1, source_target_pairs={{0,4},{1,3},{2,6},{3,1},{4,0},{5,7},{6,2},{7,5},{8,12},{9,11},{10,... | collective-permute-start | bytes 294920 | tf_op jit(solution)/shard_map/ppermute | solution.py:302
  62.8 6.5 %collective-permute-start.18 = (f32[192,128]{1,0:T(8,128)S(1)}, f32[192,128]{1,0:T(8,128)S(1)}, u32[]{:S(2)}, u32[]{:S(2)}) collective-permute-start(f32[192,128]{1,0:T(8,128)S(1)} %add.14), channel_id=1, source_target_pairs={{0,12},{1,13},{2,14},{3,15},{4,8},{5,9},{6,10},{7,11},{8,4},{9,5},... | collective-permute-start | bytes 294920 | tf_op jit(solution)/shard_map/ppermute | solution.py:302
  69.3 1.4 %collective-permute-start.19 = (f32[192,128]{1,0:T(8,128)S(1)}, f32[192,128]{1,0:T(8,128)S(1)}, u32[]{:S(2)}, u32[]{:S(2)}) collective-permute-start(f32[192,128]{1,0:T(8,128)S(1)} %add.15.mine), channel_id=1, source_target_pairs={{0,1},{1,0},{2,3},{3,2},{4,5},{5,4},{6,7},{7,6},{8,9},{9,8},{10,11... | collective-permute-start | bytes 294920 | tf_op jit(solution)/shard_map/ppermute | solution.py:55

commit v3 on v2

v3 whole, which is shorter than its diff:
```python
import functools
import math

import jax
import jax.numpy as jnp
from jax import lax
from jax.experimental import pallas as pl
from jax.experimental.pallas import tpu as pltpu
from jax.sharding import PartitionSpec as P

F32 = jnp.float32
BF16 = jnp.bfloat16
NN = (((1,), (0,)), ((), ()))
NT = (((1,), (1,)), ((), ()))
OFFSETS = (-2, -1, 0, 1, 2)
PAD = 16
LIMIT = 16 << 20
VMEM = pl.BlockSpec(memory_space=pltpu.VMEM)
SMEM = pl.BlockSpec(memory_space=pltpu.SMEM)
HBM = pl.BlockSpec(memory_space=pltpu.HBM)
STEP = 4


def kernel_call(body, out_shape, in_specs, out_specs, scratch=(), flops=1024, nbytes=1024):
    return pl.pallas_call(
        body,
        out_shape=out_shape,
        in_specs=in_specs,
        out_specs=out_specs,
        scratch_shapes=list(scratch),
        compiler_params=pltpu.CompilerParams(vmem_limit_bytes=LIMIT),
        cost_estimate=pl.CostEstimate(flops=flops, bytes_accessed=nbytes, transcendentals=0),
    )


def dot(a, b, dims=NN):
    return lax.dot_general(a, b, dims, preferred_element_type=F32)


def halves(a):
    high = a.astype(BF16)
    return high, (a - high.astype(F32)).astype(BF16)


def dot3(a, b, dims=NN):
    a_high, a_low = a
    b_high, b_low = b
    return dot(a_high, b_high, dims) + (dot(a_high, b_low, dims) + dot(a_low, b_high, dims))


held = pltpu.with_memory_space_constraint


def shifted(value, axis, steps):
    count = lax.axis_size(axis)
    pairs = [(source, (source + steps) % count) for source in range(count)]
    return lax.ppermute(value, axis, pairs)


def flipped(value):
    return shifted(value, "col", 1)


def swapped(value):
    return lax.ppermute(value, "tile", [(i, i ^ 1) for i in range(lax.axis_size("tile"))])


def spread(value, steps):
    count = lax.axis_size("tile")
    return lax.ppermute(value, "tile", [(i, (i + (steps, -steps)[i % 2]) % count) for i in range(count)])


ROLES = ("own", "back", "ahead", "partner", "beyond")


def core_index():
    return lax.axis_index("col").astype(jnp.int32)


def place_of(role):
    parity = lax.rem(lax.axis_index("tile").astype(jnp.int32), 2)
    return {
        "own": 2,
        "back": 4 - 4 * parity,
        "ahead": 4 * parity,
        "partner": 3 - 2 * parity,
        "beyond": 1 + 2 * parity,
    }[role]


def list_kernel(cap, half, footprint, live, table):
    reach, slots = footprint.shape
    core = core_index()
    counts = len(OFFSETS) * cap
    for o in range(len(OFFSETS)):
        table[counts + o] = 0

    def step(j, _):
        slot = lax.rem(j + core * half, slots)
        alive = (slot < live[0]).astype(jnp.int32)
        for f in range(reach):
            o = footprint[f, slot]
            n = table[counts + o]
            table[o * cap + n] = j * 4 + f
            table[counts + o] = n + alive
        return 0

    lax.fori_loop(0, slots, step, 0)


def stage_kernel(value, out, sem):
    copy = pltpu.make_async_copy(value, out, sem)
    copy.start()
    copy.wait()


def early_kernel(footprint, jac_near, jac_far, *rest):
    count = len(ROLES) - 1
    near, far = rest[:count], rest[count : 2 * count]
    images, aside, window = rest[2 * count :]
    slots = images.shape[0]
    _, reach, _, cells = jac_near.shape
    base = core_index() * slots
    for i in range(count):
        o = place_of(ROLES[i])
        window[o, :cells] = near[i][...]
        window[o, cells:] = far[i][...]
    last = place_of(ROLES[count])
    window[last] = jnp.zeros(window.shape[1:], BF16)
    for j in range(slots):
        places = [footprint[f, base + j] for f in range(reach)]
        pieces = [jac[base + j, f] for f in range(reach) for jac in (jac_near, jac_far)]
        bands = [window[place] for place in places]
        images[j] = dot(jnp.concatenate(pieces, axis=1), jnp.concatenate(bands, axis=0))
        chosen = sum(f * (places[f] == last).astype(jnp.int32) for f in range(reach))
        found = sum((place == last).astype(jnp.int32) for place in places)
        for side, jac in enumerate((jac_near, jac_far)):
            block = jac[base + j, chosen]
            aside[j, :, side * cells : (side + 1) * cells] = jnp.where(found > 0, block, jnp.zeros_like(block))


def late_kernel(live, images, aside, near, far, noise, out):
    half, _, rows = out.shape
    base = core_index() * half
    band = jnp.concatenate([near[...], far[...]], axis=0)
    size = half // 2
    for first in range(0, half, size):
        product = dot(jnp.concatenate([aside[first + j] for j in range(size)], axis=0), band)
        for j in range(size):
            slot = base + first + j
            scale = noise[pl.ds(slot, 1), :] * (slot < live[0]).astype(F32)
            image = images[first + j] + product[j * rows : (j + 1) * rows]
            out[first + j] = (image.T * scale).astype(BF16)


def gather_kernel(mine, other, out):
    half = mine.shape[0]

    def step(j, _):
        out[j] = mine[j]
        out[half + j] = other[j]
        return 0

    lax.fori_loop(0, half, step, 0)
    out[2 * half] = jnp.zeros(out.shape[1:], BF16)


def encode(value, out):
    width = value.shape[0]
    top = jnp.max(jnp.abs(value), axis=0, keepdims=True)
    power = jnp.clip(jnp.floor(jnp.log2(jnp.maximum(top, 1e-30))) + 1.0, -96.0, 96.0)
    coded = jnp.clip(jnp.round(value * jnp.exp2(15.0 - power)), -32767.0, 32767.0)
    out[:width] = coded.astype(jnp.int32).astype(jnp.int16)
    rows = jnp.broadcast_to(power.astype(jnp.int32), (PAD, power.shape[1]))
    out[width:] = rows.astype(jnp.int16)


def decode(part):
    width = part.shape[0] - PAD
    power = part[width:].astype(jnp.int32).astype(F32)[:1]
    return part[:width].astype(jnp.int32).astype(F32) * jnp.exp2(power - 15.0)


def backward_kernel(roles, coded, cap, table, jac, weighted, *rest):
    outs, total = rest[:-1], rest[-1]
    slots = jac.shape[0]
    half = slots // 2
    counts = len(OFFSETS) * cap
    core = core_index()
    for role, code_it, out in zip(roles, coded, outs, strict=True):
        o = place_of(role)
        count = table[counts + o]

        def product(size):
            left, right = [], []
            for n in range(size):
                code = jnp.where(n < count, table[o * cap + n], slots * 4)
                j, f = lax.shift_right_logical(code, 2), jnp.bitwise_and(code, 3)
                left.append(weighted[j])
                right.append(jac[lax.rem(j + core * half, slots), f])
            total[...] = dot(jnp.concatenate(left, axis=1), jnp.concatenate(right, axis=0))

        below = -1
        for size in range(slots * 3 // 8, slots + 1, STEP):
            pl.when((count > below) & (count <= size))(functools.partial(product, size))
            below = size
        if code_it:
            encode(total[...], out)
        else:
            out[...] = total[...]


def merge_kernel(value, part, out):
    encode(value[...] + decode(part), out)


def field_kernel(probes, own, *rest):
    parts, (field, keep, send) = rest[:3], rest[3:]
    width = own.shape[0]
    total = probes[...].astype(F32).T + own[...]
    for part in parts:
        total = total + decode(part)
    field[...] = total
    both = halves(total)
    gram = dot3(both, both, NT)
    mid, quarter = width // 2, width // 4
    lower = [gram[:mid, :mid], gram[mid : mid + quarter, :mid]]
    upper = [gram[mid:, mid:], gram[mid + quarter :, :mid]]
    first = core_index() == 0
    low, high = jnp.concatenate(lower, axis=0), jnp.concatenate(upper, axis=0)
    keep[...] = jnp.where(first, low, high)
    send[...] = jnp.where(first, high, low)


def finish_kernel(scale, rounds, mine, other, field, basis, factor, gram, inverse, a_high, a_low):
    width = gram.shape[0]
    mid, quarter = width // 2, width // 4
    first = core_index() == 0
    low = jnp.where(first, mine[...], other[...])
    high = jnp.where(first, other[...], mine[...])
    corner = jnp.concatenate([low[mid:], high[mid:]], axis=0)
    gram[:mid, :mid] = low[:mid]
    gram[mid:, mid:] = high[:mid]
    gram[mid:, :mid] = corner
    gram[:mid, mid:] = corner.T
    matrix = gram[...]
    row = lax.broadcasted_iota(jnp.int32, matrix.shape, 0)
    column = lax.broadcasted_iota(jnp.int32, matrix.shape, 1)
    eye = (row == column).astype(F32)
    diagonal = matrix * eye
    down = lax.rsqrt(jnp.sum(diagonal, axis=1, keepdims=True))
    along = lax.rsqrt(jnp.sum(diagonal, axis=0, keepdims=True))
    unit = matrix * down * along
    parts = halves(unit)
    a_high[...], a_low[...] = parts

    def correction(error):
        return jnp.where(row > column, error, 0.5 * eye * error).astype(BF16)

    now = (eye - jnp.where(row > column, unit, 0.0)).astype(BF16)
    for _ in range(rounds):
        error = dot(dot(now, a_high[...]).astype(BF16), now, NT) - eye
        exact = now.astype(F32) - dot(correction(error), now)
        now = exact.astype(BF16)
    full = halves(exact)
    error = dot3(halves(dot3(full, (a_high[...], a_low[...]))), full, NT) - eye
    inverse[...] = (exact - dot(correction(error), full[0])) * along
    left = jnp.sum(error * error)

    @pl.when(jnp.logical_not(left < 1e-2))
    def _():
        inverse[...] = eye
        across = lax.broadcasted_iota(jnp.int32, (1, width), 1)
        down_at = lax.broadcasted_iota(jnp.int32, (width, 1), 0)

        def eliminate(k, _):
            pivot_row = gram[pl.ds(k, 1), :]
            pivot = jnp.sum(jnp.where(across == k, pivot_row, 0.0), axis=1, keepdims=True)
            scaled = pivot_row * lax.rsqrt(pivot)
            now = gram[...]
            below = jnp.sum(jnp.where(column == k, now, 0.0), axis=1, keepdims=True)
            below = jnp.where(down_at > k, below * lax.rsqrt(pivot), 0.0)
            done = inverse[pl.ds(k, 1), :] * lax.rsqrt(pivot)
            gram[...] = now - below * scaled
            inverse[...] = inverse[...] - below * done
            inverse[pl.ds(k, 1), :] = done
            return 0

        lax.fori_loop(0, width, eliminate, 0)

    solved = halves(inverse[...])
    upper = dot3(solved, halves(matrix)) * (1.0 / scale)
    factor[...] = jnp.where(row <= column, upper, 0.0)
    basis[...] = (dot3(solved, halves(field[...])) * scale).T


def all_reduced(value):
    count = lax.axis_size("tile")
    if count & (count - 1):
        return lax.psum(value, "tile")

    def exchanged(jump):
        return lax.ppermute(value, "tile", [(i, i ^ jump) for i in range(count)])

    bit = 1
    while bit < count:
        if bit == 1 or 2 * bit == count:
            value = value + exchanged(bit)
            bit *= 2
        else:
            first, second, third = exchanged(bit), exchanged(2 * bit), exchanged(3 * bit)
            value = (value + first) + (second + third)
            bit *= 4
    return value


def on_device(jacobian, footprint, live, noise_weight, probes):
    slots, reach, rows, cells = jacobian.shape
    width = probes.shape[2]
    half = slots // lax.axis_size("col")
    cap = slots
    footprint = footprint.T
    mine = probes[0]

    back, ahead, partner = spread(mine, -2), spread(mine, 2), swapped(mine)
    jac_far = flipped(jacobian)
    staged = kernel_call(
        stage_kernel,
        pltpu.VMEM(jacobian.shape, BF16),
        [HBM],
        VMEM,
        [pltpu.SemaphoreType.DMA(())],
    )(held(jacobian, pltpu.HBM))
    back, staged = lax.optimization_barrier((back, staged))
    near = [mine, back, ahead, partner]
    far = [flipped(mine), flipped(back)]
    ahead, partner, _ = lax.optimization_barrier((ahead, partner, far[1]))
    far += [flipped(ahead), flipped(partner)]

    early = kernel_call(
        early_kernel,
        (
            jax.ShapeDtypeStruct((half, rows, width), F32),
            jax.ShapeDtypeStruct((half, rows, 2 * cells), BF16),
        ),
        [SMEM] + [VMEM] * 10,
        (VMEM,) * 2,
        [pltpu.VMEM((len(OFFSETS), 2 * cells, width), BF16)],
    )(footprint, held(staged, pltpu.VMEM), held(jac_far, pltpu.VMEM), *near, *far)
    beyond = swapped(back)
    weighted = kernel_call(
        late_kernel,
        jax.ShapeDtypeStruct((half, width, rows), BF16),
        [SMEM] + [VMEM] * 5,
        VMEM,
    )(live, *early, beyond, flipped(beyond), noise_weight)
    table = kernel_call(
        functools.partial(list_kernel, cap, half),
        jax.ShapeDtypeStruct((len(OFFSETS) * (cap + 1),), jnp.int32),
        [SMEM] * 2,
        SMEM,
    )(footprint, live)
    weighted = kernel_call(
        gather_kernel,
        jax.ShapeDtypeStruct((2 * half + 1, width, rows), BF16),
        [VMEM] * 2,
        VMEM,
    )(weighted, flipped(weighted))

    plain = jax.ShapeDtypeStruct((width, cells), F32)
    message = jax.ShapeDtypeStruct((width + PAD, cells), jnp.int16)

    def buckets(roles, coded, weighted):
        return kernel_call(
            functools.partial(backward_kernel, roles, coded, cap),
            [message if code_it else plain for code_it in coded],
            [SMEM] + [VMEM] * 2,
            [VMEM] * len(roles),
            [pltpu.VMEM((width, cells), F32)],
        )(table, held(staged, pltpu.VMEM), weighted)

    beyond = buckets(("beyond",), (True,), weighted)[0]
    beyond, weighted = lax.optimization_barrier((beyond, weighted))
    partner = buckets(("partner",), (True,), weighted)[0]
    partner, weighted = lax.optimization_barrier((partner, weighted))
    back, ahead = buckets(("back", "ahead"), (False, True), weighted)
    back = kernel_call(merge_kernel, message, [VMEM] * 2, VMEM)(back, swapped(beyond))
    back, ahead, weighted = lax.optimization_barrier((back, ahead, weighted))
    arrived = [spread(back, 2), spread(ahead, -2), swapped(partner)]
    own = buckets(("own",), (False,), weighted)[0]
    packed = jax.ShapeDtypeStruct((3 * width // 4, width // 2), F32)
    field, keep, send = kernel_call(
        field_kernel,
        (plain, packed, packed),
        [VMEM] * 5,
        (VMEM,) * 3,
    )(mine, own, *arrived)
    summed = all_reduced(keep + flipped(send))
    scale = math.sqrt(cells * lax.axis_size("col") * lax.axis_size("tile"))
    square = jax.ShapeDtypeStruct((width, width), F32)
    basis, factor = kernel_call(
        functools.partial(finish_kernel, scale, 2),
        (jax.ShapeDtypeStruct((cells, width), F32), square),
        [VMEM] * 3,
        (VMEM,) * 2,
        [pltpu.VMEM((width, width), F32)] * 2 + [pltpu.VMEM((width, width), BF16)] * 2,
    )(summed, flipped(summed), field)
    return (basis[None], factor)


def solution(mesh):
    placed = (
        P(("groups", "tile"), None, None, "col"),
        P(("groups", "tile"), None),
        P(("groups", "tile")),
        P(("groups", "tile"), None),
        P(("groups", "tile"), "col", None),
    )
    return jax.shard_map(
        on_device,
        mesh=mesh,
        in_specs=placed,
        out_specs=(P(("groups", "tile"), "col", None), P("groups", None)),
        check_vma=False,
    )
```

time: 114 us -> 102 us (0.89); the launches traced: 112 us -> 102 us
  Pallas kernels: 62 us -> 54.3 us
  starting transfers between devices: 17.1 us -> 23.7 us
  local copies, waits for them, and re-layouts: 5.17 us -> 0.01 us
  waiting for transfers between devices: 26.3 us -> 22 us
    pallas_call x9 -> x10, Pallas kernels: 20.3 us -> 13.6 us  [the longest x4 4.79 us: buckets(): kernel_call(functools.partial(backward_kernel, roles, coded, cap), [messa...]
    unnamed x9 -> x6, local copies, waits for them, and re-layouts: 5.17 us -> 0.01 us
    ppermute x9, waiting for transfers between devices: 6.49 us -> 2.96 us  [shifted(): return lax.ppermute(value, axis, pairs)]
    ppermute x4, starting transfers between devices: 2.14 us -> 5.59 us  [swapped(): lax.ppermute(value, 'tile', [(i, i ^ 1) for i in range(lax.axis_size('til...]
    ppermute x3 -> x4, starting transfers between devices: 4.69 us -> 7.32 us  [exchanged(): return lax.ppermute(value, 'tile', [(i, i ^ jump) for i in range(count)])]
    ppermute x4, waiting for transfers between devices: 1.08 us -> 3.38 us  [swapped(): lax.ppermute(value, 'tile', [(i, i ^ 1) for i in range(lax.axis_size('til...]
    ppermute x4, waiting for transfers between devices: 7.63 us -> 5.89 us  [spread(): lax.ppermute(value, 'tile', [(i, (i + (steps, -steps)[i % 2]) % count) fo...]
    ppermute x3 -> x4, waiting for transfers between devices: 11.2 us -> 9.76 us  [exchanged(): return lax.ppermute(value, 'tile', [(i, i ^ jump) for i in range(count)])]
  transfers between devices with their start and end apart: 20 -> 21, of which waited for: 13 -> 11; matrix products, arithmetic and copies ran while one was open for 1% -> 0% of each run, Pallas kernels for 8% -> 11%
where the time goes in v3:
time: 102 us
  Pallas kernels  54.3 us (53%)
  starting transfers between devices  23.7 us (23%)
  waiting for transfers between devices  22 us (22%)
  between operations  1.51 us (1%)
    pallas_call x1, Pallas kernels, on_device(): kernel_call(functools.partial(finish_kernel, scale, 2), (jax.ShapeDtypeSt...  40.5 us
    ppermute x4, waiting for transfers between devices, exchanged(): return lax.ppermute(value, 'tile', [(i, i ^ jump) for i in range(count)])  9.76 us
    ppermute x4, starting transfers between devices, spread(): lax.ppermute(value, 'tile', [(i, (i + (steps, -steps)[i % 2]) % count) fo...  8.94 us
    ppermute x4, starting transfers between devices, exchanged(): return lax.ppermute(value, 'tile', [(i, i ^ jump) for i in range(count)])  7.32 us
    ppermute x4, waiting for transfers between devices, spread(): lax.ppermute(value, 'tile', [(i, (i + (steps, -steps)[i % 2]) % count) fo...  5.89 us
    ppermute x4, starting transfers between devices, swapped(): lax.ppermute(value, 'tile', [(i, i ^ 1) for i in range(lax.axis_size('til...  5.59 us
    pallas_call x4, Pallas kernels, buckets(): kernel_call(functools.partial(backward_kernel, roles, coded, cap), [messa...  4.79 us
    ppermute x4, waiting for transfers between devices, swapped(): lax.ppermute(value, 'tile', [(i, i ^ 1) for i in range(lax.axis_size('til...  3.38 us
  transfers between devices with their start and end apart: 21, of which 11 were waited for; matrix products, arithmetic and copies ran while one was open for 0% of the time, Pallas kernels for 11%

profile of v3, /device:TPU:0, one launch (start us, length us, event | category | flops | bytes accessed | tf_op | source)
XLA Modules:
  0.0 101.6 jit_solution(4428657470705882230)
XLA Ops:
  1.2 4.7 %collective-permute-start = (bf16[256,256]{1,0:T(8,128)(2,1)}, bf16[256,256]{1,0:T(8,128)(2,1)S(1)}, u32[]{:S(2)}, u32[]{:S(2)}) collective-permute-start(bf16[256,256]{1,0:T(8,128)(2,1)} %bitcast.3), channel_id=1, source_target_pairs={{0,12},{2,6},{4,0},{6,10},{8,4},{10,14},{12,8},{14,2},{1,13},{3,7}... | collective-permute-start | bytes 393224 | tf_op jit(solution)/shard_map/ppermute | solution.py:70
  5.8 1.7 %collective-permute-start.3 = (bf16[256,256]{1,0:T(8,128)(2,1)}, bf16[256,256]{1,0:T(8,128)(2,1)S(1)}, u32[]{:S(2)}, u32[]{:S(2)}) collective-permute-start(bf16[256,256]{1,0:T(8,128)(2,1)} %bitcast.5), channel_id=1, source_target_pairs={{0,2},{2,0},{4,6},{6,4},{8,10},{10,8},{12,14},{14,12},{1,3},{3,1},... | collective-permute-start | bytes 393224 | tf_op jit(solution)/shard_map/ppermute | solution.py:65
  7.5 2.8 %shard_map.69.jac_near.jac = bf16[32,3,128,256]{3,2,1,0:T(8,128)(2,1)S(1)} custom-call(bf16[32,3,128,256]{3,2,1,0:T(8,128)(2,1)} %value.1), custom_call_target="tpu_custom_call" | custom-call | flops 1024 | bytes 1024 | tf_op jit(solution)/shard_map/pallas_call | solution.py:327
  10.4 1.6 %collective-permute-start.8 = (bf16[256,256]{1,0:T(8,128)(2,1)S(1)}, bf16[256,256]{1,0:T(8,128)(2,1)S(1)}, u32[]{:S(2)}, u32[]{:S(2)}) collective-permute-start(bf16[256,256]{1,0:T(8,128)(2,1)S(1)} %collective-permute-done.rest_1_), channel_id=1, source_target_pairs={{0,2},{2,0},{4,6},{6,4},{8,10},{10,8},{12,14},{14,12},{1,3},{3,1},... | collective-permute-start | bytes 393224 | tf_op jit(solution)/shard_map/ppermute | solution.py:65
  12.1 1.3 %collective-permute-done.2.rest_2_ = bf16[256,256]{1,0:T(8,128)(2,1)S(1)} collective-permute-done((bf16[256,256]{1,0:T(8,128)(2,1)}, bf16[256,256]{1,0:T(8,128)(2,1)S(1)}, u32[]{:S(2)}, u32[]{:S(2)}) %collective-permute-start.2) | collective-permute-done | bytes 131104 | tf_op jit(solution)/shard_map/ppermute | solution.py:70
  14.0 2.3 %collective-permute-done.8.near = bf16[256,256]{1,0:T(8,128)(2,1)S(1)} collective-permute-done((bf16[256,256]{1,0:T(8,128)(2,1)S(1)}, bf16[256,256]{1,0:T(8,128)(2,1)S(1)}, u32[]{:S(2)}, u32[]{:S(2)}) %collective-permute-start.8) | collective-permute-done | bytes 131104 | tf_op jit(solution)/shard_map/ppermute | solution.py:65
  17.1 2.6 %shard_map.70 = (f32[16,128,256]{2,1,0:T(8,128)S(1)}, bf16[16,128,512]{2,1,0:T(8,128)(2,1)S(1)}) custom-call(s32[3,32]{1,0:T(4,128)S(1)} %bitcast.9, bf16[32,3,128,256]{3,2,1,0:T(8,128)(2,1)S(1)} %shard_map.69.jac_near.jac, bf16[32,3,128,256]{3,2,1,0:T(8,128)(2,1)S(1)} %collective-permute-done.1.jac_far, bf16[256,256]{1,0:T(8,128)(2,1)S(1)} %bitcast.7, ...), custom_call_target="tpu_custom_call" | custom-call | flops 1024 | bytes 1024 | tf_op jit(solution)/shard_map/pallas_call | solution.py:340
  19.7 1.1 %shard_map.71.mine = bf16[16,256,128]{2,1,0:T(8,128)(2,1)S(1)} custom-call(s32[1]{0:T(128)S(6)} %copy.7.live, f32[16,128,256]{2,1,0:T(8,128)S(1)} %get-tuple-element.26.images, bf16[16,128,512]{2,1,0:T(8,128)(2,1)S(1)} %get-tuple-element.27.aside, bf16[256,256]{1,0:T(8,128)(2,1)S(1)} %collective-permute-done.8.near, ...), custom_call_target="tpu_custom_call" | custom-call | flops 1024 | bytes 1024 | tf_op jit(solution)/shard_map/pallas_call | solution.py:351
  21.3 1.9 %shard_map.68.table = s32[165]{0:T(256)S(1)} custom-call(s32[3,32]{1,0:T(4,128)S(1)} %bitcast.10, s32[1]{0:T(128)S(6)} %copy.7.live), custom_call_target="tpu_custom_call" | custom-call | flops 1024 | bytes 1024 | tf_op jit(solution)/shard_map/pallas_call | solution.py:357
  23.8 1.1 %shard_map.73 = s16[272,256]{1,0:T(8,128)(2,1)S(1)} custom-call(s32[165]{0:T(256)S(1)} %shard_map.68.table, bf16[32,3,128,256]{3,2,1,0:T(8,128)(2,1)S(1)} %shard_map.69.jac_near.jac, bf16[33,256,128]{2,1,0:T(8,128)(2,1)S(1)} %shard_map.72.weighted), custom_call_target="tpu_custom_call" | custom-call | flops 1024 | bytes 1024 | tf_op jit(solution)/shard_map/pallas_call | solution.py:374
  24.8 1.7 %collective-permute-start.11 = (s16[272,256]{1,0:T(8,128)(2,1)S(1)}, s16[272,256]{1,0:T(8,128)(2,1)S(1)}, u32[]{:S(2)}, u32[]{:S(2)}) collective-permute-start(s16[272,256]{1,0:T(8,128)(2,1)S(1)} %shard_map.73), channel_id=1, source_target_pairs={{0,2},{2,0},{4,6},{6,4},{8,10},{10,8},{12,14},{14,12},{1,3},{3,1},... | collective-permute-start | bytes 417800 | tf_op jit(solution)/shard_map/ppermute | solution.py:65
  26.6 1.1 %shard_map.74 = s16[272,256]{1,0:T(8,128)(2,1)S(1)} custom-call(s32[165]{0:T(256)S(1)} %shard_map.68.table, bf16[32,3,128,256]{3,2,1,0:T(8,128)(2,1)S(1)} %shard_map.69.jac_near.jac, bf16[33,256,128]{2,1,0:T(8,128)(2,1)S(1)} %shard_map.72.weighted), custom_call_target="tpu_custom_call" | custom-call | flops 1024 | bytes 1024 | tf_op jit(solution)/shard_map/pallas_call | solution.py:374
  27.6 1.7 %shard_map.75 = (f32[256,256]{1,0:T(8,128)S(1)}, s16[272,256]{1,0:T(8,128)(2,1)S(1)}) custom-call(s32[165]{0:T(256)S(1)} %shard_map.68.table, bf16[32,3,128,256]{3,2,1,0:T(8,128)(2,1)S(1)} %shard_map.69.jac_near.jac, bf16[33,256,128]{2,1,0:T(8,128)(2,1)S(1)} %shard_map.72.weighted), custom_call_target="tpu_custom_call" | custom-call | flops 1024 | bytes 1024 | tf_op jit(solution)/shard_map/pallas_call | solution.py:374
  31.0 4.2 %collective-permute-start.13 = (s16[272,256]{1,0:T(8,128)(2,1)S(1)}, s16[272,256]{1,0:T(8,128)(2,1)S(1)}, u32[]{:S(2)}, u32[]{:S(2)}) collective-permute-start(s16[272,256]{1,0:T(8,128)(2,1)S(1)} %get-tuple-element.35), channel_id=1, source_target_pairs={{0,12},{2,6},{4,0},{6,10},{8,4},{10,14},{12,8},{14,2},{1,13},{3,7}... | collective-permute-start | bytes 417800 | tf_op jit(solution)/shard_map/ppermute | solution.py:70
  36.3 3.5 %collective-permute-done.12.rest_0_ = s16[272,256]{1,0:T(8,128)(2,1)S(1)} collective-permute-done((s16[272,256]{1,0:T(8,128)(2,1)S(1)}, s16[272,256]{1,0:T(8,128)(2,1)S(1)}, u32[]{:S(2)}, u32[]{:S(2)}) %collective-permute-start.12) | collective-permute-done | bytes 139296 | tf_op jit(solution)/shard_map/ppermute | solution.py:70
  39.7 1.1 %collective-permute-done.13.rest_1_ = s16[272,256]{1,0:T(8,128)(2,1)S(1)} collective-permute-done((s16[272,256]{1,0:T(8,128)(2,1)S(1)}, s16[272,256]{1,0:T(8,128)(2,1)S(1)}, u32[]{:S(2)}, u32[]{:S(2)}) %collective-permute-start.13) | collective-permute-done | bytes 139296 | tf_op jit(solution)/shard_map/ppermute | solution.py:70
  41.3 1.3 %collective-permute-done.15 = f32[192,128]{1,0:T(8,128)S(1)} collective-permute-done((f32[192,128]{1,0:T(8,128)S(1)}, f32[192,128]{1,0:T(8,128)S(1)}, u32[]{:S(2)}, u32[]{:S(2)}) %collective-permute-start.15) | collective-permute-done | bytes 98336 | tf_op jit(solution)/shard_map/ppermute | solution.py:57
  42.6 2.9 %collective-permute-start.16 = (f32[192,128]{1,0:T(8,128)S(1)}, f32[192,128]{1,0:T(8,128)S(1)}, u32[]{:S(2)}, u32[]{:S(2)}) collective-permute-start(f32[192,128]{1,0:T(8,128)S(1)} %add.15), channel_id=1, source_target_pairs={{0,2},{2,0},{4,6},{6,4},{8,10},{10,8},{12,14},{14,12},{1,3},{3,1},... | collective-permute-start | bytes 294920 | tf_op jit(solution)/shard_map/ppermute | solution.py:303
  45.5 3.1 %collective-permute-done.16 = f32[192,128]{1,0:T(8,128)S(1)} collective-permute-done((f32[192,128]{1,0:T(8,128)S(1)}, f32[192,128]{1,0:T(8,128)S(1)}, u32[]{:S(2)}, u32[]{:S(2)}) %collective-permute-start.16) | collective-permute-done | bytes 98336 | tf_op jit(solution)/shard_map/ppermute | solution.py:303
  48.6 1.4 %collective-permute-start.17 = (f32[192,128]{1,0:T(8,128)S(1)}, f32[192,128]{1,0:T(8,128)S(1)}, u32[]{:S(2)}, u32[]{:S(2)}) collective-permute-start(f32[192,128]{1,0:T(8,128)S(1)} %add.16), channel_id=1, source_target_pairs={{0,4},{2,6},{4,0},{6,2},{8,12},{10,14},{12,8},{14,10},{1,5},{3,7},... | collective-permute-start | bytes 294920 | tf_op jit(solution)/shard_map/ppermute | solution.py:303
  50.9 2.1 %collective-permute-start.19 = (f32[192,128]{1,0:T(8,128)S(1)}, f32[192,128]{1,0:T(8,128)S(1)}, u32[]{:S(2)}, u32[]{:S(2)}) collective-permute-start(f32[192,128]{1,0:T(8,128)S(1)} %add.16), channel_id=1, source_target_pairs={{0,12},{2,14},{4,8},{6,10},{8,4},{10,6},{12,0},{14,2},{1,13},{3,15... | collective-permute-start | bytes 294920 | tf_op jit(solution)/shard_map/ppermute | solution.py:303
  53.6 6.1 %collective-permute-done.18 = f32[192,128]{1,0:T(8,128)S(1)} collective-permute-done((f32[192,128]{1,0:T(8,128)S(1)}, f32[192,128]{1,0:T(8,128)S(1)}, u32[]{:S(2)}, u32[]{:S(2)}) %collective-permute-start.18) | collective-permute-done | bytes 98336 | tf_op jit(solution)/shard_map/ppermute | solution.py:303
  59.8 1.3 %collective-permute-done.20.other = f32[192,128]{1,0:T(8,128)S(1)} collective-permute-done((f32[192,128]{1,0:T(8,128)S(1)}, f32[192,128]{1,0:T(8,128)S(1)}, u32[]{:S(2)}, u32[]{:S(2)}) %collective-permute-start.20) | collective-permute-done | bytes 98336 | tf_op jit(solution)/shard_map/ppermute | solution.py:57
  61.1 40.5 %shard_map.79 = (f32[256,256]{1,0:T(8,128)}, f32[256,256]{1,0:T(8,128)}) custom-call(f32[192,128]{1,0:T(8,128)S(1)} %add_add_fusion.mine, f32[192,128]{1,0:T(8,128)S(1)} %collective-permute-done.20.other, f32[256,256]{1,0:T(8,128)S(1)} %get-tuple-element.39.field), custom_call_target="tpu_custom_call" | custom-call | flops 1024 | bytes 1024 | tf_op jit(solution)/shard_map/pallas_call | solution.py:401
  (39 shorter events, 7.1 us)
Async XLA Ops:
  0.6 16.4 %collective-permute-start.1 = (bf16[32,3,128,256]{3,2,1,0:T(8,128)(2,1)}, bf16[32,3,128,256]{3,2,1,0:T(8,128)(2,1)S(1)}, u32[]{:S(2)}, u32[]{:S(2)}) collective-permute-start(bf16[32,3,128,256]{3,2,1,0:T(8,128)(2,1)} %value.1), channel_id=1, source_target_pairs={{0,1},{1,0},{2,3},{3,2},{4,5},{5,4},{6,7},{7,6},{8,9},{9,8},{10,11... | collective-permute-start | bytes 18874376 | tf_op jit(solution)/shard_map/ppermute | solution.py:57
  1.1 12.3 %copy-start = (bf16[1,256,256]{2,1,0:T(8,128)(2,1)S(1)}, bf16[1,256,256]{2,1,0:T(8,128)(2,1)}, u32[]{:S(2)}) copy-start(bf16[1,256,256]{2,1,0:T(8,128)(2,1)} %param.9) | copy-start | bytes 393220
  1.1 15.9 %copy-start.2 = (s32[32,3]{0,1:T(4,128)S(1)}, s32[32,3]{0,1:T(4,128)}, u32[]{:S(2)}) copy-start(s32[32,3]{0,1:T(4,128)} %param.6) | copy-start | bytes 1156
  1.2 9.2 %collective-permute-start = (bf16[256,256]{1,0:T(8,128)(2,1)}, bf16[256,256]{1,0:T(8,128)(2,1)S(1)}, u32[]{:S(2)}, u32[]{:S(2)}) collective-permute-start(bf16[256,256]{1,0:T(8,128)(2,1)} %bitcast.3), channel_id=1, source_target_pairs={{0,12},{2,6},{4,0},{6,10},{8,4},{10,14},{12,8},{14,2},{1,13},{3,7}... | collective-permute-start | bytes 393224 | tf_op jit(solution)/shard_map/ppermute | solution.py:70
  5.8 7.6 %collective-permute-start.2 = (bf16[256,256]{1,0:T(8,128)(2,1)}, bf16[256,256]{1,0:T(8,128)(2,1)S(1)}, u32[]{:S(2)}, u32[]{:S(2)}) collective-permute-start(bf16[256,256]{1,0:T(8,128)(2,1)} %bitcast.4), channel_id=1, source_target_pairs={{0,4},{2,14},{4,8},{6,2},{8,12},{10,6},{12,0},{14,10},{1,5},{3,15}... | collective-permute-start | bytes 393224 | tf_op jit(solution)/shard_map/ppermute | solution.py:70
  5.8 7.6 %collective-permute-start.3 = (bf16[256,256]{1,0:T(8,128)(2,1)}, bf16[256,256]{1,0:T(8,128)(2,1)S(1)}, u32[]{:S(2)}, u32[]{:S(2)}) collective-permute-start(bf16[256,256]{1,0:T(8,128)(2,1)} %bitcast.5), channel_id=1, source_target_pairs={{0,2},{2,0},{4,6},{6,4},{8,10},{10,8},{12,14},{14,12},{1,3},{3,1},... | collective-permute-start | bytes 393224 | tf_op jit(solution)/shard_map/ppermute | solution.py:65
  10.4 3.1 %collective-permute-start.5 = (bf16[256,256]{1,0:T(8,128)(2,1)S(1)}, bf16[256,256]{1,0:T(8,128)(2,1)S(1)}, u32[]{:S(2)}, u32[]{:S(2)}) collective-permute-start(bf16[256,256]{1,0:T(8,128)(2,1)S(1)} %collective-permute-done.rest_1_), channel_id=1, source_target_pairs={{0,1},{1,0},{2,3},{3,2},{4,5},{5,4},{6,7},{7,6},{8,9},{9,8},{10,11... | collective-permute-start | bytes 393224 | tf_op jit(solution)/shard_map/ppermute | solution.py:57
  10.4 5.9 %collective-permute-start.8 = (bf16[256,256]{1,0:T(8,128)(2,1)S(1)}, bf16[256,256]{1,0:T(8,128)(2,1)S(1)}, u32[]{:S(2)}, u32[]{:S(2)}) collective-permute-start(bf16[256,256]{1,0:T(8,128)(2,1)S(1)} %collective-permute-done.rest_1_), channel_id=1, source_target_pairs={{0,2},{2,0},{4,6},{6,4},{8,10},{10,8},{12,14},{14,12},{1,3},{3,1},... | collective-permute-start | bytes 393224 | tf_op jit(solution)/shard_map/ppermute | solution.py:65
  13.4 3.6 %collective-permute-start.4 = (bf16[256,256]{1,0:T(8,128)(2,1)S(1)}, bf16[256,256]{1,0:T(8,128)(2,1)S(1)}, u32[]{:S(2)}, u32[]{:S(2)}) collective-permute-start(bf16[256,256]{1,0:T(8,128)(2,1)S(1)} %bitcast.6), channel_id=1, source_target_pairs={{0,1},{1,0},{2,3},{3,2},{4,5},{5,4},{6,7},{7,6},{8,9},{9,8},{10,11... | collective-permute-start | bytes 393224 | tf_op jit(solution)/shard_map/ppermute | solution.py:57
  13.4 3.6 %collective-permute-start.6 = (bf16[256,256]{1,0:T(8,128)(2,1)S(1)}, bf16[256,256]{1,0:T(8,128)(2,1)S(1)}, u32[]{:S(2)}, u32[]{:S(2)}) collective-permute-start(bf16[256,256]{1,0:T(8,128)(2,1)S(1)} %collective-permute-done.2.rest_2_), channel_id=1, source_target_pairs={{0,1},{1,0},{2,3},{3,2},{4,5},{5,4},{6,7},{7,6},{8,9},{9,8},{10,11... | collective-permute-start | bytes 393224 | tf_op jit(solution)/shard_map/ppermute | solution.py:57
  13.9 3.1 %collective-permute-start.7 = (bf16[256,256]{1,0:T(8,128)(2,1)S(1)}, bf16[256,256]{1,0:T(8,128)(2,1)S(1)}, u32[]{:S(2)}, u32[]{:S(2)}) collective-permute-start(bf16[256,256]{1,0:T(8,128)(2,1)S(1)} %collective-permute-done.3.rest_3_), channel_id=1, source_target_pairs={{0,1},{1,0},{2,3},{3,2},{4,5},{5,4},{6,7},{7,6},{8,9},{9,8},{10,11... | collective-permute-start | bytes 393224 | tf_op jit(solution)/shard_map/ppermute | solution.py:57
  16.3 3.3 %collective-permute-start.9 = (bf16[256,256]{1,0:T(8,128)(2,1)S(1)}, bf16[256,256]{1,0:T(8,128)(2,1)S(1)}, u32[]{:S(2)}, u32[]{:S(2)}) collective-permute-start(bf16[256,256]{1,0:T(8,128)(2,1)S(1)} %collective-permute-done.8.near), channel_id=1, source_target_pairs={{0,1},{1,0},{2,3},{3,2},{4,5},{5,4},{6,7},{7,6},{8,9},{9,8},{10,11... | collective-permute-start | bytes 393224 | tf_op jit(solution)/shard_map/ppermute | solution.py:57
  17.1 2.6 %copy-start.1 = (f32[32,128]{1,0:T(8,128)S(1)}, f32[32,128]{1,0:T(8,128)}, u32[]{:S(2)}) copy-start(f32[32,128]{1,0:T(8,128)} %noise.1) | copy-start | bytes 49156
  20.8 2.9 %collective-permute-start.10 = (bf16[16,256,128]{2,1,0:T(8,128)(2,1)S(1)}, bf16[16,256,128]{2,1,0:T(8,128)(2,1)S(1)}, u32[]{:S(2)}, u32[]{:S(2)}) collective-permute-start(bf16[16,256,128]{2,1,0:T(8,128)(2,1)S(1)} %shard_map.71.mine), channel_id=1, source_target_pairs={{0,1},{1,0},{2,3},{3,2},{4,5},{5,4},{6,7},{7,6},{8,9},{9,8},{10,11... | collective-permute-start | bytes 3145736 | tf_op jit(solution)/shard_map/ppermute | solution.py:57
  24.8 6.0 %collective-permute-start.11 = (s16[272,256]{1,0:T(8,128)(2,1)S(1)}, s16[272,256]{1,0:T(8,128)(2,1)S(1)}, u32[]{:S(2)}, u32[]{:S(2)}) collective-permute-start(s16[272,256]{1,0:T(8,128)(2,1)S(1)} %shard_map.73), channel_id=1, source_target_pairs={{0,2},{2,0},{4,6},{6,4},{8,10},{10,8},{12,14},{14,12},{1,3},{3,1},... | collective-permute-start | bytes 417800 | tf_op jit(solution)/shard_map/ppermute | solution.py:65
  29.3 7.0 %collective-permute-start.14 = (s16[272,256]{1,0:T(8,128)(2,1)S(1)}, s16[272,256]{1,0:T(8,128)(2,1)S(1)}, u32[]{:S(2)}, u32[]{:S(2)}) collective-permute-start(s16[272,256]{1,0:T(8,128)(2,1)S(1)} %shard_map.74), channel_id=1, source_target_pairs={{0,2},{2,0},{4,6},{6,4},{8,10},{10,8},{12,14},{14,12},{1,3},{3,1},... | collective-permute-start | bytes 417800 | tf_op jit(solution)/shard_map/ppermute | solution.py:65
  31.0 8.7 %collective-permute-start.12 = (s16[272,256]{1,0:T(8,128)(2,1)S(1)}, s16[272,256]{1,0:T(8,128)(2,1)S(1)}, u32[]{:S(2)}, u32[]{:S(2)}) collective-permute-start(s16[272,256]{1,0:T(8,128)(2,1)S(1)} %shard_map.76), channel_id=1, source_target_pairs={{0,4},{2,14},{4,8},{6,2},{8,12},{10,6},{12,0},{14,10},{1,5},{3,15}... | collective-permute-start | bytes 417800 | tf_op jit(solution)/shard_map/ppermute | solution.py:70
  31.0 9.8 %collective-permute-start.13 = (s16[272,256]{1,0:T(8,128)(2,1)S(1)}, s16[272,256]{1,0:T(8,128)(2,1)S(1)}, u32[]{:S(2)}, u32[]{:S(2)}) collective-permute-start(s16[272,256]{1,0:T(8,128)(2,1)S(1)} %get-tuple-element.35), channel_id=1, source_target_pairs={{0,12},{2,6},{4,0},{6,10},{8,4},{10,14},{12,8},{14,2},{1,13},{3,7}... | collective-permute-start | bytes 417800 | tf_op jit(solution)/shard_map/ppermute | solution.py:70
  41.2 1.4 %collective-permute-start.15 = (f32[192,128]{1,0:T(8,128)S(1)}, f32[192,128]{1,0:T(8,128)S(1)}, u32[]{:S(2)}, u32[]{:S(2)}) collective-permute-start(f32[192,128]{1,0:T(8,128)S(1)} %get-tuple-element.38), channel_id=1, source_target_pairs={{0,1},{1,0},{2,3},{3,2},{4,5},{5,4},{6,7},{7,6},{8,9},{9,8},{10,11... | collective-permute-start | bytes 294920 | tf_op jit(solution)/shard_map/ppermute | solution.py:57
  42.6 6.0 %collective-permute-start.16 = (f32[192,128]{1,0:T(8,128)S(1)}, f32[192,128]{1,0:T(8,128)S(1)}, u32[]{:S(2)}, u32[]{:S(2)}) collective-permute-start(f32[192,128]{1,0:T(8,128)S(1)} %add.15), channel_id=1, source_target_pairs={{0,2},{2,0},{4,6},{6,4},{8,10},{10,8},{12,14},{14,12},{1,3},{3,1},... | collective-permute-start | bytes 294920 | tf_op jit(solution)/shard_map/ppermute | solution.py:303
  48.6 5.0 %collective-permute-start.17 = (f32[192,128]{1,0:T(8,128)S(1)}, f32[192,128]{1,0:T(8,128)S(1)}, u32[]{:S(2)}, u32[]{:S(2)}) collective-permute-start(f32[192,128]{1,0:T(8,128)S(1)} %add.16), channel_id=1, source_target_pairs={{0,4},{2,6},{4,0},{6,2},{8,12},{10,14},{12,8},{14,10},{1,5},{3,7},... | collective-permute-start | bytes 294920 | tf_op jit(solution)/shard_map/ppermute | solution.py:303
  50.0 9.7 %collective-permute-start.18 = (f32[192,128]{1,0:T(8,128)S(1)}, f32[192,128]{1,0:T(8,128)S(1)}, u32[]{:S(2)}, u32[]{:S(2)}) collective-permute-start(f32[192,128]{1,0:T(8,128)S(1)} %add.16), channel_id=1, source_target_pairs={{0,8},{2,10},{4,12},{6,14},{8,0},{10,2},{12,4},{14,6},{1,9},{3,11}... | collective-permute-start | bytes 294920 | tf_op jit(solution)/shard_map/ppermute | solution.py:303
  50.9 8.8 %collective-permute-start.19 = (f32[192,128]{1,0:T(8,128)S(1)}, f32[192,128]{1,0:T(8,128)S(1)}, u32[]{:S(2)}, u32[]{:S(2)}) collective-permute-start(f32[192,128]{1,0:T(8,128)S(1)} %add.16), channel_id=1, source_target_pairs={{0,12},{2,14},{4,8},{6,10},{8,4},{10,6},{12,0},{14,2},{1,13},{3,15... | collective-permute-start | bytes 294920 | tf_op jit(solution)/shard_map/ppermute | solution.py:303
  59.7 1.4 %collective-permute-start.20 = (f32[192,128]{1,0:T(8,128)S(1)}, f32[192,128]{1,0:T(8,128)S(1)}, u32[]{:S(2)}, u32[]{:S(2)}) collective-permute-start(f32[192,128]{1,0:T(8,128)S(1)} %add_add_fusion.mine), channel_id=1, source_target_pairs={{0,1},{1,0},{2,3},{3,2},{4,5},{5,4},{6,7},{7,6},{8,9},{9,8},{10,11... | collective-permute-start | bytes 294920 | tf_op jit(solution)/shard_map/ppermute | solution.py:57

commit v4 on v3

--- a/solution.py
+++ b/solution.py
@@ -139,8 +139,37 @@
             aside[j, :, side * cells : (side + 1) * cells] = jnp.where(found > 0, block, jnp.zeros_like(block))
 
 
-def late_kernel(live, images, aside, near, far, noise, out):
-    half, _, rows = out.shape
+def gather_kernel(mine, other, out):
+    half = mine.shape[0]
+
+    def step(j, _):
+        out[j] = mine[j]
+        out[half + j] = other[j]
+        return 0
+
+    lax.fori_loop(0, half, step, 0)
+    out[2 * half] = jnp.zeros(out.shape[1:], BF16)
+
+
+def encode(value, out):
+    width = value.shape[0]
+    top = jnp.max(jnp.abs(value), axis=0, keepdims=True)
+    power = jnp.clip(jnp.floor(jnp.log2(jnp.maximum(top, 1e-30))) + 1.0, -96.0, 96.0)
+    coded = jnp.clip(jnp.round(value * jnp.exp2(15.0 - power)), -32767.0, 32767.0)
+    out[:width] = coded.astype(jnp.int32).astype(jnp.int16)
+    rows = jnp.broadcast_to(power.astype(jnp.int32), (PAD, power.shape[1]))
+    out[width:] = rows.astype(jnp.int16)
+
+
+def decode(part):
+    width = part.shape[0] - PAD
+    power = part[width:].astype(jnp.int32).astype(F32)[:1]
+    return part[:width].astype(jnp.int32).astype(F32) * jnp.exp2(power - 15.0)
+
+
+def late_kernel(live, footprint, images, aside, jac_near, jac_far, near, far, noise, out, kept, sent):
+    half, width, rows = out.shape
+    reach, cells = jac_near.shape[1], jac_near.shape[3]
     base = core_index() * half
     band = jnp.concatenate([near[...], far[...]], axis=0)
     size = half // 2
@@ -152,33 +181,22 @@
             image = images[first + j] + product[j * rows : (j + 1) * rows]
             out[first + j] = (image.T * scale).astype(BF16)
 
-
-def gather_kernel(mine, other, out):
-    half = mine.shape[0]
-
-    def step(j, _):
-        out[j] = mine[j]
-        out[half + j] = other[j]
-        return 0
-
-    lax.fori_loop(0, half, step, 0)
-    out[2 * half] = jnp.zeros(out.shape[1:], BF16)
-
-
-def encode(value, out):
-    width = value.shape[0]
-    top = jnp.max(jnp.abs(value), axis=0, keepdims=True)
-    power = jnp.clip(jnp.floor(jnp.log2(jnp.maximum(top, 1e-30))) + 1.0, -96.0, 96.0)
-    coded = jnp.clip(jnp.round(value * jnp.exp2(15.0 - power)), -32767.0, 32767.0)
-    out[:width] = coded.astype(jnp.int32).astype(jnp.int16)
-    rows = jnp.broadcast_to(power.astype(jnp.int32), (PAD, power.shape[1]))
-    out[width:] = rows.astype(jnp.int16)
-
-
-def decode(part):
-    width = part.shape[0] - PAD
-    power = part[width:].astype(jnp.int32).astype(F32)[:1]
-    return part[:width].astype(jnp.int32).astype(F32) * jnp.exp2(power - 15.0)
+    left = jnp.concatenate([out[j] for j in range(half)], axis=1)
+    total = dot(left, jnp.concatenate([aside[j] for j in range(half)], axis=0))
+    kept[0] = total[:, :cells]
+    encode(total[:, cells:], sent.at[0])
+    ahead = place_of("ahead")
+    left, right = [], []
+    for j in range(half):
+        places = [footprint[f, base + j] for f in range(reach)]
+        chosen = sum(f * (places[f] == ahead).astype(jnp.int32) for f in range(reach))
+        found = sum((place == ahead).astype(jnp.int32) for place in places)
+        block = out[j]
+        left.append(jnp.where(found > 0, block, jnp.zeros_like(block)))
+        right.append(jnp.concatenate([jac_near[base + j, chosen], jac_far[base + j, chosen]], axis=1))
+    total = dot(jnp.concatenate(left, axis=1), jnp.concatenate(right, axis=0))
+    kept[1] = total[:, :cells]
+    encode(total[:, cells:], sent.at[1])
 
 
 def backward_kernel(roles, coded, cap, table, jac, weighted, *rest):
@@ -212,6 +230,11 @@
 
 def merge_kernel(value, part, out):
     encode(value[...] + decode(part), out)
+
+
+def merge_two_kernel(kept, sent, first, second):
+    encode(kept[0] + decode(sent.at[0]), first)
+    encode(kept[1] + decode(sent.at[1]), second)
 
 
 def field_kernel(probes, own, *rest):
@@ -347,28 +370,34 @@
         (VMEM,) * 2,
         [pltpu.VMEM((len(OFFSETS), 2 * cells, width), BF16)],
     )(footprint, held(staged, pltpu.VMEM), held(jac_far, pltpu.VMEM), *near, *far)
-    beyond = swapped(back)
-    weighted = kernel_call(
-        late_kernel,
-        jax.ShapeDtypeStruct((half, width, rows), BF16),
-        [SMEM] + [VMEM] * 5,
-        VMEM,
-    )(live, *early, beyond, flipped(beyond), noise_weight)
     table = kernel_call(
         functools.partial(list_kernel, cap, half),
         jax.ShapeDtypeStruct((len(OFFSETS) * (cap + 1),), jnp.int32),
         [SMEM] * 2,
         SMEM,
     )(footprint, live)
+    beyond, table = lax.optimization_barrier((swapped(back), table))
+    plain = jax.ShapeDtypeStruct((width, cells), F32)
+    message = jax.ShapeDtypeStruct((width + PAD, cells), jnp.int16)
+    weighted, kept, sent = kernel_call(
+        late_kernel,
+        (
+            jax.ShapeDtypeStruct((half, width, rows), BF16),
+            jax.ShapeDtypeStruct((2,) + plain.shape, F32),
+            jax.ShapeDtypeStruct((2,) + message.shape, jnp.int16),
+        ),
+        [SMEM] * 2 + [VMEM] * 7,
+        (VMEM,) * 3,
+    )(live, footprint, *early, held(staged, pltpu.VMEM), held(jac_far, pltpu.VMEM), beyond, flipped(beyond), noise_weight)
+    beyond, ahead = kernel_call(merge_two_kernel, (message, message), [VMEM] * 2, (VMEM,) * 2)(kept, flipped(sent))
+    beyond, ahead, weighted = lax.optimization_barrier((beyond, ahead, weighted))
+    beyond, ahead = swapped(beyond), spread(ahead, -2)
     weighted = kernel_call(
         gather_kernel,
         jax.ShapeDtypeStruct((2 * half + 1, width, rows), BF16),
         [VMEM] * 2,
         VMEM,
     )(weighted, flipped(weighted))
-
-    plain = jax.ShapeDtypeStruct((width, cells), F32)
-    message = jax.ShapeDtypeStruct((width + PAD, cells), jnp.int16)
 
     def buckets(roles, coded, weighted):
         return kernel_call(
@@ -379,14 +408,10 @@
             [pltpu.VMEM((width, cells), F32)],
         )(table, held(staged, pltpu.VMEM), weighted)
 
-    beyond = buckets(("beyond",), (True,), weighted)[0]
-    beyond, weighted = lax.optimization_barrier((beyond, weighted))
-    partner = buckets(("partner",), (True,), weighted)[0]
-    partner, weighted = lax.optimization_barrier((partner, weighted))
-    back, ahead = buckets(("back", "ahead"), (False, True), weighted)
-    back = kernel_call(merge_kernel, message, [VMEM] * 2, VMEM)(back, swapped(beyond))
-    back, ahead, weighted = lax.optimization_barrier((back, ahead, weighted))
-    arrived = [spread(back, 2), spread(ahead, -2), swapped(partner)]
+    back, partner = buckets(("back", "partner"), (False, True), weighted)
+    back = kernel_call(merge_kernel, message, [VMEM] * 2, VMEM)(back, beyond)
+    back, partner, weighted = lax.optimization_barrier((back, partner, weighted))
+    arrived = [spread(back, 2), ahead, swapped(partner)]
     own = buckets(("own",), (False,), weighted)[0]
     packed = jax.ShapeDtypeStruct((3 * width // 4, width // 2), F32)
     field, keep, send = kernel_call(

time: 102 us -> 97.9 us (0.960)
  waiting for transfers between devices: 22 us -> 16.3 us
  starting transfers between devices: 23.7 us -> 26.2 us
    ppermute x4, waiting for transfers between devices: 5.89 us -> 2.05 us  [spread(): lax.ppermute(value, 'tile', [(i, (i + (steps, -steps)[i % 2]) % count) fo...]
    ppermute x4, waiting for transfers between devices: 3.38 us -> 0.86 us  [swapped(): lax.ppermute(value, 'tile', [(i, i ^ 1) for i in range(lax.axis_size('til...]
    ppermute x4, starting transfers between devices: 5.59 us -> 7.74 us  [swapped(): lax.ppermute(value, 'tile', [(i, i ^ 1) for i in range(lax.axis_size('til...]
    pallas_call x4 -> x2, Pallas kernels: 4.79 us -> 2.67 us  [buckets(): kernel_call(functools.partial(backward_kernel, roles, coded, cap), [messa...]
    pallas_call x2 -> x3, Pallas kernels: 1.16 us -> 2.76 us  [the longest x1 2.48 us: on_device(): kernel_call(late_kernel, (jax.ShapeDtypeStruct((half, width, rows), BF16)...]
    ppermute x9 -> x10, waiting for transfers between devices: 2.96 us -> 4.3 us  [shifted(): return lax.ppermute(value, axis, pairs)]
    ppermute x9 -> x10, starting transfers between devices: 1.88 us -> 2.05 us  [shifted(): return lax.ppermute(value, axis, pairs)]
  transfers between devices with their start and end apart: 21 -> 22, of which waited for: 11 -> 12; matrix products, arithmetic and copies ran while one was open for 0% -> 0% of each run, Pallas kernels for 11% -> 10%
where the time goes in v4:
time: 97.9 us; the launch traced here: 97.8 us
  Pallas kernels  53.8 us (55%)
  starting transfers between devices  26.2 us (27%)
  waiting for transfers between devices  16.3 us (17%)
  between operations  1.46 us (1%)
    pallas_call x1, Pallas kernels, on_device(): kernel_call(functools.partial(finish_kernel, scale, 2), (jax.ShapeDtypeSt...  40.5 us
    ppermute x4, starting transfers between devices, spread(): lax.ppermute(value, 'tile', [(i, (i + (steps, -steps)[i % 2]) % count) fo...  9.91 us
    ppermute x4, waiting for transfers between devices, exchanged(): return lax.ppermute(value, 'tile', [(i, i ^ jump) for i in range(count)])  9.08 us
    ppermute x4, starting transfers between devices, swapped(): lax.ppermute(value, 'tile', [(i, i ^ 1) for i in range(lax.axis_size('til...  7.74 us
    ppermute x4, starting transfers between devices, exchanged(): return lax.ppermute(value, 'tile', [(i, i ^ jump) for i in range(count)])  6.54 us
    ppermute x10, waiting for transfers between devices, shifted(): return lax.ppermute(value, axis, pairs)  4.3 us
    pallas_call x1, Pallas kernels, on_device(): kernel_call(stage_kernel, pltpu.VMEM(jacobian.shape, BF16), [HBM], VMEM,...  2.79 us
    pallas_call x2, Pallas kernels, buckets(): kernel_call(functools.partial(backward_kernel, roles, coded, cap), [messa...  2.67 us
  transfers between devices with their start and end apart: 22, of which 12 were waited for; matrix products, arithmetic and copies ran while one was open for 0% of the time, Pallas kernels for 10%

profile of v4, /device:TPU:0, one launch (start us, length us, event | category | flops | bytes accessed | tf_op | source)
XLA Modules:
  0.0 97.8 jit_solution(14701419673388630393)
XLA Ops:
  1.2 4.7 %collective-permute-start = (bf16[256,256]{1,0:T(8,128)(2,1)}, bf16[256,256]{1,0:T(8,128)(2,1)S(1)}, u32[]{:S(2)}, u32[]{:S(2)}) collective-permute-start(bf16[256,256]{1,0:T(8,128)(2,1)} %bitcast.3), channel_id=1, source_target_pairs={{0,12},{2,6},{4,0},{6,10},{8,4},{10,14},{12,8},{14,2},{1,13},{3,7}... | collective-permute-start | bytes 393224 | tf_op jit(solution)/shard_map/ppermute | solution.py:70
  5.8 1.0 %collective-permute-start.3 = (bf16[256,256]{1,0:T(8,128)(2,1)}, bf16[256,256]{1,0:T(8,128)(2,1)S(1)}, u32[]{:S(2)}, u32[]{:S(2)}) collective-permute-start(bf16[256,256]{1,0:T(8,128)(2,1)} %bitcast.5), channel_id=1, source_target_pairs={{0,4},{2,14},{4,8},{6,2},{8,12},{10,6},{12,0},{14,10},{1,5},{3,15}... | collective-permute-start | bytes 393224 | tf_op jit(solution)/shard_map/ppermute | solution.py:70
  6.9 2.8 %shard_map.68.jac_near.jac = bf16[32,3,128,256]{3,2,1,0:T(8,128)(2,1)S(1)} custom-call(bf16[32,3,128,256]{3,2,1,0:T(8,128)(2,1)} %value.1), custom_call_target="tpu_custom_call" | custom-call | flops 1024 | bytes 1024 | tf_op jit(solution)/shard_map/pallas_call | solution.py:350
  10.0 2.1 %collective-permute-start.1 = (bf16[256,256]{1,0:T(8,128)(2,1)S(1)}, bf16[256,256]{1,0:T(8,128)(2,1)S(1)}, u32[]{:S(2)}, u32[]{:S(2)}) collective-permute-start(bf16[256,256]{1,0:T(8,128)(2,1)S(1)} %collective-permute-done.rest_1_), channel_id=1, source_target_pairs={{0,2},{2,0},{4,6},{6,4},{8,10},{10,8},{12,14},{14,12},{1,3},{3,1},... | collective-permute-start | bytes 393224 | tf_op jit(solution)/shard_map/ppermute | solution.py:65
  12.7 1.9 %shard_map.69.table = s32[165]{0:T(256)S(1)} custom-call(s32[3,32]{1,0:T(4,128)S(1)} %bitcast.9, s32[1]{0:T(128)S(6)} %copy.7.live), custom_call_target="tpu_custom_call" | custom-call | flops 1024 | bytes 1024 | tf_op jit(solution)/shard_map/pallas_call | solution.py:373
  15.5 0.7 collective-permute-done.1.near
  16.6 2.6 %shard_map.70 = (f32[16,128,256]{2,1,0:T(8,128)S(1)}, bf16[16,128,512]{2,1,0:T(8,128)(2,1)S(1)}) custom-call(s32[3,32]{1,0:T(4,128)S(1)} %bitcast.10, bf16[32,3,128,256]{3,2,1,0:T(8,128)(2,1)S(1)} %shard_map.68.jac_near.jac, bf16[32,3,128,256]{3,2,1,0:T(8,128)(2,1)S(1)} %collective-permute-done.2.jac_far, bf16[256,256]{1,0:T(8,128)(2,1)S(1)} %bitcast.7, ...), custom_call_target="tpu_custom_call" | custom-call | flops 1024 | bytes 1024 | tf_op jit(solution)/shard_map/pallas_call | solution.py:363
  19.2 2.5 %shard_map.71 = (bf16[16,256,128]{2,1,0:T(8,128)(2,1)S(1)}, f32[2,256,256]{2,1,0:T(8,128)S(1)}, s16[2,272,256]{2,1,0:T(8,128)(2,1)S(1)}) custom-call(s32[1]{0:T(128)S(6)} %copy.7.live, s32[3,32]{1,0:T(4,128)S(1)} %bitcast.11, f32[16,128,256]{2,1,0:T(8,128)S(1)} %get-tuple-element.33.images, bf16[16,128,512]{2,1,0:T(8,128)(2,1)S(1)} %get-tuple-element.34.aside, ...), custom_call_target="tpu_custom_call" | custom-call | flops 1024 | bytes 1024 | tf_op jit(solution)/shard_map/pallas_call | solution.py:382
  22.0 1.3 %collective-permute-done.10.sent = s16[2,272,256]{2,1,0:T(8,128)(2,1)S(1)} collective-permute-done((s16[2,272,256]{2,1,0:T(8,128)(2,1)S(1)}, s16[2,272,256]{2,1,0:T(8,128)(2,1)S(1)}, u32[]{:S(2)}, u32[]{:S(2)}) %collective-permute-start.10) | collective-permute-done | bytes 278560 | tf_op jit(solution)/shard_map/ppermute | solution.py:57
  23.8 1.7 %collective-permute-start.12 = (s16[272,256]{1,0:T(8,128)(2,1)S(1)}, s16[272,256]{1,0:T(8,128)(2,1)S(1)}, u32[]{:S(2)}, u32[]{:S(2)}) collective-permute-start(s16[272,256]{1,0:T(8,128)(2,1)S(1)} %get-tuple-element.43), channel_id=1, source_target_pairs={{0,2},{2,0},{4,6},{6,4},{8,10},{10,8},{12,14},{14,12},{1,3},{3,1},... | collective-permute-start | bytes 417800 | tf_op jit(solution)/shard_map/ppermute | solution.py:65
  25.5 4.1 %collective-permute-start.14 = (s16[272,256]{1,0:T(8,128)(2,1)S(1)}, s16[272,256]{1,0:T(8,128)(2,1)S(1)}, u32[]{:S(2)}, u32[]{:S(2)}) collective-permute-start(s16[272,256]{1,0:T(8,128)(2,1)S(1)} %get-tuple-element.47), channel_id=1, source_target_pairs={{0,12},{2,6},{4,0},{6,10},{8,4},{10,14},{12,8},{14,2},{1,13},{3,7}... | collective-permute-start | bytes 417800 | tf_op jit(solution)/shard_map/ppermute | solution.py:70
  29.8 1.5 %shard_map.74 = (f32[256,256]{1,0:T(8,128)S(1)}, s16[272,256]{1,0:T(8,128)(2,1)S(1)}) custom-call(s32[165]{0:T(256)S(1)} %shard_map.69.table, bf16[32,3,128,256]{3,2,1,0:T(8,128)(2,1)S(1)} %shard_map.68.jac_near.jac, bf16[33,256,128]{2,1,0:T(8,128)(2,1)S(1)} %shard_map.73.weighted), custom_call_target="tpu_custom_call" | custom-call | flops 1024 | bytes 1024 | tf_op jit(solution)/shard_map/pallas_call | solution.py:403
  31.5 4.0 %collective-permute-start.15 = (s16[272,256]{1,0:T(8,128)(2,1)S(1)}, s16[272,256]{1,0:T(8,128)(2,1)S(1)}, u32[]{:S(2)}, u32[]{:S(2)}) collective-permute-start(s16[272,256]{1,0:T(8,128)(2,1)S(1)} %get-tuple-element.48), channel_id=1, source_target_pairs={{0,2},{2,0},{4,6},{6,4},{8,10},{10,8},{12,14},{14,12},{1,3},{3,1},... | collective-permute-start | bytes 417800 | tf_op jit(solution)/shard_map/ppermute | solution.py:65
  35.5 1.2 %shard_map.76.own = f32[256,256]{1,0:T(8,128)S(1)} custom-call(s32[165]{0:T(256)S(1)} %shard_map.69.table, bf16[32,3,128,256]{3,2,1,0:T(8,128)(2,1)S(1)} %shard_map.68.jac_near.jac, bf16[33,256,128]{2,1,0:T(8,128)(2,1)S(1)} %shard_map.73.weighted), custom_call_target="tpu_custom_call" | custom-call | flops 1024 | bytes 1024 | tf_op jit(solution)/shard_map/pallas_call | solution.py:403
  36.7 1.7 %collective-permute-done.13.rest_0_ = s16[272,256]{1,0:T(8,128)(2,1)S(1)} collective-permute-done((s16[272,256]{1,0:T(8,128)(2,1)S(1)}, s16[272,256]{1,0:T(8,128)(2,1)S(1)}, u32[]{:S(2)}, u32[]{:S(2)}) %collective-permute-start.13) | collective-permute-done | bytes 139296 | tf_op jit(solution)/shard_map/ppermute | solution.py:70
  39.0 1.3 %collective-permute-done.16 = f32[192,128]{1,0:T(8,128)S(1)} collective-permute-done((f32[192,128]{1,0:T(8,128)S(1)}, f32[192,128]{1,0:T(8,128)S(1)}, u32[]{:S(2)}, u32[]{:S(2)}) %collective-permute-start.16) | collective-permute-done | bytes 98336 | tf_op jit(solution)/shard_map/ppermute | solution.py:57
  40.3 2.1 %collective-permute-start.17 = (f32[192,128]{1,0:T(8,128)S(1)}, f32[192,128]{1,0:T(8,128)S(1)}, u32[]{:S(2)}, u32[]{:S(2)}) collective-permute-start(f32[192,128]{1,0:T(8,128)S(1)} %add.15), channel_id=1, source_target_pairs={{0,2},{2,0},{4,6},{6,4},{8,10},{10,8},{12,14},{14,12},{1,3},{3,1},... | collective-permute-start | bytes 294920 | tf_op jit(solution)/shard_map/ppermute | solution.py:326
  42.4 3.1 %collective-permute-done.17 = f32[192,128]{1,0:T(8,128)S(1)} collective-permute-done((f32[192,128]{1,0:T(8,128)S(1)}, f32[192,128]{1,0:T(8,128)S(1)}, u32[]{:S(2)}, u32[]{:S(2)}) %collective-permute-start.17) | collective-permute-done | bytes 98336 | tf_op jit(solution)/shard_map/ppermute | solution.py:326
  45.5 1.9 %collective-permute-start.20 = (f32[192,128]{1,0:T(8,128)S(1)}, f32[192,128]{1,0:T(8,128)S(1)}, u32[]{:S(2)}, u32[]{:S(2)}) collective-permute-start(f32[192,128]{1,0:T(8,128)S(1)} %add.16), channel_id=1, source_target_pairs={{0,12},{2,14},{4,8},{6,10},{8,4},{10,6},{12,0},{14,2},{1,13},{3,15... | collective-permute-start | bytes 294920 | tf_op jit(solution)/shard_map/ppermute | solution.py:326
  47.4 2.6 %collective-permute-start.18 = (f32[192,128]{1,0:T(8,128)S(1)}, f32[192,128]{1,0:T(8,128)S(1)}, u32[]{:S(2)}, u32[]{:S(2)}) collective-permute-start(f32[192,128]{1,0:T(8,128)S(1)} %add.16), channel_id=1, source_target_pairs={{0,4},{2,6},{4,0},{6,2},{8,12},{10,14},{12,8},{14,10},{1,5},{3,7},... | collective-permute-start | bytes 294920 | tf_op jit(solution)/shard_map/ppermute | solution.py:326
  50.0 3.2 %collective-permute-done.20 = f32[192,128]{1,0:T(8,128)S(1)} collective-permute-done((f32[192,128]{1,0:T(8,128)S(1)}, f32[192,128]{1,0:T(8,128)S(1)}, u32[]{:S(2)}, u32[]{:S(2)}) %collective-permute-start.20) | collective-permute-done | bytes 98336 | tf_op jit(solution)/shard_map/ppermute | solution.py:326
  53.2 2.7 %collective-permute-done.19 = f32[192,128]{1,0:T(8,128)S(1)} collective-permute-done((f32[192,128]{1,0:T(8,128)S(1)}, f32[192,128]{1,0:T(8,128)S(1)}, u32[]{:S(2)}, u32[]{:S(2)}) %collective-permute-start.19) | collective-permute-done | bytes 98336 | tf_op jit(solution)/shard_map/ppermute | solution.py:326
  56.1 1.3 %collective-permute-done.21.other = f32[192,128]{1,0:T(8,128)S(1)} collective-permute-done((f32[192,128]{1,0:T(8,128)S(1)}, f32[192,128]{1,0:T(8,128)S(1)}, u32[]{:S(2)}, u32[]{:S(2)}) %collective-permute-start.21) | collective-permute-done | bytes 98336 | tf_op jit(solution)/shard_map/ppermute | solution.py:57
  57.3 40.5 %shard_map.78 = (f32[256,256]{1,0:T(8,128)}, f32[256,256]{1,0:T(8,128)}) custom-call(f32[192,128]{1,0:T(8,128)S(1)} %add_add_fusion.mine, f32[192,128]{1,0:T(8,128)S(1)} %collective-permute-done.21.other, f32[256,256]{1,0:T(8,128)S(1)} %get-tuple-element.51.field), custom_call_target="tpu_custom_call" | custom-call | flops 1024 | bytes 1024 | tf_op jit(solution)/shard_map/pallas_call | solution.py:426
  (40 shorter events, 3.9 us)
Async XLA Ops:
  0.6 16.0 %collective-permute-start.2 = (bf16[32,3,128,256]{3,2,1,0:T(8,128)(2,1)}, bf16[32,3,128,256]{3,2,1,0:T(8,128)(2,1)S(1)}, u32[]{:S(2)}, u32[]{:S(2)}) collective-permute-start(bf16[32,3,128,256]{3,2,1,0:T(8,128)(2,1)} %value.1), channel_id=1, source_target_pairs={{0,1},{1,0},{2,3},{3,2},{4,5},{5,4},{6,7},{7,6},{8,9},{9,8},{10,11... | collective-permute-start | bytes 18874376 | tf_op jit(solution)/shard_map/ppermute | solution.py:57
  1.1 11.6 %copy-start.1 = (s32[32,3]{0,1:T(4,128)S(1)}, s32[32,3]{0,1:T(4,128)}, u32[]{:S(2)}) copy-start(s32[32,3]{0,1:T(4,128)} %param.6) | copy-start | bytes 1156
  1.1 13.5 %copy-start = (bf16[1,256,256]{2,1,0:T(8,128)(2,1)S(1)}, bf16[1,256,256]{2,1,0:T(8,128)(2,1)}, u32[]{:S(2)}) copy-start(bf16[1,256,256]{2,1,0:T(8,128)(2,1)} %param.9) | copy-start | bytes 393220
  1.2 8.9 %collective-permute-start = (bf16[256,256]{1,0:T(8,128)(2,1)}, bf16[256,256]{1,0:T(8,128)(2,1)S(1)}, u32[]{:S(2)}, u32[]{:S(2)}) collective-permute-start(bf16[256,256]{1,0:T(8,128)(2,1)} %bitcast.3), channel_id=1, source_target_pairs={{0,12},{2,6},{4,0},{6,10},{8,4},{10,14},{12,8},{14,2},{1,13},{3,7}... | collective-permute-start | bytes 393224 | tf_op jit(solution)/shard_map/ppermute | solution.py:70
  5.8 8.8 %collective-permute-start.4 = (bf16[256,256]{1,0:T(8,128)(2,1)}, bf16[256,256]{1,0:T(8,128)(2,1)S(1)}, u32[]{:S(2)}, u32[]{:S(2)}) collective-permute-start(bf16[256,256]{1,0:T(8,128)(2,1)} %bitcast.4), channel_id=1, source_target_pairs={{0,2},{2,0},{4,6},{6,4},{8,10},{10,8},{12,14},{14,12},{1,3},{3,1},... | collective-permute-start | bytes 393224 | tf_op jit(solution)/shard_map/ppermute | solution.py:65
  5.8 9.1 %collective-permute-start.3 = (bf16[256,256]{1,0:T(8,128)(2,1)}, bf16[256,256]{1,0:T(8,128)(2,1)S(1)}, u32[]{:S(2)}, u32[]{:S(2)}) collective-permute-start(bf16[256,256]{1,0:T(8,128)(2,1)} %bitcast.5), channel_id=1, source_target_pairs={{0,4},{2,14},{4,8},{6,2},{8,12},{10,6},{12,0},{14,10},{1,5},{3,15}... | collective-permute-start | bytes 393224 | tf_op jit(solution)/shard_map/ppermute | solution.py:70
  10.0 5.0 %collective-permute-start.6 = (bf16[256,256]{1,0:T(8,128)(2,1)S(1)}, bf16[256,256]{1,0:T(8,128)(2,1)S(1)}, u32[]{:S(2)}, u32[]{:S(2)}) collective-permute-start(bf16[256,256]{1,0:T(8,128)(2,1)S(1)} %collective-permute-done.rest_1_), channel_id=1, source_target_pairs={{0,1},{1,0},{2,3},{3,2},{4,5},{5,4},{6,7},{7,6},{8,9},{9,8},{10,11... | collective-permute-start | bytes 393224 | tf_op jit(solution)/shard_map/ppermute | solution.py:57
  10.0 6.2 %collective-permute-start.1 = (bf16[256,256]{1,0:T(8,128)(2,1)S(1)}, bf16[256,256]{1,0:T(8,128)(2,1)S(1)}, u32[]{:S(2)}, u32[]{:S(2)}) collective-permute-start(bf16[256,256]{1,0:T(8,128)(2,1)S(1)} %collective-permute-done.rest_1_), channel_id=1, source_target_pairs={{0,2},{2,0},{4,6},{6,4},{8,10},{10,8},{12,14},{14,12},{1,3},{3,1},... | collective-permute-start | bytes 393224 | tf_op jit(solution)/shard_map/ppermute | solution.py:65
  14.7 1.6 %collective-permute-start.5 = (bf16[256,256]{1,0:T(8,128)(2,1)S(1)}, bf16[256,256]{1,0:T(8,128)(2,1)S(1)}, u32[]{:S(2)}, u32[]{:S(2)}) collective-permute-start(bf16[256,256]{1,0:T(8,128)(2,1)S(1)} %bitcast.6), channel_id=1, source_target_pairs={{0,1},{1,0},{2,3},{3,2},{4,5},{5,4},{6,7},{7,6},{8,9},{9,8},{10,11... | collective-permute-start | bytes 393224 | tf_op jit(solution)/shard_map/ppermute | solution.py:57
  15.0 1.4 %collective-permute-start.7 = (bf16[256,256]{1,0:T(8,128)(2,1)S(1)}, bf16[256,256]{1,0:T(8,128)(2,1)S(1)}, u32[]{:S(2)}, u32[]{:S(2)}) collective-permute-start(bf16[256,256]{1,0:T(8,128)(2,1)S(1)} %collective-permute-done.3.rest_2_), channel_id=1, source_target_pairs={{0,1},{1,0},{2,3},{3,2},{4,5},{5,4},{6,7},{7,6},{8,9},{9,8},{10,11... | collective-permute-start | bytes 393224 | tf_op jit(solution)/shard_map/ppermute | solution.py:57
  15.3 1.3 %collective-permute-start.8 = (bf16[256,256]{1,0:T(8,128)(2,1)S(1)}, bf16[256,256]{1,0:T(8,128)(2,1)S(1)}, u32[]{:S(2)}, u32[]{:S(2)}) collective-permute-start(bf16[256,256]{1,0:T(8,128)(2,1)S(1)} %collective-permute-done.4.rest_3_), channel_id=1, source_target_pairs={{0,1},{1,0},{2,3},{3,2},{4,5},{5,4},{6,7},{7,6},{8,9},{9,8},{10,11... | collective-permute-start | bytes 393224 | tf_op jit(solution)/shard_map/ppermute | solution.py:57
  16.2 3.0 %collective-permute-start.9 = (bf16[256,256]{1,0:T(8,128)(2,1)S(1)}, bf16[256,256]{1,0:T(8,128)(2,1)S(1)}, u32[]{:S(2)}, u32[]{:S(2)}) collective-permute-start(bf16[256,256]{1,0:T(8,128)(2,1)S(1)} %collective-permute-done.1.near), channel_id=1, source_target_pairs={{0,1},{1,0},{2,3},{3,2},{4,5},{5,4},{6,7},{7,6},{8,9},{9,8},{10,11... | collective-permute-start | bytes 393224 | tf_op jit(solution)/shard_map/ppermute | solution.py:57
  21.7 1.6 %collective-permute-start.10 = (s16[2,272,256]{2,1,0:T(8,128)(2,1)S(1)}, s16[2,272,256]{2,1,0:T(8,128)(2,1)S(1)}, u32[]{:S(2)}, u32[]{:S(2)}) collective-permute-start(s16[2,272,256]{2,1,0:T(8,128)(2,1)S(1)} %get-tuple-element.37), channel_id=1, source_target_pairs={{0,1},{1,0},{2,3},{3,2},{4,5},{5,4},{6,7},{7,6},{8,9},{9,8},{10,11... | collective-permute-start | bytes 835592 | tf_op jit(solution)/shard_map/ppermute | solution.py:57
  23.5 6.1 %collective-permute-start.11 = (bf16[16,256,128]{2,1,0:T(8,128)(2,1)S(1)}, bf16[16,256,128]{2,1,0:T(8,128)(2,1)S(1)}, u32[]{:S(2)}, u32[]{:S(2)}) collective-permute-start(bf16[16,256,128]{2,1,0:T(8,128)(2,1)S(1)} %get-tuple-element.41.mine), channel_id=1, source_target_pairs={{0,1},{1,0},{2,3},{3,2},{4,5},{5,4},{6,7},{7,6},{8,9},{9,8},{10,11... | collective-permute-start | bytes 3145736 | tf_op jit(solution)/shard_map/ppermute | solution.py:57
  23.8 7.5 %collective-permute-start.12 = (s16[272,256]{1,0:T(8,128)(2,1)S(1)}, s16[272,256]{1,0:T(8,128)(2,1)S(1)}, u32[]{:S(2)}, u32[]{:S(2)}) collective-permute-start(s16[272,256]{1,0:T(8,128)(2,1)S(1)} %get-tuple-element.43), channel_id=1, source_target_pairs={{0,2},{2,0},{4,6},{6,4},{8,10},{10,8},{12,14},{14,12},{1,3},{3,1},... | collective-permute-start | bytes 417800 | tf_op jit(solution)/shard_map/ppermute | solution.py:65
  25.5 11.2 %collective-permute-start.14 = (s16[272,256]{1,0:T(8,128)(2,1)S(1)}, s16[272,256]{1,0:T(8,128)(2,1)S(1)}, u32[]{:S(2)}, u32[]{:S(2)}) collective-permute-start(s16[272,256]{1,0:T(8,128)(2,1)S(1)} %get-tuple-element.47), channel_id=1, source_target_pairs={{0,12},{2,6},{4,0},{6,10},{8,4},{10,14},{12,8},{14,2},{1,13},{3,7}... | collective-permute-start | bytes 417800 | tf_op jit(solution)/shard_map/ppermute | solution.py:70
  31.4 7.0 %collective-permute-start.13 = (s16[272,256]{1,0:T(8,128)(2,1)S(1)}, s16[272,256]{1,0:T(8,128)(2,1)S(1)}, u32[]{:S(2)}, u32[]{:S(2)}) collective-permute-start(s16[272,256]{1,0:T(8,128)(2,1)S(1)} %shard_map.75), channel_id=1, source_target_pairs={{0,4},{2,14},{4,8},{6,2},{8,12},{10,6},{12,0},{14,10},{1,5},{3,15}... | collective-permute-start | bytes 417800 | tf_op jit(solution)/shard_map/ppermute | solution.py:70
  31.5 7.1 %collective-permute-start.15 = (s16[272,256]{1,0:T(8,128)(2,1)S(1)}, s16[272,256]{1,0:T(8,128)(2,1)S(1)}, u32[]{:S(2)}, u32[]{:S(2)}) collective-permute-start(s16[272,256]{1,0:T(8,128)(2,1)S(1)} %get-tuple-element.48), channel_id=1, source_target_pairs={{0,2},{2,0},{4,6},{6,4},{8,10},{10,8},{12,14},{14,12},{1,3},{3,1},... | collective-permute-start | bytes 417800 | tf_op jit(solution)/shard_map/ppermute | solution.py:65
  38.9 1.4 %collective-permute-start.16 = (f32[192,128]{1,0:T(8,128)S(1)}, f32[192,128]{1,0:T(8,128)S(1)}, u32[]{:S(2)}, u32[]{:S(2)}) collective-permute-start(f32[192,128]{1,0:T(8,128)S(1)} %get-tuple-element.50), channel_id=1, source_target_pairs={{0,1},{1,0},{2,3},{3,2},{4,5},{5,4},{6,7},{7,6},{8,9},{9,8},{10,11... | collective-permute-start | bytes 294920 | tf_op jit(solution)/shard_map/ppermute | solution.py:57
  40.3 5.2 %collective-permute-start.17 = (f32[192,128]{1,0:T(8,128)S(1)}, f32[192,128]{1,0:T(8,128)S(1)}, u32[]{:S(2)}, u32[]{:S(2)}) collective-permute-start(f32[192,128]{1,0:T(8,128)S(1)} %add.15), channel_id=1, source_target_pairs={{0,2},{2,0},{4,6},{6,4},{8,10},{10,8},{12,14},{14,12},{1,3},{3,1},... | collective-permute-start | bytes 294920 | tf_op jit(solution)/shard_map/ppermute | solution.py:326
  45.5 7.7 %collective-permute-start.20 = (f32[192,128]{1,0:T(8,128)S(1)}, f32[192,128]{1,0:T(8,128)S(1)}, u32[]{:S(2)}, u32[]{:S(2)}) collective-permute-start(f32[192,128]{1,0:T(8,128)S(1)} %add.16), channel_id=1, source_target_pairs={{0,12},{2,14},{4,8},{6,10},{8,4},{10,6},{12,0},{14,2},{1,13},{3,15... | collective-permute-start | bytes 294920 | tf_op jit(solution)/shard_map/ppermute | solution.py:326
  47.4 8.6 %collective-permute-start.19 = (f32[192,128]{1,0:T(8,128)S(1)}, f32[192,128]{1,0:T(8,128)S(1)}, u32[]{:S(2)}, u32[]{:S(2)}) collective-permute-start(f32[192,128]{1,0:T(8,128)S(1)} %add.16), channel_id=1, source_target_pairs={{0,8},{2,10},{4,12},{6,14},{8,0},{10,2},{12,4},{14,6},{1,9},{3,11}... | collective-permute-start | bytes 294920 | tf_op jit(solution)/shard_map/ppermute | solution.py:326
  47.4 8.6 %collective-permute-start.18 = (f32[192,128]{1,0:T(8,128)S(1)}, f32[192,128]{1,0:T(8,128)S(1)}, u32[]{:S(2)}, u32[]{:S(2)}) collective-permute-start(f32[192,128]{1,0:T(8,128)S(1)} %add.16), channel_id=1, source_target_pairs={{0,4},{2,6},{4,0},{6,2},{8,12},{10,14},{12,8},{14,10},{1,5},{3,7},... | collective-permute-start | bytes 294920 | tf_op jit(solution)/shard_map/ppermute | solution.py:326
  56.0 1.4 %collective-permute-start.21 = (f32[192,128]{1,0:T(8,128)S(1)}, f32[192,128]{1,0:T(8,128)S(1)}, u32[]{:S(2)}, u32[]{:S(2)}) collective-permute-start(f32[192,128]{1,0:T(8,128)S(1)} %add_add_fusion.mine), channel_id=1, source_target_pairs={{0,1},{1,0},{2,3},{3,2},{4,5},{5,4},{6,7},{7,6},{8,9},{9,8},{10,11... | collective-permute-start | bytes 294920 | tf_op jit(solution)/shard_map/ppermute | solution.py:57
  (1 other events, 4.6 us)

commit v5 on v4

--- a/solution.py
+++ b/solution.py
@@ -14,6 +14,7 @@
 NT = (((1,), (1,)), ((), ()))
 OFFSETS = (-2, -1, 0, 1, 2)
 PAD = 16
+ROWS = 8
 LIMIT = 16 << 20
 VMEM = pl.BlockSpec(memory_space=pltpu.VMEM)
 SMEM = pl.BlockSpec(memory_space=pltpu.SMEM)
@@ -247,12 +248,32 @@
     both = halves(total)
     gram = dot3(both, both, NT)
     mid, quarter = width // 2, width // 4
-    lower = [gram[:mid, :mid], gram[mid : mid + quarter, :mid]]
-    upper = [gram[mid:, mid:], gram[mid + quarter :, :mid]]
     first = core_index() == 0
-    low, high = jnp.concatenate(lower, axis=0), jnp.concatenate(upper, axis=0)
+    corner = gram[mid:, :mid]
+    folded, ends = fold(gram[:mid, :mid], gram[mid:, mid:])
+    low = jnp.concatenate([corner[:quarter], folded[:quarter], ends], axis=0)
+    high = jnp.concatenate([corner[quarter:], folded[quarter:], ends], axis=0)
     keep[...] = jnp.where(first, low, high)
     send[...] = jnp.where(first, high, low)
+
+
+def positions(square):
+    row = lax.broadcasted_iota(jnp.int32, square.shape, 0)
+    return row, lax.broadcasted_iota(jnp.int32, square.shape, 1)
+
+
+def fold(lower, upper):
+    row, column = positions(lower)
+    diagonal = jnp.sum(jnp.where(row == column, upper, 0.0), axis=0, keepdims=True)
+    return jnp.where(row >= column, lower, upper), jnp.broadcast_to(diagonal, (ROWS, lower.shape[1]))
+
+
+def unfold(folded, ends):
+    row, column = positions(folded)
+    other = folded.T
+    lower = jnp.where(row >= column, folded, other)
+    upper = jnp.where(row < column, folded, other)
+    return lower, jnp.where(row == column, ends[:1], upper)
 
 
 def finish_kernel(scale, rounds, mine, other, field, basis, factor, gram, inverse, a_high, a_low):
@@ -261,9 +282,9 @@
     first = core_index() == 0
     low = jnp.where(first, mine[...], other[...])
     high = jnp.where(first, other[...], mine[...])
-    corner = jnp.concatenate([low[mid:], high[mid:]], axis=0)
-    gram[:mid, :mid] = low[:mid]
-    gram[mid:, mid:] = high[:mid]
+    folded = jnp.concatenate([low[quarter:mid], high[quarter:mid]], axis=0)
+    gram[:mid, :mid], gram[mid:, mid:] = unfold(folded, low[mid:])
+    corner = jnp.concatenate([low[:quarter], high[:quarter]], axis=0)
     gram[mid:, :mid] = corner
     gram[:mid, mid:] = corner.T
     matrix = gram[...]
@@ -287,8 +308,11 @@
         now = exact.astype(BF16)
     full = halves(exact)
     error = dot3(halves(dot3(full, (a_high[...], a_low[...]))), full, NT) - eye
-    inverse[...] = (exact - dot(correction(error), full[0])) * along
     left = jnp.sum(error * error)
+    solution_of = (exact - dot(correction(error), full[0])) * along
+    inverse[...] = solution_of
+    upper = dot3(halves(solution_of), halves(matrix)) * (1.0 / scale)
+    factor[...] = jnp.where(row <= column, upper, 0.0)
 
     @pl.when(jnp.logical_not(left < 1e-2))
     def _():
@@ -304,6 +328,7 @@
             below = jnp.sum(jnp.where(column == k, now, 0.0), axis=1, keepdims=True)
             below = jnp.where(down_at > k, below * lax.rsqrt(pivot), 0.0)
             done = inverse[pl.ds(k, 1), :] * lax.rsqrt(pivot)
+            factor[pl.ds(k, 1), :] = jnp.where(across >= k, scaled * (1.0 / scale), 0.0)
             gram[...] = now - below * scaled
             inverse[...] = inverse[...] - below * done
             inverse[pl.ds(k, 1), :] = done
@@ -312,8 +337,6 @@
         lax.fori_loop(0, width, eliminate, 0)
 
     solved = halves(inverse[...])
-    upper = dot3(solved, halves(matrix)) * (1.0 / scale)
-    factor[...] = jnp.where(row <= column, upper, 0.0)
     basis[...] = (dot3(solved, halves(field[...])) * scale).T
 
 
@@ -413,7 +436,7 @@
     back, partner, weighted = lax.optimization_barrier((back, partner, weighted))
     arrived = [spread(back, 2), ahead, swapped(partner)]
     own = buckets(("own",), (False,), weighted)[0]
-    packed = jax.ShapeDtypeStruct((3 * width // 4, width // 2), F32)
+    packed = jax.ShapeDtypeStruct((width // 2 + ROWS, width // 2), F32)
     field, keep, send = kernel_call(
         field_kernel,
         (plain, packed, packed),

time: 97.9 us -> 96.2 us (0.983)
  waiting for transfers between devices: 16.3 us -> 13.8 us
    ppermute x4, waiting for transfers between devices: 9.08 us -> 6.63 us  [exchanged(): return lax.ppermute(value, 'tile', [(i, i ^ jump) for i in range(count)])]
  transfers between devices with their start and end apart: 22 -> 22, of which waited for: 12 -> 12; matrix products, arithmetic and copies ran while one was open for 0% -> 0% of each run, Pallas kernels for 10% -> 11%
where the time goes in v5:
time: 96.2 us; the launch traced here: 96.1 us
  Pallas kernels  54.6 us (57%)
  starting transfers between devices  26.2 us (27%)
  waiting for transfers between devices  13.8 us (14%)
  between operations  1.47 us (2%)
    pallas_call x1, Pallas kernels, on_device(): kernel_call(functools.partial(finish_kernel, scale, 2), (jax.ShapeDtypeSt...  41.4 us
    ppermute x4, starting transfers between devices, spread(): lax.ppermute(value, 'tile', [(i, (i + (steps, -steps)[i % 2]) % count) fo...  9.9 us
    ppermute x4, starting transfers between devices, swapped(): lax.ppermute(value, 'tile', [(i, i ^ 1) for i in range(lax.axis_size('til...  7.74 us
    ppermute x4, waiting for transfers between devices, exchanged(): return lax.ppermute(value, 'tile', [(i, i ^ jump) for i in range(count)])  6.63 us
    ppermute x4, starting transfers between devices, exchanged(): return lax.ppermute(value, 'tile', [(i, i ^ jump) for i in range(count)])  6.54 us
    ppermute x10, waiting for transfers between devices, shifted(): return lax.ppermute(value, axis, pairs)  4.21 us
    pallas_call x1, Pallas kernels, on_device(): kernel_call(stage_kernel, pltpu.VMEM(jacobian.shape, BF16), [HBM], VMEM,...  2.79 us
    pallas_call x2, Pallas kernels, buckets(): kernel_call(functools.partial(backward_kernel, roles, coded, cap), [messa...  2.67 us
  transfers between devices with their start and end apart: 22, of which 12 were waited for; matrix products, arithmetic and copies ran while one was open for 0% of the time, Pallas kernels for 11%

profile of v5, /device:TPU:0, one launch (start us, length us, event | category | flops | bytes accessed | tf_op | source)
XLA Modules:
  0.0 96.1 jit_solution(3327474466389708583)
XLA Ops:
  1.2 4.7 %collective-permute-start = (bf16[256,256]{1,0:T(8,128)(2,1)}, bf16[256,256]{1,0:T(8,128)(2,1)S(1)}, u32[]{:S(2)}, u32[]{:S(2)}) collective-permute-start(bf16[256,256]{1,0:T(8,128)(2,1)} %bitcast.3), channel_id=1, source_target_pairs={{0,12},{2,6},{4,0},{6,10},{8,4},{10,14},{12,8},{14,2},{1,13},{3,7}... | collective-permute-start | bytes 393224 | tf_op jit(solution)/shard_map/ppermute | solution.py:71
  5.8 1.0 %collective-permute-start.3 = (bf16[256,256]{1,0:T(8,128)(2,1)}, bf16[256,256]{1,0:T(8,128)(2,1)S(1)}, u32[]{:S(2)}, u32[]{:S(2)}) collective-permute-start(bf16[256,256]{1,0:T(8,128)(2,1)} %bitcast.5), channel_id=1, source_target_pairs={{0,4},{2,14},{4,8},{6,2},{8,12},{10,6},{12,0},{14,10},{1,5},{3,15}... | collective-permute-start | bytes 393224 | tf_op jit(solution)/shard_map/ppermute | solution.py:71
  6.9 2.8 %shard_map.68.jac_near.jac = bf16[32,3,128,256]{3,2,1,0:T(8,128)(2,1)S(1)} custom-call(bf16[32,3,128,256]{3,2,1,0:T(8,128)(2,1)} %value.1), custom_call_target="tpu_custom_call" | custom-call | flops 1024 | bytes 1024 | tf_op jit(solution)/shard_map/pallas_call | solution.py:373
  10.0 2.1 %collective-permute-start.1 = (bf16[256,256]{1,0:T(8,128)(2,1)S(1)}, bf16[256,256]{1,0:T(8,128)(2,1)S(1)}, u32[]{:S(2)}, u32[]{:S(2)}) collective-permute-start(bf16[256,256]{1,0:T(8,128)(2,1)S(1)} %collective-permute-done.rest_1_), channel_id=1, source_target_pairs={{0,2},{2,0},{4,6},{6,4},{8,10},{10,8},{12,14},{14,12},{1,3},{3,1},... | collective-permute-start | bytes 393224 | tf_op jit(solution)/shard_map/ppermute | solution.py:66
  12.7 1.9 %shard_map.69.table = s32[165]{0:T(256)S(1)} custom-call(s32[3,32]{1,0:T(4,128)S(1)} %bitcast.9, s32[1]{0:T(128)S(6)} %copy.7.live), custom_call_target="tpu_custom_call" | custom-call | flops 1024 | bytes 1024 | tf_op jit(solution)/shard_map/pallas_call | solution.py:396
  15.5 0.7 collective-permute-done.1.near
  16.6 2.6 %shard_map.70 = (f32[16,128,256]{2,1,0:T(8,128)S(1)}, bf16[16,128,512]{2,1,0:T(8,128)(2,1)S(1)}) custom-call(s32[3,32]{1,0:T(4,128)S(1)} %bitcast.10, bf16[32,3,128,256]{3,2,1,0:T(8,128)(2,1)S(1)} %shard_map.68.jac_near.jac, bf16[32,3,128,256]{3,2,1,0:T(8,128)(2,1)S(1)} %collective-permute-done.2.jac_far, bf16[256,256]{1,0:T(8,128)(2,1)S(1)} %bitcast.7, ...), custom_call_target="tpu_custom_call" | custom-call | flops 1024 | bytes 1024 | tf_op jit(solution)/shard_map/pallas_call | solution.py:386
  19.2 2.5 %shard_map.71 = (bf16[16,256,128]{2,1,0:T(8,128)(2,1)S(1)}, f32[2,256,256]{2,1,0:T(8,128)S(1)}, s16[2,272,256]{2,1,0:T(8,128)(2,1)S(1)}) custom-call(s32[1]{0:T(128)S(6)} %copy.7.live, s32[3,32]{1,0:T(4,128)S(1)} %bitcast.11, f32[16,128,256]{2,1,0:T(8,128)S(1)} %get-tuple-element.33.images, bf16[16,128,512]{2,1,0:T(8,128)(2,1)S(1)} %get-tuple-element.34.aside, ...), custom_call_target="tpu_custom_call" | custom-call | flops 1024 | bytes 1024 | tf_op jit(solution)/shard_map/pallas_call | solution.py:405
  22.0 1.3 %collective-permute-done.10.sent = s16[2,272,256]{2,1,0:T(8,128)(2,1)S(1)} collective-permute-done((s16[2,272,256]{2,1,0:T(8,128)(2,1)S(1)}, s16[2,272,256]{2,1,0:T(8,128)(2,1)S(1)}, u32[]{:S(2)}, u32[]{:S(2)}) %collective-permute-start.10) | collective-permute-done | bytes 278560 | tf_op jit(solution)/shard_map/ppermute | solution.py:58
  23.8 1.7 %collective-permute-start.12 = (s16[272,256]{1,0:T(8,128)(2,1)S(1)}, s16[272,256]{1,0:T(8,128)(2,1)S(1)}, u32[]{:S(2)}, u32[]{:S(2)}) collective-permute-start(s16[272,256]{1,0:T(8,128)(2,1)S(1)} %get-tuple-element.43), channel_id=1, source_target_pairs={{0,2},{2,0},{4,6},{6,4},{8,10},{10,8},{12,14},{14,12},{1,3},{3,1},... | collective-permute-start | bytes 417800 | tf_op jit(solution)/shard_map/ppermute | solution.py:66
  25.5 4.1 %collective-permute-start.14 = (s16[272,256]{1,0:T(8,128)(2,1)S(1)}, s16[272,256]{1,0:T(8,128)(2,1)S(1)}, u32[]{:S(2)}, u32[]{:S(2)}) collective-permute-start(s16[272,256]{1,0:T(8,128)(2,1)S(1)} %get-tuple-element.47), channel_id=1, source_target_pairs={{0,12},{2,6},{4,0},{6,10},{8,4},{10,14},{12,8},{14,2},{1,13},{3,7}... | collective-permute-start | bytes 417800 | tf_op jit(solution)/shard_map/ppermute | solution.py:71
  29.8 1.5 %shard_map.74 = (f32[256,256]{1,0:T(8,128)S(1)}, s16[272,256]{1,0:T(8,128)(2,1)S(1)}) custom-call(s32[165]{0:T(256)S(1)} %shard_map.69.table, bf16[32,3,128,256]{3,2,1,0:T(8,128)(2,1)S(1)} %shard_map.68.jac_near.jac, bf16[33,256,128]{2,1,0:T(8,128)(2,1)S(1)} %shard_map.73.weighted), custom_call_target="tpu_custom_call" | custom-call | flops 1024 | bytes 1024 | tf_op jit(solution)/shard_map/pallas_call | solution.py:426
  31.5 4.0 %collective-permute-start.15 = (s16[272,256]{1,0:T(8,128)(2,1)S(1)}, s16[272,256]{1,0:T(8,128)(2,1)S(1)}, u32[]{:S(2)}, u32[]{:S(2)}) collective-permute-start(s16[272,256]{1,0:T(8,128)(2,1)S(1)} %get-tuple-element.48), channel_id=1, source_target_pairs={{0,2},{2,0},{4,6},{6,4},{8,10},{10,8},{12,14},{14,12},{1,3},{3,1},... | collective-permute-start | bytes 417800 | tf_op jit(solution)/shard_map/ppermute | solution.py:66
  35.5 1.2 %shard_map.76.own = f32[256,256]{1,0:T(8,128)S(1)} custom-call(s32[165]{0:T(256)S(1)} %shard_map.69.table, bf16[32,3,128,256]{3,2,1,0:T(8,128)(2,1)S(1)} %shard_map.68.jac_near.jac, bf16[33,256,128]{2,1,0:T(8,128)(2,1)S(1)} %shard_map.73.weighted), custom_call_target="tpu_custom_call" | custom-call | flops 1024 | bytes 1024 | tf_op jit(solution)/shard_map/pallas_call | solution.py:426
  36.7 1.7 %collective-permute-done.13.rest_0_ = s16[272,256]{1,0:T(8,128)(2,1)S(1)} collective-permute-done((s16[272,256]{1,0:T(8,128)(2,1)S(1)}, s16[272,256]{1,0:T(8,128)(2,1)S(1)}, u32[]{:S(2)}, u32[]{:S(2)}) %collective-permute-start.13) | collective-permute-done | bytes 139296 | tf_op jit(solution)/shard_map/ppermute | solution.py:71
  39.0 1.2 %collective-permute-done.16 = f32[136,128]{1,0:T(8,128)S(1)} collective-permute-done((f32[136,128]{1,0:T(8,128)S(1)}, f32[136,128]{1,0:T(8,128)S(1)}, u32[]{:S(2)}, u32[]{:S(2)}) %collective-permute-start.16) | collective-permute-done | bytes 69664 | tf_op jit(solution)/shard_map/ppermute | solution.py:58
  40.3 2.1 %collective-permute-start.17 = (f32[136,128]{1,0:T(8,128)S(1)}, f32[136,128]{1,0:T(8,128)S(1)}, u32[]{:S(2)}, u32[]{:S(2)}) collective-permute-start(f32[136,128]{1,0:T(8,128)S(1)} %add.15), channel_id=1, source_target_pairs={{0,2},{2,0},{4,6},{6,4},{8,10},{10,8},{12,14},{14,12},{1,3},{3,1},... | collective-permute-start | bytes 208904 | tf_op jit(solution)/shard_map/ppermute | solution.py:349
  42.3 2.5 %collective-permute-done.17 = f32[136,128]{1,0:T(8,128)S(1)} collective-permute-done((f32[136,128]{1,0:T(8,128)S(1)}, f32[136,128]{1,0:T(8,128)S(1)}, u32[]{:S(2)}, u32[]{:S(2)}) %collective-permute-start.17) | collective-permute-done | bytes 69664 | tf_op jit(solution)/shard_map/ppermute | solution.py:349
  44.9 1.9 %collective-permute-start.20 = (f32[136,128]{1,0:T(8,128)S(1)}, f32[136,128]{1,0:T(8,128)S(1)}, u32[]{:S(2)}, u32[]{:S(2)}) collective-permute-start(f32[136,128]{1,0:T(8,128)S(1)} %add.16), channel_id=1, source_target_pairs={{0,12},{2,14},{4,8},{6,10},{8,4},{10,6},{12,0},{14,2},{1,13},{3,15... | collective-permute-start | bytes 208904 | tf_op jit(solution)/shard_map/ppermute | solution.py:349
  46.7 2.6 %collective-permute-start.18 = (f32[136,128]{1,0:T(8,128)S(1)}, f32[136,128]{1,0:T(8,128)S(1)}, u32[]{:S(2)}, u32[]{:S(2)}) collective-permute-start(f32[136,128]{1,0:T(8,128)S(1)} %add.16), channel_id=1, source_target_pairs={{0,4},{2,6},{4,0},{6,2},{8,12},{10,14},{12,8},{14,10},{1,5},{3,7},... | collective-permute-start | bytes 208904 | tf_op jit(solution)/shard_map/ppermute | solution.py:349
  49.3 2.4 %collective-permute-done.20 = f32[136,128]{1,0:T(8,128)S(1)} collective-permute-done((f32[136,128]{1,0:T(8,128)S(1)}, f32[136,128]{1,0:T(8,128)S(1)}, u32[]{:S(2)}, u32[]{:S(2)}) %collective-permute-start.20) | collective-permute-done | bytes 69664 | tf_op jit(solution)/shard_map/ppermute | solution.py:349
  51.7 1.7 %collective-permute-done.19 = f32[136,128]{1,0:T(8,128)S(1)} collective-permute-done((f32[136,128]{1,0:T(8,128)S(1)}, f32[136,128]{1,0:T(8,128)S(1)}, u32[]{:S(2)}, u32[]{:S(2)}) %collective-permute-start.19) | collective-permute-done | bytes 69664 | tf_op jit(solution)/shard_map/ppermute | solution.py:349
  53.5 1.2 %collective-permute-done.21.other = f32[136,128]{1,0:T(8,128)S(1)} collective-permute-done((f32[136,128]{1,0:T(8,128)S(1)}, f32[136,128]{1,0:T(8,128)S(1)}, u32[]{:S(2)}, u32[]{:S(2)}) %collective-permute-start.21) | collective-permute-done | bytes 69664 | tf_op jit(solution)/shard_map/ppermute | solution.py:58
  54.8 41.4 %shard_map.78 = (f32[256,256]{1,0:T(8,128)}, f32[256,256]{1,0:T(8,128)}) custom-call(f32[136,128]{1,0:T(8,128)S(1)} %add_add_fusion.mine, f32[136,128]{1,0:T(8,128)S(1)} %collective-permute-done.21.other, f32[256,256]{1,0:T(8,128)S(1)} %get-tuple-element.51.field), custom_call_target="tpu_custom_call" | custom-call | flops 1024 | bytes 1024 | tf_op jit(solution)/shard_map/pallas_call | solution.py:449
  (40 shorter events, 3.9 us)
Async XLA Ops:
  0.6 16.0 %collective-permute-start.2 = (bf16[32,3,128,256]{3,2,1,0:T(8,128)(2,1)}, bf16[32,3,128,256]{3,2,1,0:T(8,128)(2,1)S(1)}, u32[]{:S(2)}, u32[]{:S(2)}) collective-permute-start(bf16[32,3,128,256]{3,2,1,0:T(8,128)(2,1)} %value.1), channel_id=1, source_target_pairs={{0,1},{1,0},{2,3},{3,2},{4,5},{5,4},{6,7},{7,6},{8,9},{9,8},{10,11... | collective-permute-start | bytes 18874376 | tf_op jit(solution)/shard_map/ppermute | solution.py:58
  1.1 11.6 %copy-start.1 = (s32[32,3]{0,1:T(4,128)S(1)}, s32[32,3]{0,1:T(4,128)}, u32[]{:S(2)}) copy-start(s32[32,3]{0,1:T(4,128)} %param.6) | copy-start | bytes 1156
  1.1 13.5 %copy-start = (bf16[1,256,256]{2,1,0:T(8,128)(2,1)S(1)}, bf16[1,256,256]{2,1,0:T(8,128)(2,1)}, u32[]{:S(2)}) copy-start(bf16[1,256,256]{2,1,0:T(8,128)(2,1)} %param.9) | copy-start | bytes 393220
  1.2 8.9 %collective-permute-start = (bf16[256,256]{1,0:T(8,128)(2,1)}, bf16[256,256]{1,0:T(8,128)(2,1)S(1)}, u32[]{:S(2)}, u32[]{:S(2)}) collective-permute-start(bf16[256,256]{1,0:T(8,128)(2,1)} %bitcast.3), channel_id=1, source_target_pairs={{0,12},{2,6},{4,0},{6,10},{8,4},{10,14},{12,8},{14,2},{1,13},{3,7}... | collective-permute-start | bytes 393224 | tf_op jit(solution)/shard_map/ppermute | solution.py:71
  5.8 8.8 %collective-permute-start.4 = (bf16[256,256]{1,0:T(8,128)(2,1)}, bf16[256,256]{1,0:T(8,128)(2,1)S(1)}, u32[]{:S(2)}, u32[]{:S(2)}) collective-permute-start(bf16[256,256]{1,0:T(8,128)(2,1)} %bitcast.4), channel_id=1, source_target_pairs={{0,2},{2,0},{4,6},{6,4},{8,10},{10,8},{12,14},{14,12},{1,3},{3,1},... | collective-permute-start | bytes 393224 | tf_op jit(solution)/shard_map/ppermute | solution.py:66
  5.8 9.1 %collective-permute-start.3 = (bf16[256,256]{1,0:T(8,128)(2,1)}, bf16[256,256]{1,0:T(8,128)(2,1)S(1)}, u32[]{:S(2)}, u32[]{:S(2)}) collective-permute-start(bf16[256,256]{1,0:T(8,128)(2,1)} %bitcast.5), channel_id=1, source_target_pairs={{0,4},{2,14},{4,8},{6,2},{8,12},{10,6},{12,0},{14,10},{1,5},{3,15}... | collective-permute-start | bytes 393224 | tf_op jit(solution)/shard_map/ppermute | solution.py:71
  10.0 5.0 %collective-permute-start.6 = (bf16[256,256]{1,0:T(8,128)(2,1)S(1)}, bf16[256,256]{1,0:T(8,128)(2,1)S(1)}, u32[]{:S(2)}, u32[]{:S(2)}) collective-permute-start(bf16[256,256]{1,0:T(8,128)(2,1)S(1)} %collective-permute-done.rest_1_), channel_id=1, source_target_pairs={{0,1},{1,0},{2,3},{3,2},{4,5},{5,4},{6,7},{7,6},{8,9},{9,8},{10,11... | collective-permute-start | bytes 393224 | tf_op jit(solution)/shard_map/ppermute | solution.py:58
  10.0 6.2 %collective-permute-start.1 = (bf16[256,256]{1,0:T(8,128)(2,1)S(1)}, bf16[256,256]{1,0:T(8,128)(2,1)S(1)}, u32[]{:S(2)}, u32[]{:S(2)}) collective-permute-start(bf16[256,256]{1,0:T(8,128)(2,1)S(1)} %collective-permute-done.rest_1_), channel_id=1, source_target_pairs={{0,2},{2,0},{4,6},{6,4},{8,10},{10,8},{12,14},{14,12},{1,3},{3,1},... | collective-permute-start | bytes 393224 | tf_op jit(solution)/shard_map/ppermute | solution.py:66
  14.7 1.6 %collective-permute-start.5 = (bf16[256,256]{1,0:T(8,128)(2,1)S(1)}, bf16[256,256]{1,0:T(8,128)(2,1)S(1)}, u32[]{:S(2)}, u32[]{:S(2)}) collective-permute-start(bf16[256,256]{1,0:T(8,128)(2,1)S(1)} %bitcast.6), channel_id=1, source_target_pairs={{0,1},{1,0},{2,3},{3,2},{4,5},{5,4},{6,7},{7,6},{8,9},{9,8},{10,11... | collective-permute-start | bytes 393224 | tf_op jit(solution)/shard_map/ppermute | solution.py:58
  15.0 1.4 %collective-permute-start.7 = (bf16[256,256]{1,0:T(8,128)(2,1)S(1)}, bf16[256,256]{1,0:T(8,128)(2,1)S(1)}, u32[]{:S(2)}, u32[]{:S(2)}) collective-permute-start(bf16[256,256]{1,0:T(8,128)(2,1)S(1)} %collective-permute-done.3.rest_2_), channel_id=1, source_target_pairs={{0,1},{1,0},{2,3},{3,2},{4,5},{5,4},{6,7},{7,6},{8,9},{9,8},{10,11... | collective-permute-start | bytes 393224 | tf_op jit(solution)/shard_map/ppermute | solution.py:58
  15.3 1.3 %collective-permute-start.8 = (bf16[256,256]{1,0:T(8,128)(2,1)S(1)}, bf16[256,256]{1,0:T(8,128)(2,1)S(1)}, u32[]{:S(2)}, u32[]{:S(2)}) collective-permute-start(bf16[256,256]{1,0:T(8,128)(2,1)S(1)} %collective-permute-done.4.rest_3_), channel_id=1, source_target_pairs={{0,1},{1,0},{2,3},{3,2},{4,5},{5,4},{6,7},{7,6},{8,9},{9,8},{10,11... | collective-permute-start | bytes 393224 | tf_op jit(solution)/shard_map/ppermute | solution.py:58
  16.2 3.0 %collective-permute-start.9 = (bf16[256,256]{1,0:T(8,128)(2,1)S(1)}, bf16[256,256]{1,0:T(8,128)(2,1)S(1)}, u32[]{:S(2)}, u32[]{:S(2)}) collective-permute-start(bf16[256,256]{1,0:T(8,128)(2,1)S(1)} %collective-permute-done.1.near), channel_id=1, source_target_pairs={{0,1},{1,0},{2,3},{3,2},{4,5},{5,4},{6,7},{7,6},{8,9},{9,8},{10,11... | collective-permute-start | bytes 393224 | tf_op jit(solution)/shard_map/ppermute | solution.py:58
  21.7 1.6 %collective-permute-start.10 = (s16[2,272,256]{2,1,0:T(8,128)(2,1)S(1)}, s16[2,272,256]{2,1,0:T(8,128)(2,1)S(1)}, u32[]{:S(2)}, u32[]{:S(2)}) collective-permute-start(s16[2,272,256]{2,1,0:T(8,128)(2,1)S(1)} %get-tuple-element.37), channel_id=1, source_target_pairs={{0,1},{1,0},{2,3},{3,2},{4,5},{5,4},{6,7},{7,6},{8,9},{9,8},{10,11... | collective-permute-start | bytes 835592 | tf_op jit(solution)/shard_map/ppermute | solution.py:58
  23.5 6.1 %collective-permute-start.11 = (bf16[16,256,128]{2,1,0:T(8,128)(2,1)S(1)}, bf16[16,256,128]{2,1,0:T(8,128)(2,1)S(1)}, u32[]{:S(2)}, u32[]{:S(2)}) collective-permute-start(bf16[16,256,128]{2,1,0:T(8,128)(2,1)S(1)} %get-tuple-element.41.mine), channel_id=1, source_target_pairs={{0,1},{1,0},{2,3},{3,2},{4,5},{5,4},{6,7},{7,6},{8,9},{9,8},{10,11... | collective-permute-start | bytes 3145736 | tf_op jit(solution)/shard_map/ppermute | solution.py:58
  23.8 7.5 %collective-permute-start.12 = (s16[272,256]{1,0:T(8,128)(2,1)S(1)}, s16[272,256]{1,0:T(8,128)(2,1)S(1)}, u32[]{:S(2)}, u32[]{:S(2)}) collective-permute-start(s16[272,256]{1,0:T(8,128)(2,1)S(1)} %get-tuple-element.43), channel_id=1, source_target_pairs={{0,2},{2,0},{4,6},{6,4},{8,10},{10,8},{12,14},{14,12},{1,3},{3,1},... | collective-permute-start | bytes 417800 | tf_op jit(solution)/shard_map/ppermute | solution.py:66
  25.5 11.2 %collective-permute-start.14 = (s16[272,256]{1,0:T(8,128)(2,1)S(1)}, s16[272,256]{1,0:T(8,128)(2,1)S(1)}, u32[]{:S(2)}, u32[]{:S(2)}) collective-permute-start(s16[272,256]{1,0:T(8,128)(2,1)S(1)} %get-tuple-element.47), channel_id=1, source_target_pairs={{0,12},{2,6},{4,0},{6,10},{8,4},{10,14},{12,8},{14,2},{1,13},{3,7}... | collective-permute-start | bytes 417800 | tf_op jit(solution)/shard_map/ppermute | solution.py:71
  31.4 7.0 %collective-permute-start.13 = (s16[272,256]{1,0:T(8,128)(2,1)S(1)}, s16[272,256]{1,0:T(8,128)(2,1)S(1)}, u32[]{:S(2)}, u32[]{:S(2)}) collective-permute-start(s16[272,256]{1,0:T(8,128)(2,1)S(1)} %shard_map.75), channel_id=1, source_target_pairs={{0,4},{2,14},{4,8},{6,2},{8,12},{10,6},{12,0},{14,10},{1,5},{3,15}... | collective-permute-start | bytes 417800 | tf_op jit(solution)/shard_map/ppermute | solution.py:71
  31.5 7.1 %collective-permute-start.15 = (s16[272,256]{1,0:T(8,128)(2,1)S(1)}, s16[272,256]{1,0:T(8,128)(2,1)S(1)}, u32[]{:S(2)}, u32[]{:S(2)}) collective-permute-start(s16[272,256]{1,0:T(8,128)(2,1)S(1)} %get-tuple-element.48), channel_id=1, source_target_pairs={{0,2},{2,0},{4,6},{6,4},{8,10},{10,8},{12,14},{14,12},{1,3},{3,1},... | collective-permute-start | bytes 417800 | tf_op jit(solution)/shard_map/ppermute | solution.py:66
  38.9 1.3 %collective-permute-start.16 = (f32[136,128]{1,0:T(8,128)S(1)}, f32[136,128]{1,0:T(8,128)S(1)}, u32[]{:S(2)}, u32[]{:S(2)}) collective-permute-start(f32[136,128]{1,0:T(8,128)S(1)} %get-tuple-element.50), channel_id=1, source_target_pairs={{0,1},{1,0},{2,3},{3,2},{4,5},{5,4},{6,7},{7,6},{8,9},{9,8},{10,11... | collective-permute-start | bytes 208904 | tf_op jit(solution)/shard_map/ppermute | solution.py:58
  40.3 4.6 %collective-permute-start.17 = (f32[136,128]{1,0:T(8,128)S(1)}, f32[136,128]{1,0:T(8,128)S(1)}, u32[]{:S(2)}, u32[]{:S(2)}) collective-permute-start(f32[136,128]{1,0:T(8,128)S(1)} %add.15), channel_id=1, source_target_pairs={{0,2},{2,0},{4,6},{6,4},{8,10},{10,8},{12,14},{14,12},{1,3},{3,1},... | collective-permute-start | bytes 208904 | tf_op jit(solution)/shard_map/ppermute | solution.py:349
  44.9 6.8 %collective-permute-start.20 = (f32[136,128]{1,0:T(8,128)S(1)}, f32[136,128]{1,0:T(8,128)S(1)}, u32[]{:S(2)}, u32[]{:S(2)}) collective-permute-start(f32[136,128]{1,0:T(8,128)S(1)} %add.16), channel_id=1, source_target_pairs={{0,12},{2,14},{4,8},{6,10},{8,4},{10,6},{12,0},{14,2},{1,13},{3,15... | collective-permute-start | bytes 208904 | tf_op jit(solution)/shard_map/ppermute | solution.py:349
  46.7 6.7 %collective-permute-start.19 = (f32[136,128]{1,0:T(8,128)S(1)}, f32[136,128]{1,0:T(8,128)S(1)}, u32[]{:S(2)}, u32[]{:S(2)}) collective-permute-start(f32[136,128]{1,0:T(8,128)S(1)} %add.16), channel_id=1, source_target_pairs={{0,8},{2,10},{4,12},{6,14},{8,0},{10,2},{12,4},{14,6},{1,9},{3,11}... | collective-permute-start | bytes 208904 | tf_op jit(solution)/shard_map/ppermute | solution.py:349
  46.7 6.7 %collective-permute-start.18 = (f32[136,128]{1,0:T(8,128)S(1)}, f32[136,128]{1,0:T(8,128)S(1)}, u32[]{:S(2)}, u32[]{:S(2)}) collective-permute-start(f32[136,128]{1,0:T(8,128)S(1)} %add.16), channel_id=1, source_target_pairs={{0,4},{2,6},{4,0},{6,2},{8,12},{10,14},{12,8},{14,10},{1,5},{3,7},... | collective-permute-start | bytes 208904 | tf_op jit(solution)/shard_map/ppermute | solution.py:349
  53.5 1.3 %collective-permute-start.21 = (f32[136,128]{1,0:T(8,128)S(1)}, f32[136,128]{1,0:T(8,128)S(1)}, u32[]{:S(2)}, u32[]{:S(2)}) collective-permute-start(f32[136,128]{1,0:T(8,128)S(1)} %add_add_fusion.mine), channel_id=1, source_target_pairs={{0,1},{1,0},{2,3},{3,2},{4,5},{5,4},{6,7},{7,6},{8,9},{9,8},{10,11... | collective-permute-start | bytes 208904 | tf_op jit(solution)/shard_map/ppermute | solution.py:58
  (1 other events, 4.6 us)

commit v6 on v5

--- a/solution.py
+++ b/solution.py
@@ -93,6 +93,8 @@
     reach, slots = footprint.shape
     core = core_index()
     counts = len(OFFSETS) * cap
+    places = counts + len(OFFSETS)
+    table[places + reach * slots] = live[0]
     for o in range(len(OFFSETS)):
         table[counts + o] = 0
 
@@ -101,6 +103,7 @@
         alive = (slot < live[0]).astype(jnp.int32)
         for f in range(reach):
             o = footprint[f, slot]
+            table[places + f * slots + slot] = o
             n = table[counts + o]
             table[o * cap + n] = j * 4 + f
             table[counts + o] = n + alive
@@ -115,13 +118,14 @@
     copy.wait()
 
 
-def early_kernel(footprint, jac_near, jac_far, *rest):
+def early_kernel(cap, table, jac_near, jac_far, *rest):
     count = len(ROLES) - 1
     near, far = rest[:count], rest[count : 2 * count]
     images, aside, window = rest[2 * count :]
     slots = images.shape[0]
-    _, reach, _, cells = jac_near.shape
+    total, reach, _, cells = jac_near.shape
     base = core_index() * slots
+    at = len(OFFSETS) * (cap + 1) + base
     for i in range(count):
         o = place_of(ROLES[i])
         window[o, :cells] = near[i][...]
@@ -129,7 +133,7 @@
     last = place_of(ROLES[count])
     window[last] = jnp.zeros(window.shape[1:], BF16)
     for j in range(slots):
-        places = [footprint[f, base + j] for f in range(reach)]
+        places = [table[at + f * total + j] for f in range(reach)]
         pieces = [jac[base + j, f] for f in range(reach) for jac in (jac_near, jac_far)]
         bands = [window[place] for place in places]
         images[j] = dot(jnp.concatenate(pieces, axis=1), jnp.concatenate(bands, axis=0))
@@ -168,17 +172,19 @@
     return part[:width].astype(jnp.int32).astype(F32) * jnp.exp2(power - 15.0)
 
 
-def late_kernel(live, footprint, images, aside, jac_near, jac_far, near, far, noise, out, kept, sent):
+def late_kernel(cap, table, images, aside, jac_near, jac_far, near, far, noise, out, kept, sent):
     half, width, rows = out.shape
-    reach, cells = jac_near.shape[1], jac_near.shape[3]
+    slots, reach, _, cells = jac_near.shape
     base = core_index() * half
+    at = len(OFFSETS) * (cap + 1) + base
+    live = table[len(OFFSETS) * (cap + 1) + reach * slots]
     band = jnp.concatenate([near[...], far[...]], axis=0)
     size = half // 2
     for first in range(0, half, size):
         product = dot(jnp.concatenate([aside[first + j] for j in range(size)], axis=0), band)
         for j in range(size):
             slot = base + first + j
-            scale = noise[pl.ds(slot, 1), :] * (slot < live[0]).astype(F32)
+            scale = noise[pl.ds(slot, 1), :] * (slot < live).astype(F32)
             image = images[first + j] + product[j * rows : (j + 1) * rows]
             out[first + j] = (image.T * scale).astype(BF16)
 
@@ -189,7 +195,7 @@
     ahead = place_of("ahead")
     left, right = [], []
     for j in range(half):
-        places = [footprint[f, base + j] for f in range(reach)]
+        places = [table[at + f * slots + j] for f in range(reach)]
         chosen = sum(f * (places[f] == ahead).astype(jnp.int32) for f in range(reach))
         found = sum((place == ahead).astype(jnp.int32) for place in places)
         block = out[j]
@@ -365,7 +371,6 @@
     width = probes.shape[2]
     half = slots // lax.axis_size("col")
     cap = slots
-    footprint = footprint.T
     mine = probes[0]
 
     back, ahead, partner = spread(mine, -2), spread(mine, 2), swapped(mine)
@@ -378,13 +383,20 @@
         [pltpu.SemaphoreType.DMA(())],
     )(held(jacobian, pltpu.HBM))
     back, staged = lax.optimization_barrier((back, staged))
+    table = kernel_call(
+        functools.partial(list_kernel, cap, half),
+        pltpu.SMEM((len(OFFSETS) * (cap + 1) + reach * slots + 1,), jnp.int32),
+        [SMEM] * 2,
+        SMEM,
+    )(footprint.T, live)
     near = [mine, back, ahead, partner]
     far = [flipped(mine), flipped(back)]
-    ahead, partner, _ = lax.optimization_barrier((ahead, partner, far[1]))
+    ahead, partner, _, table = lax.optimization_barrier((ahead, partner, far[1], table))
+    table = held(table, pltpu.SMEM)
     far += [flipped(ahead), flipped(partner)]
 
     early = kernel_call(
-        early_kernel,
+        functools.partial(early_kernel, cap),
         (
             jax.ShapeDtypeStruct((half, rows, width), F32),
             jax.ShapeDtypeStruct((half, rows, 2 * cells), BF16),
@@ -392,26 +404,20 @@
         [SMEM] + [VMEM] * 10,
         (VMEM,) * 2,
         [pltpu.VMEM((len(OFFSETS), 2 * cells, width), BF16)],
-    )(footprint, held(staged, pltpu.VMEM), held(jac_far, pltpu.VMEM), *near, *far)
-    table = kernel_call(
-        functools.partial(list_kernel, cap, half),
-        jax.ShapeDtypeStruct((len(OFFSETS) * (cap + 1),), jnp.int32),
-        [SMEM] * 2,
-        SMEM,
-    )(footprint, live)
-    beyond, table = lax.optimization_barrier((swapped(back), table))
+    )(table, held(staged, pltpu.VMEM), held(jac_far, pltpu.VMEM), *near, *far)
+    beyond = swapped(back)
     plain = jax.ShapeDtypeStruct((width, cells), F32)
     message = jax.ShapeDtypeStruct((width + PAD, cells), jnp.int16)
     weighted, kept, sent = kernel_call(
-        late_kernel,
+        functools.partial(late_kernel, cap),
         (
             jax.ShapeDtypeStruct((half, width, rows), BF16),
             jax.ShapeDtypeStruct((2,) + plain.shape, F32),
             jax.ShapeDtypeStruct((2,) + message.shape, jnp.int16),
         ),
-        [SMEM] * 2 + [VMEM] * 7,
+        [SMEM] + [VMEM] * 7,
         (VMEM,) * 3,
-    )(live, footprint, *early, held(staged, pltpu.VMEM), held(jac_far, pltpu.VMEM), beyond, flipped(beyond), noise_weight)
+    )(table, *early, held(staged, pltpu.VMEM), held(jac_far, pltpu.VMEM), beyond, flipped(beyond), noise_weight)
     beyond, ahead = kernel_call(merge_two_kernel, (message, message), [VMEM] * 2, (VMEM,) * 2)(kept, flipped(sent))
     beyond, ahead, weighted = lax.optimization_barrier((beyond, ahead, weighted))
     beyond, ahead = swapped(beyond), spread(ahead, -2)

time: 96.2 us -> 95.4 us (level)
  Pallas kernels: 54.6 us -> 52.1 us
  waiting for transfers between devices: 13.8 us -> 15.9 us
    pallas_call x3, Pallas kernels: 6.97 us -> 5.13 us  [the longest x1 1.9 us: on_device(): kernel_call(functools.partial(early_kernel, cap), (jax.ShapeDtypeStruct((...]
    ppermute x4, waiting for transfers between devices: 2.06 us -> 3.37 us  [spread(): lax.ppermute(value, 'tile', [(i, (i + (steps, -steps)[i % 2]) % count) fo...]
  transfers between devices with their start and end apart: 22 -> 22, of which waited for: 12 -> 10; matrix products, arithmetic and copies ran while one was open for 0% -> 0% of each run, Pallas kernels for 11% -> 9%
where the time goes in v6:
time: 95.4 us; the launch traced here: 95.2 us
  Pallas kernels  52.1 us (55%)
  starting transfers between devices  25.7 us (27%)
  waiting for transfers between devices  15.9 us (17%)
  between operations  1.49 us (2%)
    pallas_call x1, Pallas kernels, on_device(): kernel_call(functools.partial(finish_kernel, scale, 2), (jax.ShapeDtypeSt...  41.4 us
    ppermute x4, starting transfers between devices, spread(): lax.ppermute(value, 'tile', [(i, (i + (steps, -steps)[i % 2]) % count) fo...  9.97 us
    ppermute x4, starting transfers between devices, swapped(): lax.ppermute(value, 'tile', [(i, i ^ 1) for i in range(lax.axis_size('til...  7.47 us
    ppermute x4, waiting for transfers between devices, exchanged(): return lax.ppermute(value, 'tile', [(i, i ^ jump) for i in range(count)])  6.97 us
    ppermute x4, starting transfers between devices, exchanged(): return lax.ppermute(value, 'tile', [(i, i ^ jump) for i in range(count)])  5.8 us
    ppermute x10, waiting for transfers between devices, shifted(): return lax.ppermute(value, axis, pairs)  4.24 us
    ppermute x4, waiting for transfers between devices, spread(): lax.ppermute(value, 'tile', [(i, (i + (steps, -steps)[i % 2]) % count) fo...  3.37 us
    pallas_call x1, Pallas kernels, on_device(): kernel_call(stage_kernel, pltpu.VMEM(jacobian.shape, BF16), [HBM], VMEM,...  2.79 us
  transfers between devices with their start and end apart: 22, of which 10 were waited for; matrix products, arithmetic and copies ran while one was open for 0% of the time, Pallas kernels for 9%

profile of v6, /device:TPU:0, one launch (start us, length us, event | category | flops | bytes accessed | tf_op | source)
XLA Modules:
  0.0 95.2 jit_solution(18318606363724505294)
XLA Ops:
  1.2 4.7 %collective-permute-start.2 = (bf16[256,256]{1,0:T(8,128)(2,1)}, bf16[256,256]{1,0:T(8,128)(2,1)S(1)}, u32[]{:S(2)}, u32[]{:S(2)}) collective-permute-start(bf16[256,256]{1,0:T(8,128)(2,1)} %bitcast.3), channel_id=1, source_target_pairs={{0,12},{2,6},{4,0},{6,10},{8,4},{10,14},{12,8},{14,2},{1,13},{3,7}... | collective-permute-start | bytes 393224 | tf_op jit(solution)/shard_map/ppermute | solution.py:71
  5.8 1.0 %collective-permute-start = (bf16[256,256]{1,0:T(8,128)(2,1)}, bf16[256,256]{1,0:T(8,128)(2,1)S(1)}, u32[]{:S(2)}, u32[]{:S(2)}) collective-permute-start(bf16[256,256]{1,0:T(8,128)(2,1)} %bitcast.5), channel_id=1, source_target_pairs={{0,4},{2,14},{4,8},{6,2},{8,12},{10,6},{12,0},{14,10},{1,5},{3,15}... | collective-permute-start | bytes 393224 | tf_op jit(solution)/shard_map/ppermute | solution.py:71
  6.9 2.8 %shard_map.68.jac_near.jac = bf16[32,3,128,256]{3,2,1,0:T(8,128)(2,1)S(1)} custom-call(bf16[32,3,128,256]{3,2,1,0:T(8,128)(2,1)} %value.1), custom_call_target="tpu_custom_call" | custom-call | flops 1024 | bytes 1024 | tf_op jit(solution)/shard_map/pallas_call | solution.py:378
  10.0 2.1 %collective-permute-start.8 = (bf16[256,256]{1,0:T(8,128)(2,1)S(1)}, bf16[256,256]{1,0:T(8,128)(2,1)S(1)}, u32[]{:S(2)}, u32[]{:S(2)}) collective-permute-start(bf16[256,256]{1,0:T(8,128)(2,1)S(1)} %collective-permute-done.2.rest_1_), channel_id=1, source_target_pairs={{0,2},{2,0},{4,6},{6,4},{8,10},{10,8},{12,14},{14,12},{1,3},{3,1},... | collective-permute-start | bytes 393224 | tf_op jit(solution)/shard_map/ppermute | solution.py:66
  12.7 1.3 %shard_map.69.table = s32[262]{0:T(512)S(4)} custom-call(s32[3,32]{1,0:T(4,128)S(1)} %bitcast.9, s32[1]{0:T(128)S(6)} %copy.7.live), custom_call_target="tpu_custom_call" | custom-call | flops 1024 | bytes 1024 | tf_op jit(solution)/shard_map/pallas_call | solution.py:386
  14.9 1.3 %collective-permute-done.8.near = bf16[256,256]{1,0:T(8,128)(2,1)S(1)} collective-permute-done((bf16[256,256]{1,0:T(8,128)(2,1)S(1)}, bf16[256,256]{1,0:T(8,128)(2,1)S(1)}, u32[]{:S(2)}, u32[]{:S(2)}) %collective-permute-start.8) | collective-permute-done | bytes 131104 | tf_op jit(solution)/shard_map/ppermute | solution.py:66
  16.3 1.9 %shard_map.70 = (f32[16,128,256]{2,1,0:T(8,128)S(1)}, bf16[16,128,512]{2,1,0:T(8,128)(2,1)S(1)}) custom-call(s32[262]{0:T(512)S(4)} %shard_map.69.table, bf16[32,3,128,256]{3,2,1,0:T(8,128)(2,1)S(1)} %shard_map.68.jac_near.jac, bf16[32,3,128,256]{3,2,1,0:T(8,128)(2,1)S(1)} %collective-permute-done.4.jac_far, bf16[256,256]{1,0:T(8,128)(2,1)S(1)} %bitcast.7, ...), custom_call_target="tpu_custom_call" | custom-call | flops 1024 | bytes 1024 | tf_op jit(solution)/shard_map/pallas_call | solution.py:398
  18.2 1.9 %shard_map.71 = (bf16[16,256,128]{2,1,0:T(8,128)(2,1)S(1)}, f32[2,256,256]{2,1,0:T(8,128)S(1)}, s16[2,272,256]{2,1,0:T(8,128)(2,1)S(1)}) custom-call(s32[262]{0:T(512)S(4)} %shard_map.69.table, f32[16,128,256]{2,1,0:T(8,128)S(1)} %get-tuple-element.32.images, bf16[16,128,512]{2,1,0:T(8,128)(2,1)S(1)} %get-tuple-element.33.aside, ...), custom_call_target="tpu_custom_call" | custom-call | flops 1024 | bytes 1024 | tf_op jit(solution)/shard_map/pallas_call | solution.py:411
  20.7 1.2 %collective-permute-done.10.sent = s16[2,272,256]{2,1,0:T(8,128)(2,1)S(1)} collective-permute-done((s16[2,272,256]{2,1,0:T(8,128)(2,1)S(1)}, s16[2,272,256]{2,1,0:T(8,128)(2,1)S(1)}, u32[]{:S(2)}, u32[]{:S(2)}) %collective-permute-start.10) | collective-permute-done | bytes 278560 | tf_op jit(solution)/shard_map/ppermute | solution.py:58
  22.5 1.7 %collective-permute-start.12 = (s16[272,256]{1,0:T(8,128)(2,1)S(1)}, s16[272,256]{1,0:T(8,128)(2,1)S(1)}, u32[]{:S(2)}, u32[]{:S(2)}) collective-permute-start(s16[272,256]{1,0:T(8,128)(2,1)S(1)} %get-tuple-element.41), channel_id=1, source_target_pairs={{0,2},{2,0},{4,6},{6,4},{8,10},{10,8},{12,14},{14,12},{1,3},{3,1},... | collective-permute-start | bytes 417800 | tf_op jit(solution)/shard_map/ppermute | solution.py:66
  24.9 4.2 %collective-permute-start.14 = (s16[272,256]{1,0:T(8,128)(2,1)S(1)}, s16[272,256]{1,0:T(8,128)(2,1)S(1)}, u32[]{:S(2)}, u32[]{:S(2)}) collective-permute-start(s16[272,256]{1,0:T(8,128)(2,1)S(1)} %get-tuple-element.45), channel_id=1, source_target_pairs={{0,12},{2,6},{4,0},{6,10},{8,4},{10,14},{12,8},{14,2},{1,13},{3,7}... | collective-permute-start | bytes 417800 | tf_op jit(solution)/shard_map/ppermute | solution.py:71
  29.1 1.2 %shard_map.74 = (f32[256,256]{1,0:T(8,128)S(1)}, s16[272,256]{1,0:T(8,128)(2,1)S(1)}) custom-call(s32[262]{0:T(512)S(4)} %shard_map.69.table, bf16[32,3,128,256]{3,2,1,0:T(8,128)(2,1)S(1)} %shard_map.68.jac_near.jac, bf16[33,256,128]{2,1,0:T(8,128)(2,1)S(1)} %shard_map.73.weighted), custom_call_target="tpu_custom_call" | custom-call | flops 1024 | bytes 1024 | tf_op jit(solution)/shard_map/pallas_call | solution.py:432
  30.5 3.7 %collective-permute-start.15 = (s16[272,256]{1,0:T(8,128)(2,1)S(1)}, s16[272,256]{1,0:T(8,128)(2,1)S(1)}, u32[]{:S(2)}, u32[]{:S(2)}) collective-permute-start(s16[272,256]{1,0:T(8,128)(2,1)S(1)} %get-tuple-element.46), channel_id=1, source_target_pairs={{0,2},{2,0},{4,6},{6,4},{8,10},{10,8},{12,14},{14,12},{1,3},{3,1},... | collective-permute-start | bytes 417800 | tf_op jit(solution)/shard_map/ppermute | solution.py:66
  34.2 0.7 shard_map.76.own
  34.9 3.0 %collective-permute-done.13.rest_0_ = s16[272,256]{1,0:T(8,128)(2,1)S(1)} collective-permute-done((s16[272,256]{1,0:T(8,128)(2,1)S(1)}, s16[272,256]{1,0:T(8,128)(2,1)S(1)}, u32[]{:S(2)}, u32[]{:S(2)}) %collective-permute-start.13) | collective-permute-done | bytes 139296 | tf_op jit(solution)/shard_map/ppermute | solution.py:71
  38.5 1.2 %collective-permute-done.16 = f32[136,128]{1,0:T(8,128)S(1)} collective-permute-done((f32[136,128]{1,0:T(8,128)S(1)}, f32[136,128]{1,0:T(8,128)S(1)}, u32[]{:S(2)}, u32[]{:S(2)}) %collective-permute-start.16) | collective-permute-done | bytes 69664 | tf_op jit(solution)/shard_map/ppermute | solution.py:58
  39.7 1.3 %collective-permute-start.17 = (f32[136,128]{1,0:T(8,128)S(1)}, f32[136,128]{1,0:T(8,128)S(1)}, u32[]{:S(2)}, u32[]{:S(2)}) collective-permute-start(f32[136,128]{1,0:T(8,128)S(1)} %add.15), channel_id=1, source_target_pairs={{0,2},{2,0},{4,6},{6,4},{8,10},{10,8},{12,14},{14,12},{1,3},{3,1},... | collective-permute-start | bytes 208904 | tf_op jit(solution)/shard_map/ppermute | solution.py:355
  41.1 3.0 %collective-permute-done.17 = f32[136,128]{1,0:T(8,128)S(1)} collective-permute-done((f32[136,128]{1,0:T(8,128)S(1)}, f32[136,128]{1,0:T(8,128)S(1)}, u32[]{:S(2)}, u32[]{:S(2)}) %collective-permute-start.17) | collective-permute-done | bytes 69664 | tf_op jit(solution)/shard_map/ppermute | solution.py:355
  44.1 1.9 %collective-permute-start.20 = (f32[136,128]{1,0:T(8,128)S(1)}, f32[136,128]{1,0:T(8,128)S(1)}, u32[]{:S(2)}, u32[]{:S(2)}) collective-permute-start(f32[136,128]{1,0:T(8,128)S(1)} %add.16), channel_id=1, source_target_pairs={{0,12},{2,14},{4,8},{6,10},{8,4},{10,6},{12,0},{14,2},{1,13},{3,15... | collective-permute-start | bytes 208904 | tf_op jit(solution)/shard_map/ppermute | solution.py:355
  46.0 2.5 %collective-permute-start.18 = (f32[136,128]{1,0:T(8,128)S(1)}, f32[136,128]{1,0:T(8,128)S(1)}, u32[]{:S(2)}, u32[]{:S(2)}) collective-permute-start(f32[136,128]{1,0:T(8,128)S(1)} %add.16), channel_id=1, source_target_pairs={{0,4},{2,6},{4,0},{6,2},{8,12},{10,14},{12,8},{14,10},{1,5},{3,7},... | collective-permute-start | bytes 208904 | tf_op jit(solution)/shard_map/ppermute | solution.py:355
  48.6 2.5 %collective-permute-done.20 = f32[136,128]{1,0:T(8,128)S(1)} collective-permute-done((f32[136,128]{1,0:T(8,128)S(1)}, f32[136,128]{1,0:T(8,128)S(1)}, u32[]{:S(2)}, u32[]{:S(2)}) %collective-permute-start.20) | collective-permute-done | bytes 69664 | tf_op jit(solution)/shard_map/ppermute | solution.py:355
  51.0 1.5 %collective-permute-done.19 = f32[136,128]{1,0:T(8,128)S(1)} collective-permute-done((f32[136,128]{1,0:T(8,128)S(1)}, f32[136,128]{1,0:T(8,128)S(1)}, u32[]{:S(2)}, u32[]{:S(2)}) %collective-permute-start.19) | collective-permute-done | bytes 69664 | tf_op jit(solution)/shard_map/ppermute | solution.py:355
  52.6 1.2 %collective-permute-done.21.other = f32[136,128]{1,0:T(8,128)S(1)} collective-permute-done((f32[136,128]{1,0:T(8,128)S(1)}, f32[136,128]{1,0:T(8,128)S(1)}, u32[]{:S(2)}, u32[]{:S(2)}) %collective-permute-start.21) | collective-permute-done | bytes 69664 | tf_op jit(solution)/shard_map/ppermute | solution.py:58
  53.9 41.4 %shard_map.78 = (f32[256,256]{1,0:T(8,128)}, f32[256,256]{1,0:T(8,128)}) custom-call(f32[136,128]{1,0:T(8,128)S(1)} %add_add_fusion.mine, f32[136,128]{1,0:T(8,128)S(1)} %collective-permute-done.21.other, f32[256,256]{1,0:T(8,128)S(1)} %get-tuple-element.49.field), custom_call_target="tpu_custom_call" | custom-call | flops 1024 | bytes 1024 | tf_op jit(solution)/shard_map/pallas_call | solution.py:455
  (40 shorter events, 4.3 us)
Async XLA Ops:
  0.6 15.6 %collective-permute-start.4 = (bf16[32,3,128,256]{3,2,1,0:T(8,128)(2,1)}, bf16[32,3,128,256]{3,2,1,0:T(8,128)(2,1)S(1)}, u32[]{:S(2)}, u32[]{:S(2)}) collective-permute-start(bf16[32,3,128,256]{3,2,1,0:T(8,128)(2,1)} %value.1), channel_id=1, source_target_pairs={{0,1},{1,0},{2,3},{3,2},{4,5},{5,4},{6,7},{7,6},{8,9},{9,8},{10,11... | collective-permute-start | bytes 18874376 | tf_op jit(solution)/shard_map/ppermute | solution.py:58
  1.1 11.6 %copy-start.2 = (s32[32,3]{0,1:T(4,128)S(1)}, s32[32,3]{0,1:T(4,128)}, u32[]{:S(2)}) copy-start(s32[32,3]{0,1:T(4,128)} %param.6) | copy-start | bytes 1156
  1.1 13.0 %copy-start = (bf16[1,256,256]{2,1,0:T(8,128)(2,1)S(1)}, bf16[1,256,256]{2,1,0:T(8,128)(2,1)}, u32[]{:S(2)}) copy-start(bf16[1,256,256]{2,1,0:T(8,128)(2,1)} %param.9) | copy-start | bytes 393220
  1.2 8.9 %collective-permute-start.2 = (bf16[256,256]{1,0:T(8,128)(2,1)}, bf16[256,256]{1,0:T(8,128)(2,1)S(1)}, u32[]{:S(2)}, u32[]{:S(2)}) collective-permute-start(bf16[256,256]{1,0:T(8,128)(2,1)} %bitcast.3), channel_id=1, source_target_pairs={{0,12},{2,6},{4,0},{6,10},{8,4},{10,14},{12,8},{14,2},{1,13},{3,7}... | collective-permute-start | bytes 393224 | tf_op jit(solution)/shard_map/ppermute | solution.py:71
  5.8 8.3 %collective-permute-start.1 = (bf16[256,256]{1,0:T(8,128)(2,1)}, bf16[256,256]{1,0:T(8,128)(2,1)S(1)}, u32[]{:S(2)}, u32[]{:S(2)}) collective-permute-start(bf16[256,256]{1,0:T(8,128)(2,1)} %bitcast.4), channel_id=1, source_target_pairs={{0,2},{2,0},{4,6},{6,4},{8,10},{10,8},{12,14},{14,12},{1,3},{3,1},... | collective-permute-start | bytes 393224 | tf_op jit(solution)/shard_map/ppermute | solution.py:66
  5.8 8.6 %collective-permute-start = (bf16[256,256]{1,0:T(8,128)(2,1)}, bf16[256,256]{1,0:T(8,128)(2,1)S(1)}, u32[]{:S(2)}, u32[]{:S(2)}) collective-permute-start(bf16[256,256]{1,0:T(8,128)(2,1)} %bitcast.5), channel_id=1, source_target_pairs={{0,4},{2,14},{4,8},{6,2},{8,12},{10,6},{12,0},{14,10},{1,5},{3,15}... | collective-permute-start | bytes 393224 | tf_op jit(solution)/shard_map/ppermute | solution.py:71
  10.0 4.4 %collective-permute-start.3 = (bf16[256,256]{1,0:T(8,128)(2,1)S(1)}, bf16[256,256]{1,0:T(8,128)(2,1)S(1)}, u32[]{:S(2)}, u32[]{:S(2)}) collective-permute-start(bf16[256,256]{1,0:T(8,128)(2,1)S(1)} %collective-permute-done.2.rest_1_), channel_id=1, source_target_pairs={{0,1},{1,0},{2,3},{3,2},{4,5},{5,4},{6,7},{7,6},{8,9},{9,8},{10,11... | collective-permute-start | bytes 393224 | tf_op jit(solution)/shard_map/ppermute | solution.py:58
  10.0 6.2 %collective-permute-start.8 = (bf16[256,256]{1,0:T(8,128)(2,1)S(1)}, bf16[256,256]{1,0:T(8,128)(2,1)S(1)}, u32[]{:S(2)}, u32[]{:S(2)}) collective-permute-start(bf16[256,256]{1,0:T(8,128)(2,1)S(1)} %collective-permute-done.2.rest_1_), channel_id=1, source_target_pairs={{0,2},{2,0},{4,6},{6,4},{8,10},{10,8},{12,14},{14,12},{1,3},{3,1},... | collective-permute-start | bytes 393224 | tf_op jit(solution)/shard_map/ppermute | solution.py:66
  14.1 2.1 %collective-permute-start.5 = (bf16[256,256]{1,0:T(8,128)(2,1)S(1)}, bf16[256,256]{1,0:T(8,128)(2,1)S(1)}, u32[]{:S(2)}, u32[]{:S(2)}) collective-permute-start(bf16[256,256]{1,0:T(8,128)(2,1)S(1)} %bitcast.6), channel_id=1, source_target_pairs={{0,1},{1,0},{2,3},{3,2},{4,5},{5,4},{6,7},{7,6},{8,9},{9,8},{10,11... | collective-permute-start | bytes 393224 | tf_op jit(solution)/shard_map/ppermute | solution.py:58
  14.4 1.8 %collective-permute-start.6 = (bf16[256,256]{1,0:T(8,128)(2,1)S(1)}, bf16[256,256]{1,0:T(8,128)(2,1)S(1)}, u32[]{:S(2)}, u32[]{:S(2)}) collective-permute-start(bf16[256,256]{1,0:T(8,128)(2,1)S(1)} %collective-permute-done.rest_2_), channel_id=1, source_target_pairs={{0,1},{1,0},{2,3},{3,2},{4,5},{5,4},{6,7},{7,6},{8,9},{9,8},{10,11... | collective-permute-start | bytes 393224 | tf_op jit(solution)/shard_map/ppermute | solution.py:58
  14.7 1.5 %collective-permute-start.7 = (bf16[256,256]{1,0:T(8,128)(2,1)S(1)}, bf16[256,256]{1,0:T(8,128)(2,1)S(1)}, u32[]{:S(2)}, u32[]{:S(2)}) collective-permute-start(bf16[256,256]{1,0:T(8,128)(2,1)S(1)} %collective-permute-done.1.rest_3_), channel_id=1, source_target_pairs={{0,1},{1,0},{2,3},{3,2},{4,5},{5,4},{6,7},{7,6},{8,9},{9,8},{10,11... | collective-permute-start | bytes 393224 | tf_op jit(solution)/shard_map/ppermute | solution.py:58
  16.2 1.9 %collective-permute-start.9 = (bf16[256,256]{1,0:T(8,128)(2,1)S(1)}, bf16[256,256]{1,0:T(8,128)(2,1)S(1)}, u32[]{:S(2)}, u32[]{:S(2)}) collective-permute-start(bf16[256,256]{1,0:T(8,128)(2,1)S(1)} %collective-permute-done.8.near), channel_id=1, source_target_pairs={{0,1},{1,0},{2,3},{3,2},{4,5},{5,4},{6,7},{7,6},{8,9},{9,8},{10,11... | collective-permute-start | bytes 393224 | tf_op jit(solution)/shard_map/ppermute | solution.py:58
  20.1 1.8 %collective-permute-start.10 = (s16[2,272,256]{2,1,0:T(8,128)(2,1)S(1)}, s16[2,272,256]{2,1,0:T(8,128)(2,1)S(1)}, u32[]{:S(2)}, u32[]{:S(2)}) collective-permute-start(s16[2,272,256]{2,1,0:T(8,128)(2,1)S(1)} %get-tuple-element.35), channel_id=1, source_target_pairs={{0,1},{1,0},{2,3},{3,2},{4,5},{5,4},{6,7},{7,6},{8,9},{9,8},{10,11... | collective-permute-start | bytes 835592 | tf_op jit(solution)/shard_map/ppermute | solution.py:58
  22.0 2.7 %collective-permute-start.11 = (bf16[16,256,128]{2,1,0:T(8,128)(2,1)S(1)}, bf16[16,256,128]{2,1,0:T(8,128)(2,1)S(1)}, u32[]{:S(2)}, u32[]{:S(2)}) collective-permute-start(bf16[16,256,128]{2,1,0:T(8,128)(2,1)S(1)} %get-tuple-element.39.mine), channel_id=1, source_target_pairs={{0,1},{1,0},{2,3},{3,2},{4,5},{5,4},{6,7},{7,6},{8,9},{9,8},{10,11... | collective-permute-start | bytes 3145736 | tf_op jit(solution)/shard_map/ppermute | solution.py:58
  22.5 7.9 %collective-permute-start.12 = (s16[272,256]{1,0:T(8,128)(2,1)S(1)}, s16[272,256]{1,0:T(8,128)(2,1)S(1)}, u32[]{:S(2)}, u32[]{:S(2)}) collective-permute-start(s16[272,256]{1,0:T(8,128)(2,1)S(1)} %get-tuple-element.41), channel_id=1, source_target_pairs={{0,2},{2,0},{4,6},{6,4},{8,10},{10,8},{12,14},{14,12},{1,3},{3,1},... | collective-permute-start | bytes 417800 | tf_op jit(solution)/shard_map/ppermute | solution.py:66
  24.9 10.0 %collective-permute-start.14 = (s16[272,256]{1,0:T(8,128)(2,1)S(1)}, s16[272,256]{1,0:T(8,128)(2,1)S(1)}, u32[]{:S(2)}, u32[]{:S(2)}) collective-permute-start(s16[272,256]{1,0:T(8,128)(2,1)S(1)} %get-tuple-element.45), channel_id=1, source_target_pairs={{0,12},{2,6},{4,0},{6,10},{8,4},{10,14},{12,8},{14,2},{1,13},{3,7}... | collective-permute-start | bytes 417800 | tf_op jit(solution)/shard_map/ppermute | solution.py:71
  30.5 7.5 %collective-permute-start.13 = (s16[272,256]{1,0:T(8,128)(2,1)S(1)}, s16[272,256]{1,0:T(8,128)(2,1)S(1)}, u32[]{:S(2)}, u32[]{:S(2)}) collective-permute-start(s16[272,256]{1,0:T(8,128)(2,1)S(1)} %shard_map.75), channel_id=1, source_target_pairs={{0,4},{2,14},{4,8},{6,2},{8,12},{10,6},{12,0},{14,10},{1,5},{3,15}... | collective-permute-start | bytes 417800 | tf_op jit(solution)/shard_map/ppermute | solution.py:71
  30.5 7.4 %collective-permute-start.15 = (s16[272,256]{1,0:T(8,128)(2,1)S(1)}, s16[272,256]{1,0:T(8,128)(2,1)S(1)}, u32[]{:S(2)}, u32[]{:S(2)}) collective-permute-start(s16[272,256]{1,0:T(8,128)(2,1)S(1)} %get-tuple-element.46), channel_id=1, source_target_pairs={{0,2},{2,0},{4,6},{6,4},{8,10},{10,8},{12,14},{14,12},{1,3},{3,1},... | collective-permute-start | bytes 417800 | tf_op jit(solution)/shard_map/ppermute | solution.py:66
  38.4 1.3 %collective-permute-start.16 = (f32[136,128]{1,0:T(8,128)S(1)}, f32[136,128]{1,0:T(8,128)S(1)}, u32[]{:S(2)}, u32[]{:S(2)}) collective-permute-start(f32[136,128]{1,0:T(8,128)S(1)} %get-tuple-element.48), channel_id=1, source_target_pairs={{0,1},{1,0},{2,3},{3,2},{4,5},{5,4},{6,7},{7,6},{8,9},{9,8},{10,11... | collective-permute-start | bytes 208904 | tf_op jit(solution)/shard_map/ppermute | solution.py:58
  39.7 4.4 %collective-permute-start.17 = (f32[136,128]{1,0:T(8,128)S(1)}, f32[136,128]{1,0:T(8,128)S(1)}, u32[]{:S(2)}, u32[]{:S(2)}) collective-permute-start(f32[136,128]{1,0:T(8,128)S(1)} %add.15), channel_id=1, source_target_pairs={{0,2},{2,0},{4,6},{6,4},{8,10},{10,8},{12,14},{14,12},{1,3},{3,1},... | collective-permute-start | bytes 208904 | tf_op jit(solution)/shard_map/ppermute | solution.py:355
  44.1 6.9 %collective-permute-start.20 = (f32[136,128]{1,0:T(8,128)S(1)}, f32[136,128]{1,0:T(8,128)S(1)}, u32[]{:S(2)}, u32[]{:S(2)}) collective-permute-start(f32[136,128]{1,0:T(8,128)S(1)} %add.16), channel_id=1, source_target_pairs={{0,12},{2,14},{4,8},{6,10},{8,4},{10,6},{12,0},{14,2},{1,13},{3,15... | collective-permute-start | bytes 208904 | tf_op jit(solution)/shard_map/ppermute | solution.py:355
  46.0 6.5 %collective-permute-start.19 = (f32[136,128]{1,0:T(8,128)S(1)}, f32[136,128]{1,0:T(8,128)S(1)}, u32[]{:S(2)}, u32[]{:S(2)}) collective-permute-start(f32[136,128]{1,0:T(8,128)S(1)} %add.16), channel_id=1, source_target_pairs={{0,8},{2,10},{4,12},{6,14},{8,0},{10,2},{12,4},{14,6},{1,9},{3,11}... | collective-permute-start | bytes 208904 | tf_op jit(solution)/shard_map/ppermute | solution.py:355
  46.0 6.5 %collective-permute-start.18 = (f32[136,128]{1,0:T(8,128)S(1)}, f32[136,128]{1,0:T(8,128)S(1)}, u32[]{:S(2)}, u32[]{:S(2)}) collective-permute-start(f32[136,128]{1,0:T(8,128)S(1)} %add.16), channel_id=1, source_target_pairs={{0,4},{2,6},{4,0},{6,2},{8,12},{10,14},{12,8},{14,10},{1,5},{3,7},... | collective-permute-start | bytes 208904 | tf_op jit(solution)/shard_map/ppermute | solution.py:355
  52.5 1.3 %collective-permute-start.21 = (f32[136,128]{1,0:T(8,128)S(1)}, f32[136,128]{1,0:T(8,128)S(1)}, u32[]{:S(2)}, u32[]{:S(2)}) collective-permute-start(f32[136,128]{1,0:T(8,128)S(1)} %add_add_fusion.mine), channel_id=1, source_target_pairs={{0,1},{1,0},{2,3},{3,2},{4,5},{5,4},{6,7},{7,6},{8,9},{9,8},{10,11... | collective-permute-start | bytes 208904 | tf_op jit(solution)/shard_map/ppermute | solution.py:58
  (1 other events, 4.1 us)

commit v7 on v6

--- a/solution.py
+++ b/solution.py
@@ -172,12 +172,10 @@
     return part[:width].astype(jnp.int32).astype(F32) * jnp.exp2(power - 15.0)
 
 
-def late_kernel(cap, table, images, aside, jac_near, jac_far, near, far, noise, out, kept, sent):
+def late_kernel(cap, table, images, aside, near, far, noise, out, kept, sent):
     half, width, rows = out.shape
-    slots, reach, _, cells = jac_near.shape
     base = core_index() * half
-    at = len(OFFSETS) * (cap + 1) + base
-    live = table[len(OFFSETS) * (cap + 1) + reach * slots]
+    live = table[table.shape[0] - 1]
     band = jnp.concatenate([near[...], far[...]], axis=0)
     size = half // 2
     for first in range(0, half, size):
@@ -189,21 +187,30 @@
             out[first + j] = (image.T * scale).astype(BF16)
 
     left = jnp.concatenate([out[j] for j in range(half)], axis=1)
-    total = dot(left, jnp.concatenate([aside[j] for j in range(half)], axis=0))
-    kept[0] = total[:, :cells]
-    encode(total[:, cells:], sent.at[0])
-    ahead = place_of("ahead")
+    put_bucket(dot(left, jnp.concatenate([aside[j] for j in range(half)], axis=0)), kept, sent)
+
+
+def put_bucket(total, kept, sent):
+    cells = kept.shape[1]
+    kept[...] = total[:, :cells]
+    encode(total[:, cells:], sent)
+
+
+def ahead_kernel(cap, table, weighted, jac_near, jac_far, kept, sent):
+    half = weighted.shape[0]
+    slots, reach = jac_near.shape[:2]
+    base = core_index() * half
+    at = len(OFFSETS) * (cap + 1) + base
+    wanted = place_of("ahead")
     left, right = [], []
     for j in range(half):
         places = [table[at + f * slots + j] for f in range(reach)]
-        chosen = sum(f * (places[f] == ahead).astype(jnp.int32) for f in range(reach))
-        found = sum((place == ahead).astype(jnp.int32) for place in places)
-        block = out[j]
+        chosen = sum(f * (places[f] == wanted).astype(jnp.int32) for f in range(reach))
+        found = sum((place == wanted).astype(jnp.int32) for place in places)
+        block = weighted[j]
         left.append(jnp.where(found > 0, block, jnp.zeros_like(block)))
         right.append(jnp.concatenate([jac_near[base + j, chosen], jac_far[base + j, chosen]], axis=1))
-    total = dot(jnp.concatenate(left, axis=1), jnp.concatenate(right, axis=0))
-    kept[1] = total[:, :cells]
-    encode(total[:, cells:], sent.at[1])
+    put_bucket(dot(jnp.concatenate(left, axis=1), jnp.concatenate(right, axis=0)), kept, sent)
 
 
 def backward_kernel(roles, coded, cap, table, jac, weighted, *rest):
@@ -237,11 +244,6 @@
 
 def merge_kernel(value, part, out):
     encode(value[...] + decode(part), out)
-
-
-def merge_two_kernel(kept, sent, first, second):
-    encode(kept[0] + decode(sent.at[0]), first)
-    encode(kept[1] + decode(sent.at[1]), second)
 
 
 def field_kernel(probes, own, *rest):
@@ -408,19 +410,27 @@
     beyond = swapped(back)
     plain = jax.ShapeDtypeStruct((width, cells), F32)
     message = jax.ShapeDtypeStruct((width + PAD, cells), jnp.int16)
+    shares = (held(staged, pltpu.VMEM), held(jac_far, pltpu.VMEM))
     weighted, kept, sent = kernel_call(
         functools.partial(late_kernel, cap),
-        (
-            jax.ShapeDtypeStruct((half, width, rows), BF16),
-            jax.ShapeDtypeStruct((2,) + plain.shape, F32),
-            jax.ShapeDtypeStruct((2,) + message.shape, jnp.int16),
-        ),
-        [SMEM] + [VMEM] * 7,
+        (jax.ShapeDtypeStruct((half, width, rows), BF16), plain, message),
+        [SMEM] + [VMEM] * 5,
         (VMEM,) * 3,
-    )(table, *early, held(staged, pltpu.VMEM), held(jac_far, pltpu.VMEM), beyond, flipped(beyond), noise_weight)
-    beyond, ahead = kernel_call(merge_two_kernel, (message, message), [VMEM] * 2, (VMEM,) * 2)(kept, flipped(sent))
-    beyond, ahead, weighted = lax.optimization_barrier((beyond, ahead, weighted))
-    beyond, ahead = swapped(beyond), spread(ahead, -2)
+    )(table, *early, beyond, flipped(beyond), noise_weight)
+    kept_ahead, sent_ahead = kernel_call(
+        functools.partial(ahead_kernel, cap),
+        (plain, message),
+        [SMEM] + [VMEM] * 3,
+        (VMEM,) * 2,
+    )(table, weighted, *shares)
+
+    def merged(value, part):
+        return kernel_call(merge_kernel, message, [VMEM] * 2, VMEM)(value, part)
+
+    sent, sent_ahead = lax.optimization_barrier((flipped(sent), sent_ahead))
+    beyond = merged(kept, sent)
+    beyond, sent_ahead, weighted = lax.optimization_barrier((beyond, sent_ahead, weighted))
+    beyond, ahead = swapped(beyond), spread(merged(kept_ahead, flipped(sent_ahead)), -2)
     weighted = kernel_call(
         gather_kernel,
         jax.ShapeDtypeStruct((2 * half + 1, width, rows), BF16),
@@ -438,7 +448,7 @@
         )(table, held(staged, pltpu.VMEM), weighted)
 
     back, partner = buckets(("back", "partner"), (False, True), weighted)
-    back = kernel_call(merge_kernel, message, [VMEM] * 2, VMEM)(back, beyond)
+    back = merged(back, beyond)
     back, partner, weighted = lax.optimization_barrier((back, partner, weighted))
     arrived = [spread(back, 2), ahead, swapped(partner)]
     own = buckets(("own",), (False,), weighted)[0]

time: 95.4 us -> 94.8 us (level)
  waiting for transfers between devices: 15.9 us -> 14.6 us
    ppermute x10 -> x11, waiting for transfers between devices: 4.24 us -> 3.33 us  [shifted(): return lax.ppermute(value, axis, pairs)]
    ppermute x10 -> x11, starting transfers between devices: 2.48 us -> 2.61 us  [shifted(): return lax.ppermute(value, axis, pairs)]
  transfers between devices with their start and end apart: 22 -> 23, of which waited for: 10 -> 10; matrix products, arithmetic and copies ran while one was open for 0% -> 0% of each run, Pallas kernels for 9% -> 9%
where the time goes in v7:
time: 94.8 us; the launch traced here: 94.7 us
  Pallas kernels  51.9 us (55%)
  starting transfers between devices  26.6 us (28%)
  waiting for transfers between devices  14.6 us (15%)
  between operations  1.51 us (2%)
    pallas_call x1, Pallas kernels, on_device(): kernel_call(functools.partial(finish_kernel, scale, 2), (jax.ShapeDtypeSt...  41.4 us
    ppermute x4, starting transfers between devices, spread(): lax.ppermute(value, 'tile', [(i, (i + (steps, -steps)[i % 2]) % count) fo...  9.97 us
    ppermute x4, starting transfers between devices, swapped(): lax.ppermute(value, 'tile', [(i, i ^ 1) for i in range(lax.axis_size('til...  7.85 us
    ppermute x4, waiting for transfers between devices, exchanged(): return lax.ppermute(value, 'tile', [(i, i ^ jump) for i in range(count)])  6.88 us
    ppermute x4, starting transfers between devices, exchanged(): return lax.ppermute(value, 'tile', [(i, i ^ jump) for i in range(count)])  6.18 us
    ppermute x11, waiting for transfers between devices, shifted(): return lax.ppermute(value, axis, pairs)  3.33 us
    ppermute x4, waiting for transfers between devices, spread(): lax.ppermute(value, 'tile', [(i, (i + (steps, -steps)[i % 2]) % count) fo...  3.11 us
    pallas_call x1, Pallas kernels, on_device(): kernel_call(stage_kernel, pltpu.VMEM(jacobian.shape, BF16), [HBM], VMEM,...  2.79 us
  transfers between devices with their start and end apart: 23, of which 10 were waited for; matrix products, arithmetic and copies ran while one was open for 0% of the time, Pallas kernels for 9%

profile of v7, /device:TPU:0, one launch (start us, length us, event | category | flops | bytes accessed | tf_op | source)
XLA Modules:
  0.0 94.7 jit_solution(9610737467208525318)
XLA Ops:
  1.2 4.7 %collective-permute-start.2 = (bf16[256,256]{1,0:T(8,128)(2,1)}, bf16[256,256]{1,0:T(8,128)(2,1)S(1)}, u32[]{:S(2)}, u32[]{:S(2)}) collective-permute-start(bf16[256,256]{1,0:T(8,128)(2,1)} %bitcast.3), channel_id=1, source_target_pairs={{0,12},{2,6},{4,0},{6,10},{8,4},{10,14},{12,8},{14,2},{1,13},{3,7}... | collective-permute-start | bytes 393224 | tf_op jit(solution)/shard_map/ppermute | solution.py:71
  5.8 1.0 %collective-permute-start = (bf16[256,256]{1,0:T(8,128)(2,1)}, bf16[256,256]{1,0:T(8,128)(2,1)S(1)}, u32[]{:S(2)}, u32[]{:S(2)}) collective-permute-start(bf16[256,256]{1,0:T(8,128)(2,1)} %bitcast.5), channel_id=1, source_target_pairs={{0,4},{2,14},{4,8},{6,2},{8,12},{10,6},{12,0},{14,10},{1,5},{3,15}... | collective-permute-start | bytes 393224 | tf_op jit(solution)/shard_map/ppermute | solution.py:71
  6.9 2.8 %shard_map.68.jac_near.jac = bf16[32,3,128,256]{3,2,1,0:T(8,128)(2,1)S(1)} custom-call(bf16[32,3,128,256]{3,2,1,0:T(8,128)(2,1)} %value.1), custom_call_target="tpu_custom_call" | custom-call | flops 1024 | bytes 1024 | tf_op jit(solution)/shard_map/pallas_call | solution.py:380
  10.0 2.1 %collective-permute-start.8 = (bf16[256,256]{1,0:T(8,128)(2,1)S(1)}, bf16[256,256]{1,0:T(8,128)(2,1)S(1)}, u32[]{:S(2)}, u32[]{:S(2)}) collective-permute-start(bf16[256,256]{1,0:T(8,128)(2,1)S(1)} %collective-permute-done.2.rest_1_), channel_id=1, source_target_pairs={{0,2},{2,0},{4,6},{6,4},{8,10},{10,8},{12,14},{14,12},{1,3},{3,1},... | collective-permute-start | bytes 393224 | tf_op jit(solution)/shard_map/ppermute | solution.py:66
  12.7 1.3 %shard_map.69.table = s32[262]{0:T(512)S(4)} custom-call(s32[3,32]{1,0:T(4,128)S(1)} %bitcast.9, s32[1]{0:T(128)S(6)} %copy.7.live), custom_call_target="tpu_custom_call" | custom-call | flops 1024 | bytes 1024 | tf_op jit(solution)/shard_map/pallas_call | solution.py:388
  14.9 1.3 %collective-permute-done.8.near = bf16[256,256]{1,0:T(8,128)(2,1)S(1)} collective-permute-done((bf16[256,256]{1,0:T(8,128)(2,1)S(1)}, bf16[256,256]{1,0:T(8,128)(2,1)S(1)}, u32[]{:S(2)}, u32[]{:S(2)}) %collective-permute-start.8) | collective-permute-done | bytes 131104 | tf_op jit(solution)/shard_map/ppermute | solution.py:66
  16.3 1.9 %shard_map.70 = (f32[16,128,256]{2,1,0:T(8,128)S(1)}, bf16[16,128,512]{2,1,0:T(8,128)(2,1)S(1)}) custom-call(s32[262]{0:T(512)S(4)} %shard_map.69.table, bf16[32,3,128,256]{3,2,1,0:T(8,128)(2,1)S(1)} %shard_map.68.jac_near.jac, bf16[32,3,128,256]{3,2,1,0:T(8,128)(2,1)S(1)} %collective-permute-done.4.jac_far, bf16[256,256]{1,0:T(8,128)(2,1)S(1)} %bitcast.7, ...), custom_call_target="tpu_custom_call" | custom-call | flops 1024 | bytes 1024 | tf_op jit(solution)/shard_map/pallas_call | solution.py:400
  18.2 1.3 %shard_map.71 = (bf16[16,256,128]{2,1,0:T(8,128)(2,1)S(1)}, f32[256,256]{1,0:T(8,128)S(1)}, s16[272,256]{1,0:T(8,128)(2,1)S(1)}) custom-call(s32[262]{0:T(512)S(4)} %shard_map.69.table, f32[16,128,256]{2,1,0:T(8,128)S(1)} %get-tuple-element.34.images, bf16[16,128,512]{2,1,0:T(8,128)(2,1)S(1)} %get-tuple-element.35.aside, ...), custom_call_target="tpu_custom_call" | custom-call | flops 1024 | bytes 1024 | tf_op jit(solution)/shard_map/pallas_call | solution.py:414
  20.1 0.8 shard_map.72
  21.8 1.8 %collective-permute-start.12 = (s16[272,256]{1,0:T(8,128)(2,1)S(1)}, s16[272,256]{1,0:T(8,128)(2,1)S(1)}, u32[]{:S(2)}, u32[]{:S(2)}) collective-permute-start(s16[272,256]{1,0:T(8,128)(2,1)S(1)} %shard_map.73), channel_id=1, source_target_pairs={{0,2},{2,0},{4,6},{6,4},{8,10},{10,8},{12,14},{14,12},{1,3},{3,1},... | collective-permute-start | bytes 417800 | tf_op jit(solution)/shard_map/ppermute | solution.py:66
  24.4 4.2 %collective-permute-start.15 = (s16[272,256]{1,0:T(8,128)(2,1)S(1)}, s16[272,256]{1,0:T(8,128)(2,1)S(1)}, u32[]{:S(2)}, u32[]{:S(2)}) collective-permute-start(s16[272,256]{1,0:T(8,128)(2,1)S(1)} %shard_map.78), channel_id=1, source_target_pairs={{0,12},{2,6},{4,0},{6,10},{8,4},{10,14},{12,8},{14,2},{1,13},{3,7}... | collective-permute-start | bytes 417800 | tf_op jit(solution)/shard_map/ppermute | solution.py:71
  28.6 0.9 shard_map.75
  29.7 4.0 %collective-permute-start.16 = (s16[272,256]{1,0:T(8,128)(2,1)S(1)}, s16[272,256]{1,0:T(8,128)(2,1)S(1)}, u32[]{:S(2)}, u32[]{:S(2)}) collective-permute-start(s16[272,256]{1,0:T(8,128)(2,1)S(1)} %get-tuple-element.50), channel_id=1, source_target_pairs={{0,2},{2,0},{4,6},{6,4},{8,10},{10,8},{12,14},{14,12},{1,3},{3,1},... | collective-permute-start | bytes 417800 | tf_op jit(solution)/shard_map/ppermute | solution.py:66
  33.7 0.6 shard_map.77.own
  34.4 2.8 %collective-permute-done.13.rest_0_ = s16[272,256]{1,0:T(8,128)(2,1)S(1)} collective-permute-done((s16[272,256]{1,0:T(8,128)(2,1)S(1)}, s16[272,256]{1,0:T(8,128)(2,1)S(1)}, u32[]{:S(2)}, u32[]{:S(2)}) %collective-permute-start.13) | collective-permute-done | bytes 139296 | tf_op jit(solution)/shard_map/ppermute | solution.py:71
  37.6 1.2 %collective-permute-done.17 = f32[136,128]{1,0:T(8,128)S(1)} collective-permute-done((f32[136,128]{1,0:T(8,128)S(1)}, f32[136,128]{1,0:T(8,128)S(1)}, u32[]{:S(2)}, u32[]{:S(2)}) %collective-permute-start.17) | collective-permute-done | bytes 69664 | tf_op jit(solution)/shard_map/ppermute | solution.py:58
  38.9 1.7 %collective-permute-start.18 = (f32[136,128]{1,0:T(8,128)S(1)}, f32[136,128]{1,0:T(8,128)S(1)}, u32[]{:S(2)}, u32[]{:S(2)}) collective-permute-start(f32[136,128]{1,0:T(8,128)S(1)} %add.15), channel_id=1, source_target_pairs={{0,2},{2,0},{4,6},{6,4},{8,10},{10,8},{12,14},{14,12},{1,3},{3,1},... | collective-permute-start | bytes 208904 | tf_op jit(solution)/shard_map/ppermute | solution.py:357
  40.6 2.6 %collective-permute-done.18 = f32[136,128]{1,0:T(8,128)S(1)} collective-permute-done((f32[136,128]{1,0:T(8,128)S(1)}, f32[136,128]{1,0:T(8,128)S(1)}, u32[]{:S(2)}, u32[]{:S(2)}) %collective-permute-start.18) | collective-permute-done | bytes 69664 | tf_op jit(solution)/shard_map/ppermute | solution.py:357
  43.3 2.3 %collective-permute-start.21 = (f32[136,128]{1,0:T(8,128)S(1)}, f32[136,128]{1,0:T(8,128)S(1)}, u32[]{:S(2)}, u32[]{:S(2)}) collective-permute-start(f32[136,128]{1,0:T(8,128)S(1)} %add.16), channel_id=1, source_target_pairs={{0,12},{2,14},{4,8},{6,10},{8,4},{10,6},{12,0},{14,2},{1,13},{3,15... | collective-permute-start | bytes 208904 | tf_op jit(solution)/shard_map/ppermute | solution.py:357
  45.5 2.2 %collective-permute-start.19 = (f32[136,128]{1,0:T(8,128)S(1)}, f32[136,128]{1,0:T(8,128)S(1)}, u32[]{:S(2)}, u32[]{:S(2)}) collective-permute-start(f32[136,128]{1,0:T(8,128)S(1)} %add.16), channel_id=1, source_target_pairs={{0,4},{2,6},{4,0},{6,2},{8,12},{10,14},{12,8},{14,10},{1,5},{3,7},... | collective-permute-start | bytes 208904 | tf_op jit(solution)/shard_map/ppermute | solution.py:357
  47.7 2.2 %collective-permute-done.21 = f32[136,128]{1,0:T(8,128)S(1)} collective-permute-done((f32[136,128]{1,0:T(8,128)S(1)}, f32[136,128]{1,0:T(8,128)S(1)}, u32[]{:S(2)}, u32[]{:S(2)}) %collective-permute-start.21) | collective-permute-done | bytes 69664 | tf_op jit(solution)/shard_map/ppermute | solution.py:357
  49.9 2.0 %collective-permute-done.20 = f32[136,128]{1,0:T(8,128)S(1)} collective-permute-done((f32[136,128]{1,0:T(8,128)S(1)}, f32[136,128]{1,0:T(8,128)S(1)}, u32[]{:S(2)}, u32[]{:S(2)}) %collective-permute-start.20) | collective-permute-done | bytes 69664 | tf_op jit(solution)/shard_map/ppermute | solution.py:357
  52.1 1.2 %collective-permute-done.22.other = f32[136,128]{1,0:T(8,128)S(1)} collective-permute-done((f32[136,128]{1,0:T(8,128)S(1)}, f32[136,128]{1,0:T(8,128)S(1)}, u32[]{:S(2)}, u32[]{:S(2)}) %collective-permute-start.22) | collective-permute-done | bytes 69664 | tf_op jit(solution)/shard_map/ppermute | solution.py:58
  53.3 41.4 %shard_map.80 = (f32[256,256]{1,0:T(8,128)}, f32[256,256]{1,0:T(8,128)}) custom-call(f32[136,128]{1,0:T(8,128)S(1)} %add_add_fusion.mine, f32[136,128]{1,0:T(8,128)S(1)} %collective-permute-done.22.other, f32[256,256]{1,0:T(8,128)S(1)} %get-tuple-element.53.field), custom_call_target="tpu_custom_call" | custom-call | flops 1024 | bytes 1024 | tf_op jit(solution)/shard_map/pallas_call | solution.py:465
  (44 shorter events, 4.8 us)
Async XLA Ops:
  0.6 15.6 %collective-permute-start.4 = (bf16[32,3,128,256]{3,2,1,0:T(8,128)(2,1)}, bf16[32,3,128,256]{3,2,1,0:T(8,128)(2,1)S(1)}, u32[]{:S(2)}, u32[]{:S(2)}) collective-permute-start(bf16[32,3,128,256]{3,2,1,0:T(8,128)(2,1)} %value.1), channel_id=1, source_target_pairs={{0,1},{1,0},{2,3},{3,2},{4,5},{5,4},{6,7},{7,6},{8,9},{9,8},{10,11... | collective-permute-start | bytes 18874376 | tf_op jit(solution)/shard_map/ppermute | solution.py:58
  1.1 13.0 %copy-start = (bf16[1,256,256]{2,1,0:T(8,128)(2,1)S(1)}, bf16[1,256,256]{2,1,0:T(8,128)(2,1)}, u32[]{:S(2)}) copy-start(bf16[1,256,256]{2,1,0:T(8,128)(2,1)} %param.9) | copy-start | bytes 393220
  1.2 8.9 %collective-permute-start.2 = (bf16[256,256]{1,0:T(8,128)(2,1)}, bf16[256,256]{1,0:T(8,128)(2,1)S(1)}, u32[]{:S(2)}, u32[]{:S(2)}) collective-permute-start(bf16[256,256]{1,0:T(8,128)(2,1)} %bitcast.3), channel_id=1, source_target_pairs={{0,12},{2,6},{4,0},{6,10},{8,4},{10,14},{12,8},{14,2},{1,13},{3,7}... | collective-permute-start | bytes 393224 | tf_op jit(solution)/shard_map/ppermute | solution.py:71
  5.8 8.3 %collective-permute-start.1 = (bf16[256,256]{1,0:T(8,128)(2,1)}, bf16[256,256]{1,0:T(8,128)(2,1)S(1)}, u32[]{:S(2)}, u32[]{:S(2)}) collective-permute-start(bf16[256,256]{1,0:T(8,128)(2,1)} %bitcast.4), channel_id=1, source_target_pairs={{0,2},{2,0},{4,6},{6,4},{8,10},{10,8},{12,14},{14,12},{1,3},{3,1},... | collective-permute-start | bytes 393224 | tf_op jit(solution)/shard_map/ppermute | solution.py:66
  5.8 8.6 %collective-permute-start = (bf16[256,256]{1,0:T(8,128)(2,1)}, bf16[256,256]{1,0:T(8,128)(2,1)S(1)}, u32[]{:S(2)}, u32[]{:S(2)}) collective-permute-start(bf16[256,256]{1,0:T(8,128)(2,1)} %bitcast.5), channel_id=1, source_target_pairs={{0,4},{2,14},{4,8},{6,2},{8,12},{10,6},{12,0},{14,10},{1,5},{3,15}... | collective-permute-start | bytes 393224 | tf_op jit(solution)/shard_map/ppermute | solution.py:71
  10.0 4.4 %collective-permute-start.3 = (bf16[256,256]{1,0:T(8,128)(2,1)S(1)}, bf16[256,256]{1,0:T(8,128)(2,1)S(1)}, u32[]{:S(2)}, u32[]{:S(2)}) collective-permute-start(bf16[256,256]{1,0:T(8,128)(2,1)S(1)} %collective-permute-done.2.rest_1_), channel_id=1, source_target_pairs={{0,1},{1,0},{2,3},{3,2},{4,5},{5,4},{6,7},{7,6},{8,9},{9,8},{10,11... | collective-permute-start | bytes 393224 | tf_op jit(solution)/shard_map/ppermute | solution.py:58
  10.0 6.2 %collective-permute-start.8 = (bf16[256,256]{1,0:T(8,128)(2,1)S(1)}, bf16[256,256]{1,0:T(8,128)(2,1)S(1)}, u32[]{:S(2)}, u32[]{:S(2)}) collective-permute-start(bf16[256,256]{1,0:T(8,128)(2,1)S(1)} %collective-permute-done.2.rest_1_), channel_id=1, source_target_pairs={{0,2},{2,0},{4,6},{6,4},{8,10},{10,8},{12,14},{14,12},{1,3},{3,1},... | collective-permute-start | bytes 393224 | tf_op jit(solution)/shard_map/ppermute | solution.py:66
  14.1 2.1 %collective-permute-start.5 = (bf16[256,256]{1,0:T(8,128)(2,1)S(1)}, bf16[256,256]{1,0:T(8,128)(2,1)S(1)}, u32[]{:S(2)}, u32[]{:S(2)}) collective-permute-start(bf16[256,256]{1,0:T(8,128)(2,1)S(1)} %bitcast.6), channel_id=1, source_target_pairs={{0,1},{1,0},{2,3},{3,2},{4,5},{5,4},{6,7},{7,6},{8,9},{9,8},{10,11... | collective-permute-start | bytes 393224 | tf_op jit(solution)/shard_map/ppermute | solution.py:58
  14.4 1.8 %collective-permute-start.6 = (bf16[256,256]{1,0:T(8,128)(2,1)S(1)}, bf16[256,256]{1,0:T(8,128)(2,1)S(1)}, u32[]{:S(2)}, u32[]{:S(2)}) collective-permute-start(bf16[256,256]{1,0:T(8,128)(2,1)S(1)} %collective-permute-done.rest_2_), channel_id=1, source_target_pairs={{0,1},{1,0},{2,3},{3,2},{4,5},{5,4},{6,7},{7,6},{8,9},{9,8},{10,11... | collective-permute-start | bytes 393224 | tf_op jit(solution)/shard_map/ppermute | solution.py:58
  14.7 1.5 %collective-permute-start.7 = (bf16[256,256]{1,0:T(8,128)(2,1)S(1)}, bf16[256,256]{1,0:T(8,128)(2,1)S(1)}, u32[]{:S(2)}, u32[]{:S(2)}) collective-permute-start(bf16[256,256]{1,0:T(8,128)(2,1)S(1)} %collective-permute-done.1.rest_3_), channel_id=1, source_target_pairs={{0,1},{1,0},{2,3},{3,2},{4,5},{5,4},{6,7},{7,6},{8,9},{9,8},{10,11... | collective-permute-start | bytes 393224 | tf_op jit(solution)/shard_map/ppermute | solution.py:58
  16.2 1.9 %collective-permute-start.9 = (bf16[256,256]{1,0:T(8,128)(2,1)S(1)}, bf16[256,256]{1,0:T(8,128)(2,1)S(1)}, u32[]{:S(2)}, u32[]{:S(2)}) collective-permute-start(bf16[256,256]{1,0:T(8,128)(2,1)S(1)} %collective-permute-done.8.near), channel_id=1, source_target_pairs={{0,1},{1,0},{2,3},{3,2},{4,5},{5,4},{6,7},{7,6},{8,9},{9,8},{10,11... | collective-permute-start | bytes 393224 | tf_op jit(solution)/shard_map/ppermute | solution.py:58
  19.5 1.6 %collective-permute-start.10 = (s16[272,256]{1,0:T(8,128)(2,1)S(1)}, s16[272,256]{1,0:T(8,128)(2,1)S(1)}, u32[]{:S(2)}, u32[]{:S(2)}) collective-permute-start(s16[272,256]{1,0:T(8,128)(2,1)S(1)} %get-tuple-element.37), channel_id=1, source_target_pairs={{0,1},{1,0},{2,3},{3,2},{4,5},{5,4},{6,7},{7,6},{8,9},{9,8},{10,11... | collective-permute-start | bytes 417800 | tf_op jit(solution)/shard_map/ppermute | solution.py:58
  21.2 3.0 %collective-permute-start.11 = (bf16[16,256,128]{2,1,0:T(8,128)(2,1)S(1)}, bf16[16,256,128]{2,1,0:T(8,128)(2,1)S(1)}, u32[]{:S(2)}, u32[]{:S(2)}) collective-permute-start(bf16[16,256,128]{2,1,0:T(8,128)(2,1)S(1)} %get-tuple-element.42.weighted.mine), channel_id=1, source_target_pairs={{0,1},{1,0},{2,3},{3,2},{4,5},{5,4},{6,7},{7,6},{8,9},{9,8},{10,11... | collective-permute-start | bytes 3145736 | tf_op jit(solution)/shard_map/ppermute | solution.py:58
  21.6 2.5 %collective-permute-start.14 = (s16[272,256]{1,0:T(8,128)(2,1)S(1)}, s16[272,256]{1,0:T(8,128)(2,1)S(1)}, u32[]{:S(2)}, u32[]{:S(2)}) collective-permute-start(s16[272,256]{1,0:T(8,128)(2,1)S(1)} %get-tuple-element.49), channel_id=1, source_target_pairs={{0,1},{1,0},{2,3},{3,2},{4,5},{5,4},{6,7},{7,6},{8,9},{9,8},{10,11... | collective-permute-start | bytes 417800 | tf_op jit(solution)/shard_map/ppermute | solution.py:58
  21.8 7.7 %collective-permute-start.12 = (s16[272,256]{1,0:T(8,128)(2,1)S(1)}, s16[272,256]{1,0:T(8,128)(2,1)S(1)}, u32[]{:S(2)}, u32[]{:S(2)}) collective-permute-start(s16[272,256]{1,0:T(8,128)(2,1)S(1)} %shard_map.73), channel_id=1, source_target_pairs={{0,2},{2,0},{4,6},{6,4},{8,10},{10,8},{12,14},{14,12},{1,3},{3,1},... | collective-permute-start | bytes 417800 | tf_op jit(solution)/shard_map/ppermute | solution.py:66
  24.4 9.9 %collective-permute-start.15 = (s16[272,256]{1,0:T(8,128)(2,1)S(1)}, s16[272,256]{1,0:T(8,128)(2,1)S(1)}, u32[]{:S(2)}, u32[]{:S(2)}) collective-permute-start(s16[272,256]{1,0:T(8,128)(2,1)S(1)} %shard_map.78), channel_id=1, source_target_pairs={{0,12},{2,6},{4,0},{6,10},{8,4},{10,14},{12,8},{14,2},{1,13},{3,7}... | collective-permute-start | bytes 417800 | tf_op jit(solution)/shard_map/ppermute | solution.py:71
  29.6 7.5 %collective-permute-start.13 = (s16[272,256]{1,0:T(8,128)(2,1)S(1)}, s16[272,256]{1,0:T(8,128)(2,1)S(1)}, u32[]{:S(2)}, u32[]{:S(2)}) collective-permute-start(s16[272,256]{1,0:T(8,128)(2,1)S(1)} %shard_map.76), channel_id=1, source_target_pairs={{0,4},{2,14},{4,8},{6,2},{8,12},{10,6},{12,0},{14,10},{1,5},{3,15}... | collective-permute-start | bytes 417800 | tf_op jit(solution)/shard_map/ppermute | solution.py:71
  29.7 7.4 %collective-permute-start.16 = (s16[272,256]{1,0:T(8,128)(2,1)S(1)}, s16[272,256]{1,0:T(8,128)(2,1)S(1)}, u32[]{:S(2)}, u32[]{:S(2)}) collective-permute-start(s16[272,256]{1,0:T(8,128)(2,1)S(1)} %get-tuple-element.50), channel_id=1, source_target_pairs={{0,2},{2,0},{4,6},{6,4},{8,10},{10,8},{12,14},{14,12},{1,3},{3,1},... | collective-permute-start | bytes 417800 | tf_op jit(solution)/shard_map/ppermute | solution.py:66
  37.5 1.3 %collective-permute-start.17 = (f32[136,128]{1,0:T(8,128)S(1)}, f32[136,128]{1,0:T(8,128)S(1)}, u32[]{:S(2)}, u32[]{:S(2)}) collective-permute-start(f32[136,128]{1,0:T(8,128)S(1)} %get-tuple-element.52), channel_id=1, source_target_pairs={{0,1},{1,0},{2,3},{3,2},{4,5},{5,4},{6,7},{7,6},{8,9},{9,8},{10,11... | collective-permute-start | bytes 208904 | tf_op jit(solution)/shard_map/ppermute | solution.py:58
  38.9 4.4 %collective-permute-start.18 = (f32[136,128]{1,0:T(8,128)S(1)}, f32[136,128]{1,0:T(8,128)S(1)}, u32[]{:S(2)}, u32[]{:S(2)}) collective-permute-start(f32[136,128]{1,0:T(8,128)S(1)} %add.15), channel_id=1, source_target_pairs={{0,2},{2,0},{4,6},{6,4},{8,10},{10,8},{12,14},{14,12},{1,3},{3,1},... | collective-permute-start | bytes 208904 | tf_op jit(solution)/shard_map/ppermute | solution.py:357
  43.3 6.7 %collective-permute-start.21 = (f32[136,128]{1,0:T(8,128)S(1)}, f32[136,128]{1,0:T(8,128)S(1)}, u32[]{:S(2)}, u32[]{:S(2)}) collective-permute-start(f32[136,128]{1,0:T(8,128)S(1)} %add.16), channel_id=1, source_target_pairs={{0,12},{2,14},{4,8},{6,10},{8,4},{10,6},{12,0},{14,2},{1,13},{3,15... | collective-permute-start | bytes 208904 | tf_op jit(solution)/shard_map/ppermute | solution.py:357
  45.5 6.4 %collective-permute-start.20 = (f32[136,128]{1,0:T(8,128)S(1)}, f32[136,128]{1,0:T(8,128)S(1)}, u32[]{:S(2)}, u32[]{:S(2)}) collective-permute-start(f32[136,128]{1,0:T(8,128)S(1)} %add.16), channel_id=1, source_target_pairs={{0,8},{2,10},{4,12},{6,14},{8,0},{10,2},{12,4},{14,6},{1,9},{3,11}... | collective-permute-start | bytes 208904 | tf_op jit(solution)/shard_map/ppermute | solution.py:357
  45.5 6.4 %collective-permute-start.19 = (f32[136,128]{1,0:T(8,128)S(1)}, f32[136,128]{1,0:T(8,128)S(1)}, u32[]{:S(2)}, u32[]{:S(2)}) collective-permute-start(f32[136,128]{1,0:T(8,128)S(1)} %add.16), channel_id=1, source_target_pairs={{0,4},{2,6},{4,0},{6,2},{8,12},{10,14},{12,8},{14,10},{1,5},{3,7},... | collective-permute-start | bytes 208904 | tf_op jit(solution)/shard_map/ppermute | solution.py:357
  52.0 1.3 %collective-permute-start.22 = (f32[136,128]{1,0:T(8,128)S(1)}, f32[136,128]{1,0:T(8,128)S(1)}, u32[]{:S(2)}, u32[]{:S(2)}) collective-permute-start(f32[136,128]{1,0:T(8,128)S(1)} %add_add_fusion.mine), channel_id=1, source_target_pairs={{0,1},{1,0},{2,3},{3,2},{4,5},{5,4},{6,7},{7,6},{8,9},{9,8},{10,11... | collective-permute-start | bytes 208904 | tf_op jit(solution)/shard_map/ppermute | solution.py:58
  (2 other events, 15.7 us)

commit v8 on v7

--- a/solution.py
+++ b/solution.py
@@ -14,6 +14,8 @@
 NT = (((1,), (1,)), ((), ()))
 OFFSETS = (-2, -1, 0, 1, 2)
 PAD = 16
+ENOUGH = 1e-2
+REFINED = 6
 ROWS = 8
 LIMIT = 16 << 20
 VMEM = pl.BlockSpec(memory_space=pltpu.VMEM)
@@ -314,15 +316,22 @@
         error = dot(dot(now, a_high[...]).astype(BF16), now, NT) - eye
         exact = now.astype(F32) - dot(correction(error), now)
         now = exact.astype(BF16)
-    full = halves(exact)
-    error = dot3(halves(dot3(full, (a_high[...], a_low[...]))), full, NT) - eye
-    left = jnp.sum(error * error)
-    solution_of = (exact - dot(correction(error), full[0])) * along
+    inverse[...] = exact
+
+    def refined(state):
+        full = halves(inverse[...])
+        error = dot3(halves(dot3(full, (a_high[...], a_low[...]))), full, NT) - eye
+        inverse[...] = inverse[...] - dot(correction(error), full[0])
+        return state[0] + 1, jnp.sum(error * error)
+
+    first = refined((0, 0.0))
+    _, left = lax.while_loop(lambda state: (state[0] < REFINED) & (state[1] >= ENOUGH), refined, first)
+    solution_of = inverse[...] * along
     inverse[...] = solution_of
     upper = dot3(halves(solution_of), halves(matrix)) * (1.0 / scale)
     factor[...] = jnp.where(row <= column, upper, 0.0)
 
-    @pl.when(jnp.logical_not(left < 1e-2))
+    @pl.when(jnp.logical_not(left < ENOUGH))
     def _():
         inverse[...] = eye
         across = lax.broadcasted_iota(jnp.int32, (1, width), 1)

time: 94.8 us -> 95.4 us (level)
  no operation moved by 1% of the time
where the time goes in v8:
time: 95.4 us; the launch traced here: 95.2 us
  Pallas kernels  52.4 us (55%)
  starting transfers between devices  26.6 us (28%)
  waiting for transfers between devices  14.6 us (15%)
  between operations  1.51 us (2%)
    pallas_call x1, Pallas kernels, on_device(): kernel_call(functools.partial(finish_kernel, scale, 2), (jax.ShapeDtypeSt...  41.9 us
    ppermute x4, starting transfers between devices, spread(): lax.ppermute(value, 'tile', [(i, (i + (steps, -steps)[i % 2]) % count) fo...  9.97 us
    ppermute x4, starting transfers between devices, swapped(): lax.ppermute(value, 'tile', [(i, i ^ 1) for i in range(lax.axis_size('til...  7.85 us
    ppermute x4, waiting for transfers between devices, exchanged(): return lax.ppermute(value, 'tile', [(i, i ^ jump) for i in range(count)])  6.88 us
    ppermute x4, starting transfers between devices, exchanged(): return lax.ppermute(value, 'tile', [(i, i ^ jump) for i in range(count)])  6.18 us
    ppermute x11, waiting for transfers between devices, shifted(): return lax.ppermute(value, axis, pairs)  3.33 us
    ppermute x4, waiting for transfers between devices, spread(): lax.ppermute(value, 'tile', [(i, (i + (steps, -steps)[i % 2]) % count) fo...  3.11 us
    pallas_call x1, Pallas kernels, on_device(): kernel_call(stage_kernel, pltpu.VMEM(jacobian.shape, BF16), [HBM], VMEM,...  2.79 us
  transfers between devices with their start and end apart: 23, of which 10 were waited for; matrix products, arithmetic and copies ran while one was open for 0% of the time, Pallas kernels for 9%

profile of v8, /device:TPU:0, one launch (start us, length us, event | category | flops | bytes accessed | tf_op | source)
XLA Modules:
  0.0 95.2 jit_solution(3433148800856317667)
XLA Ops:
  1.2 4.7 %collective-permute-start.2 = (bf16[256,256]{1,0:T(8,128)(2,1)}, bf16[256,256]{1,0:T(8,128)(2,1)S(1)}, u32[]{:S(2)}, u32[]{:S(2)}) collective-permute-start(bf16[256,256]{1,0:T(8,128)(2,1)} %bitcast.3), channel_id=1, source_target_pairs={{0,12},{2,6},{4,0},{6,10},{8,4},{10,14},{12,8},{14,2},{1,13},{3,7}... | collective-permute-start | bytes 393224 | tf_op jit(solution)/shard_map/ppermute | solution.py:73
  5.8 1.0 %collective-permute-start = (bf16[256,256]{1,0:T(8,128)(2,1)}, bf16[256,256]{1,0:T(8,128)(2,1)S(1)}, u32[]{:S(2)}, u32[]{:S(2)}) collective-permute-start(bf16[256,256]{1,0:T(8,128)(2,1)} %bitcast.5), channel_id=1, source_target_pairs={{0,4},{2,14},{4,8},{6,2},{8,12},{10,6},{12,0},{14,10},{1,5},{3,15}... | collective-permute-start | bytes 393224 | tf_op jit(solution)/shard_map/ppermute | solution.py:73
  6.9 2.8 %shard_map.68.jac_near.jac = bf16[32,3,128,256]{3,2,1,0:T(8,128)(2,1)S(1)} custom-call(bf16[32,3,128,256]{3,2,1,0:T(8,128)(2,1)} %value.1), custom_call_target="tpu_custom_call" | custom-call | flops 1024 | bytes 1024 | tf_op jit(solution)/shard_map/pallas_call | solution.py:389
  10.0 2.1 %collective-permute-start.8 = (bf16[256,256]{1,0:T(8,128)(2,1)S(1)}, bf16[256,256]{1,0:T(8,128)(2,1)S(1)}, u32[]{:S(2)}, u32[]{:S(2)}) collective-permute-start(bf16[256,256]{1,0:T(8,128)(2,1)S(1)} %collective-permute-done.2.rest_1_), channel_id=1, source_target_pairs={{0,2},{2,0},{4,6},{6,4},{8,10},{10,8},{12,14},{14,12},{1,3},{3,1},... | collective-permute-start | bytes 393224 | tf_op jit(solution)/shard_map/ppermute | solution.py:68
  12.7 1.3 %shard_map.69.table = s32[262]{0:T(512)S(4)} custom-call(s32[3,32]{1,0:T(4,128)S(1)} %bitcast.9, s32[1]{0:T(128)S(6)} %copy.7.live), custom_call_target="tpu_custom_call" | custom-call | flops 1024 | bytes 1024 | tf_op jit(solution)/shard_map/pallas_call | solution.py:397
  14.9 1.3 %collective-permute-done.8.near = bf16[256,256]{1,0:T(8,128)(2,1)S(1)} collective-permute-done((bf16[256,256]{1,0:T(8,128)(2,1)S(1)}, bf16[256,256]{1,0:T(8,128)(2,1)S(1)}, u32[]{:S(2)}, u32[]{:S(2)}) %collective-permute-start.8) | collective-permute-done | bytes 131104 | tf_op jit(solution)/shard_map/ppermute | solution.py:68
  16.3 1.9 %shard_map.70 = (f32[16,128,256]{2,1,0:T(8,128)S(1)}, bf16[16,128,512]{2,1,0:T(8,128)(2,1)S(1)}) custom-call(s32[262]{0:T(512)S(4)} %shard_map.69.table, bf16[32,3,128,256]{3,2,1,0:T(8,128)(2,1)S(1)} %shard_map.68.jac_near.jac, bf16[32,3,128,256]{3,2,1,0:T(8,128)(2,1)S(1)} %collective-permute-done.4.jac_far, bf16[256,256]{1,0:T(8,128)(2,1)S(1)} %bitcast.7, ...), custom_call_target="tpu_custom_call" | custom-call | flops 1024 | bytes 1024 | tf_op jit(solution)/shard_map/pallas_call | solution.py:409
  18.2 1.3 %shard_map.71 = (bf16[16,256,128]{2,1,0:T(8,128)(2,1)S(1)}, f32[256,256]{1,0:T(8,128)S(1)}, s16[272,256]{1,0:T(8,128)(2,1)S(1)}) custom-call(s32[262]{0:T(512)S(4)} %shard_map.69.table, f32[16,128,256]{2,1,0:T(8,128)S(1)} %get-tuple-element.34.images, bf16[16,128,512]{2,1,0:T(8,128)(2,1)S(1)} %get-tuple-element.35.aside, ...), custom_call_target="tpu_custom_call" | custom-call | flops 1024 | bytes 1024 | tf_op jit(solution)/shard_map/pallas_call | solution.py:423
  20.1 0.8 shard_map.72
  21.8 1.8 %collective-permute-start.12 = (s16[272,256]{1,0:T(8,128)(2,1)S(1)}, s16[272,256]{1,0:T(8,128)(2,1)S(1)}, u32[]{:S(2)}, u32[]{:S(2)}) collective-permute-start(s16[272,256]{1,0:T(8,128)(2,1)S(1)} %shard_map.73), channel_id=1, source_target_pairs={{0,2},{2,0},{4,6},{6,4},{8,10},{10,8},{12,14},{14,12},{1,3},{3,1},... | collective-permute-start | bytes 417800 | tf_op jit(solution)/shard_map/ppermute | solution.py:68
  24.4 4.2 %collective-permute-start.15 = (s16[272,256]{1,0:T(8,128)(2,1)S(1)}, s16[272,256]{1,0:T(8,128)(2,1)S(1)}, u32[]{:S(2)}, u32[]{:S(2)}) collective-permute-start(s16[272,256]{1,0:T(8,128)(2,1)S(1)} %shard_map.78), channel_id=1, source_target_pairs={{0,12},{2,6},{4,0},{6,10},{8,4},{10,14},{12,8},{14,2},{1,13},{3,7}... | collective-permute-start | bytes 417800 | tf_op jit(solution)/shard_map/ppermute | solution.py:73
  28.6 0.9 shard_map.75
  29.7 4.0 %collective-permute-start.16 = (s16[272,256]{1,0:T(8,128)(2,1)S(1)}, s16[272,256]{1,0:T(8,128)(2,1)S(1)}, u32[]{:S(2)}, u32[]{:S(2)}) collective-permute-start(s16[272,256]{1,0:T(8,128)(2,1)S(1)} %get-tuple-element.50), channel_id=1, source_target_pairs={{0,2},{2,0},{4,6},{6,4},{8,10},{10,8},{12,14},{14,12},{1,3},{3,1},... | collective-permute-start | bytes 417800 | tf_op jit(solution)/shard_map/ppermute | solution.py:68
  33.7 0.6 shard_map.77.own
  34.4 2.8 %collective-permute-done.13.rest_0_ = s16[272,256]{1,0:T(8,128)(2,1)S(1)} collective-permute-done((s16[272,256]{1,0:T(8,128)(2,1)S(1)}, s16[272,256]{1,0:T(8,128)(2,1)S(1)}, u32[]{:S(2)}, u32[]{:S(2)}) %collective-permute-start.13) | collective-permute-done | bytes 139296 | tf_op jit(solution)/shard_map/ppermute | solution.py:73
  37.6 1.2 %collective-permute-done.17 = f32[136,128]{1,0:T(8,128)S(1)} collective-permute-done((f32[136,128]{1,0:T(8,128)S(1)}, f32[136,128]{1,0:T(8,128)S(1)}, u32[]{:S(2)}, u32[]{:S(2)}) %collective-permute-start.17) | collective-permute-done | bytes 69664 | tf_op jit(solution)/shard_map/ppermute | solution.py:60
  38.9 1.7 %collective-permute-start.18 = (f32[136,128]{1,0:T(8,128)S(1)}, f32[136,128]{1,0:T(8,128)S(1)}, u32[]{:S(2)}, u32[]{:S(2)}) collective-permute-start(f32[136,128]{1,0:T(8,128)S(1)} %add.15), channel_id=1, source_target_pairs={{0,2},{2,0},{4,6},{6,4},{8,10},{10,8},{12,14},{14,12},{1,3},{3,1},... | collective-permute-start | bytes 208904 | tf_op jit(solution)/shard_map/ppermute | solution.py:366
  40.6 2.6 %collective-permute-done.18 = f32[136,128]{1,0:T(8,128)S(1)} collective-permute-done((f32[136,128]{1,0:T(8,128)S(1)}, f32[136,128]{1,0:T(8,128)S(1)}, u32[]{:S(2)}, u32[]{:S(2)}) %collective-permute-start.18) | collective-permute-done | bytes 69664 | tf_op jit(solution)/shard_map/ppermute | solution.py:366
  43.3 2.3 %collective-permute-start.21 = (f32[136,128]{1,0:T(8,128)S(1)}, f32[136,128]{1,0:T(8,128)S(1)}, u32[]{:S(2)}, u32[]{:S(2)}) collective-permute-start(f32[136,128]{1,0:T(8,128)S(1)} %add.16), channel_id=1, source_target_pairs={{0,12},{2,14},{4,8},{6,10},{8,4},{10,6},{12,0},{14,2},{1,13},{3,15... | collective-permute-start | bytes 208904 | tf_op jit(solution)/shard_map/ppermute | solution.py:366
  45.5 2.2 %collective-permute-start.19 = (f32[136,128]{1,0:T(8,128)S(1)}, f32[136,128]{1,0:T(8,128)S(1)}, u32[]{:S(2)}, u32[]{:S(2)}) collective-permute-start(f32[136,128]{1,0:T(8,128)S(1)} %add.16), channel_id=1, source_target_pairs={{0,4},{2,6},{4,0},{6,2},{8,12},{10,14},{12,8},{14,10},{1,5},{3,7},... | collective-permute-start | bytes 208904 | tf_op jit(solution)/shard_map/ppermute | solution.py:366
  47.7 2.2 %collective-permute-done.21 = f32[136,128]{1,0:T(8,128)S(1)} collective-permute-done((f32[136,128]{1,0:T(8,128)S(1)}, f32[136,128]{1,0:T(8,128)S(1)}, u32[]{:S(2)}, u32[]{:S(2)}) %collective-permute-start.21) | collective-permute-done | bytes 69664 | tf_op jit(solution)/shard_map/ppermute | solution.py:366
  49.9 2.0 %collective-permute-done.20 = f32[136,128]{1,0:T(8,128)S(1)} collective-permute-done((f32[136,128]{1,0:T(8,128)S(1)}, f32[136,128]{1,0:T(8,128)S(1)}, u32[]{:S(2)}, u32[]{:S(2)}) %collective-permute-start.20) | collective-permute-done | bytes 69664 | tf_op jit(solution)/shard_map/ppermute | solution.py:366
  52.1 1.2 %collective-permute-done.22.other = f32[136,128]{1,0:T(8,128)S(1)} collective-permute-done((f32[136,128]{1,0:T(8,128)S(1)}, f32[136,128]{1,0:T(8,128)S(1)}, u32[]{:S(2)}, u32[]{:S(2)}) %collective-permute-start.22) | collective-permute-done | bytes 69664 | tf_op jit(solution)/shard_map/ppermute | solution.py:60
  53.3 41.9 %shard_map.80 = (f32[256,256]{1,0:T(8,128)}, f32[256,256]{1,0:T(8,128)}) custom-call(f32[136,128]{1,0:T(8,128)S(1)} %add_add_fusion.mine, f32[136,128]{1,0:T(8,128)S(1)} %collective-permute-done.22.other, f32[256,256]{1,0:T(8,128)S(1)} %get-tuple-element.53.field), custom_call_target="tpu_custom_call" | custom-call | flops 1024 | bytes 1024 | tf_op jit(solution)/shard_map/pallas_call | solution.py:474
  (44 shorter events, 4.8 us)
Async XLA Ops:
  0.6 15.6 %collective-permute-start.4 = (bf16[32,3,128,256]{3,2,1,0:T(8,128)(2,1)}, bf16[32,3,128,256]{3,2,1,0:T(8,128)(2,1)S(1)}, u32[]{:S(2)}, u32[]{:S(2)}) collective-permute-start(bf16[32,3,128,256]{3,2,1,0:T(8,128)(2,1)} %value.1), channel_id=1, source_target_pairs={{0,1},{1,0},{2,3},{3,2},{4,5},{5,4},{6,7},{7,6},{8,9},{9,8},{10,11... | collective-permute-start | bytes 18874376 | tf_op jit(solution)/shard_map/ppermute | solution.py:60
  1.1 13.0 %copy-start = (bf16[1,256,256]{2,1,0:T(8,128)(2,1)S(1)}, bf16[1,256,256]{2,1,0:T(8,128)(2,1)}, u32[]{:S(2)}) copy-start(bf16[1,256,256]{2,1,0:T(8,128)(2,1)} %param.9) | copy-start | bytes 393220
  1.2 8.9 %collective-permute-start.2 = (bf16[256,256]{1,0:T(8,128)(2,1)}, bf16[256,256]{1,0:T(8,128)(2,1)S(1)}, u32[]{:S(2)}, u32[]{:S(2)}) collective-permute-start(bf16[256,256]{1,0:T(8,128)(2,1)} %bitcast.3), channel_id=1, source_target_pairs={{0,12},{2,6},{4,0},{6,10},{8,4},{10,14},{12,8},{14,2},{1,13},{3,7}... | collective-permute-start | bytes 393224 | tf_op jit(solution)/shard_map/ppermute | solution.py:73
  5.8 8.3 %collective-permute-start.1 = (bf16[256,256]{1,0:T(8,128)(2,1)}, bf16[256,256]{1,0:T(8,128)(2,1)S(1)}, u32[]{:S(2)}, u32[]{:S(2)}) collective-permute-start(bf16[256,256]{1,0:T(8,128)(2,1)} %bitcast.4), channel_id=1, source_target_pairs={{0,2},{2,0},{4,6},{6,4},{8,10},{10,8},{12,14},{14,12},{1,3},{3,1},... | collective-permute-start | bytes 393224 | tf_op jit(solution)/shard_map/ppermute | solution.py:68
  5.8 8.6 %collective-permute-start = (bf16[256,256]{1,0:T(8,128)(2,1)}, bf16[256,256]{1,0:T(8,128)(2,1)S(1)}, u32[]{:S(2)}, u32[]{:S(2)}) collective-permute-start(bf16[256,256]{1,0:T(8,128)(2,1)} %bitcast.5), channel_id=1, source_target_pairs={{0,4},{2,14},{4,8},{6,2},{8,12},{10,6},{12,0},{14,10},{1,5},{3,15}... | collective-permute-start | bytes 393224 | tf_op jit(solution)/shard_map/ppermute | solution.py:73
  10.0 4.4 %collective-permute-start.3 = (bf16[256,256]{1,0:T(8,128)(2,1)S(1)}, bf16[256,256]{1,0:T(8,128)(2,1)S(1)}, u32[]{:S(2)}, u32[]{:S(2)}) collective-permute-start(bf16[256,256]{1,0:T(8,128)(2,1)S(1)} %collective-permute-done.2.rest_1_), channel_id=1, source_target_pairs={{0,1},{1,0},{2,3},{3,2},{4,5},{5,4},{6,7},{7,6},{8,9},{9,8},{10,11... | collective-permute-start | bytes 393224 | tf_op jit(solution)/shard_map/ppermute | solution.py:60
  10.0 6.2 %collective-permute-start.8 = (bf16[256,256]{1,0:T(8,128)(2,1)S(1)}, bf16[256,256]{1,0:T(8,128)(2,1)S(1)}, u32[]{:S(2)}, u32[]{:S(2)}) collective-permute-start(bf16[256,256]{1,0:T(8,128)(2,1)S(1)} %collective-permute-done.2.rest_1_), channel_id=1, source_target_pairs={{0,2},{2,0},{4,6},{6,4},{8,10},{10,8},{12,14},{14,12},{1,3},{3,1},... | collective-permute-start | bytes 393224 | tf_op jit(solution)/shard_map/ppermute | solution.py:68
  14.1 2.1 %collective-permute-start.5 = (bf16[256,256]{1,0:T(8,128)(2,1)S(1)}, bf16[256,256]{1,0:T(8,128)(2,1)S(1)}, u32[]{:S(2)}, u32[]{:S(2)}) collective-permute-start(bf16[256,256]{1,0:T(8,128)(2,1)S(1)} %bitcast.6), channel_id=1, source_target_pairs={{0,1},{1,0},{2,3},{3,2},{4,5},{5,4},{6,7},{7,6},{8,9},{9,8},{10,11... | collective-permute-start | bytes 393224 | tf_op jit(solution)/shard_map/ppermute | solution.py:60
  14.4 1.8 %collective-permute-start.6 = (bf16[256,256]{1,0:T(8,128)(2,1)S(1)}, bf16[256,256]{1,0:T(8,128)(2,1)S(1)}, u32[]{:S(2)}, u32[]{:S(2)}) collective-permute-start(bf16[256,256]{1,0:T(8,128)(2,1)S(1)} %collective-permute-done.rest_2_), channel_id=1, source_target_pairs={{0,1},{1,0},{2,3},{3,2},{4,5},{5,4},{6,7},{7,6},{8,9},{9,8},{10,11... | collective-permute-start | bytes 393224 | tf_op jit(solution)/shard_map/ppermute | solution.py:60
  14.7 1.5 %collective-permute-start.7 = (bf16[256,256]{1,0:T(8,128)(2,1)S(1)}, bf16[256,256]{1,0:T(8,128)(2,1)S(1)}, u32[]{:S(2)}, u32[]{:S(2)}) collective-permute-start(bf16[256,256]{1,0:T(8,128)(2,1)S(1)} %collective-permute-done.1.rest_3_), channel_id=1, source_target_pairs={{0,1},{1,0},{2,3},{3,2},{4,5},{5,4},{6,7},{7,6},{8,9},{9,8},{10,11... | collective-permute-start | bytes 393224 | tf_op jit(solution)/shard_map/ppermute | solution.py:60
  16.2 1.9 %collective-permute-start.9 = (bf16[256,256]{1,0:T(8,128)(2,1)S(1)}, bf16[256,256]{1,0:T(8,128)(2,1)S(1)}, u32[]{:S(2)}, u32[]{:S(2)}) collective-permute-start(bf16[256,256]{1,0:T(8,128)(2,1)S(1)} %collective-permute-done.8.near), channel_id=1, source_target_pairs={{0,1},{1,0},{2,3},{3,2},{4,5},{5,4},{6,7},{7,6},{8,9},{9,8},{10,11... | collective-permute-start | bytes 393224 | tf_op jit(solution)/shard_map/ppermute | solution.py:60
  19.5 1.6 %collective-permute-start.10 = (s16[272,256]{1,0:T(8,128)(2,1)S(1)}, s16[272,256]{1,0:T(8,128)(2,1)S(1)}, u32[]{:S(2)}, u32[]{:S(2)}) collective-permute-start(s16[272,256]{1,0:T(8,128)(2,1)S(1)} %get-tuple-element.37), channel_id=1, source_target_pairs={{0,1},{1,0},{2,3},{3,2},{4,5},{5,4},{6,7},{7,6},{8,9},{9,8},{10,11... | collective-permute-start | bytes 417800 | tf_op jit(solution)/shard_map/ppermute | solution.py:60
  21.2 3.0 %collective-permute-start.11 = (bf16[16,256,128]{2,1,0:T(8,128)(2,1)S(1)}, bf16[16,256,128]{2,1,0:T(8,128)(2,1)S(1)}, u32[]{:S(2)}, u32[]{:S(2)}) collective-permute-start(bf16[16,256,128]{2,1,0:T(8,128)(2,1)S(1)} %get-tuple-element.42.weighted.mine), channel_id=1, source_target_pairs={{0,1},{1,0},{2,3},{3,2},{4,5},{5,4},{6,7},{7,6},{8,9},{9,8},{10,11... | collective-permute-start | bytes 3145736 | tf_op jit(solution)/shard_map/ppermute | solution.py:60
  21.6 2.5 %collective-permute-start.14 = (s16[272,256]{1,0:T(8,128)(2,1)S(1)}, s16[272,256]{1,0:T(8,128)(2,1)S(1)}, u32[]{:S(2)}, u32[]{:S(2)}) collective-permute-start(s16[272,256]{1,0:T(8,128)(2,1)S(1)} %get-tuple-element.49), channel_id=1, source_target_pairs={{0,1},{1,0},{2,3},{3,2},{4,5},{5,4},{6,7},{7,6},{8,9},{9,8},{10,11... | collective-permute-start | bytes 417800 | tf_op jit(solution)/shard_map/ppermute | solution.py:60
  21.8 7.7 %collective-permute-start.12 = (s16[272,256]{1,0:T(8,128)(2,1)S(1)}, s16[272,256]{1,0:T(8,128)(2,1)S(1)}, u32[]{:S(2)}, u32[]{:S(2)}) collective-permute-start(s16[272,256]{1,0:T(8,128)(2,1)S(1)} %shard_map.73), channel_id=1, source_target_pairs={{0,2},{2,0},{4,6},{6,4},{8,10},{10,8},{12,14},{14,12},{1,3},{3,1},... | collective-permute-start | bytes 417800 | tf_op jit(solution)/shard_map/ppermute | solution.py:68
  24.4 9.9 %collective-permute-start.15 = (s16[272,256]{1,0:T(8,128)(2,1)S(1)}, s16[272,256]{1,0:T(8,128)(2,1)S(1)}, u32[]{:S(2)}, u32[]{:S(2)}) collective-permute-start(s16[272,256]{1,0:T(8,128)(2,1)S(1)} %shard_map.78), channel_id=1, source_target_pairs={{0,12},{2,6},{4,0},{6,10},{8,4},{10,14},{12,8},{14,2},{1,13},{3,7}... | collective-permute-start | bytes 417800 | tf_op jit(solution)/shard_map/ppermute | solution.py:73
  29.6 7.5 %collective-permute-start.13 = (s16[272,256]{1,0:T(8,128)(2,1)S(1)}, s16[272,256]{1,0:T(8,128)(2,1)S(1)}, u32[]{:S(2)}, u32[]{:S(2)}) collective-permute-start(s16[272,256]{1,0:T(8,128)(2,1)S(1)} %shard_map.76), channel_id=1, source_target_pairs={{0,4},{2,14},{4,8},{6,2},{8,12},{10,6},{12,0},{14,10},{1,5},{3,15}... | collective-permute-start | bytes 417800 | tf_op jit(solution)/shard_map/ppermute | solution.py:73
  29.7 7.4 %collective-permute-start.16 = (s16[272,256]{1,0:T(8,128)(2,1)S(1)}, s16[272,256]{1,0:T(8,128)(2,1)S(1)}, u32[]{:S(2)}, u32[]{:S(2)}) collective-permute-start(s16[272,256]{1,0:T(8,128)(2,1)S(1)} %get-tuple-element.50), channel_id=1, source_target_pairs={{0,2},{2,0},{4,6},{6,4},{8,10},{10,8},{12,14},{14,12},{1,3},{3,1},... | collective-permute-start | bytes 417800 | tf_op jit(solution)/shard_map/ppermute | solution.py:68
  37.5 1.3 %collective-permute-start.17 = (f32[136,128]{1,0:T(8,128)S(1)}, f32[136,128]{1,0:T(8,128)S(1)}, u32[]{:S(2)}, u32[]{:S(2)}) collective-permute-start(f32[136,128]{1,0:T(8,128)S(1)} %get-tuple-element.52), channel_id=1, source_target_pairs={{0,1},{1,0},{2,3},{3,2},{4,5},{5,4},{6,7},{7,6},{8,9},{9,8},{10,11... | collective-permute-start | bytes 208904 | tf_op jit(solution)/shard_map/ppermute | solution.py:60
  38.9 4.4 %collective-permute-start.18 = (f32[136,128]{1,0:T(8,128)S(1)}, f32[136,128]{1,0:T(8,128)S(1)}, u32[]{:S(2)}, u32[]{:S(2)}) collective-permute-start(f32[136,128]{1,0:T(8,128)S(1)} %add.15), channel_id=1, source_target_pairs={{0,2},{2,0},{4,6},{6,4},{8,10},{10,8},{12,14},{14,12},{1,3},{3,1},... | collective-permute-start | bytes 208904 | tf_op jit(solution)/shard_map/ppermute | solution.py:366
  43.3 6.7 %collective-permute-start.21 = (f32[136,128]{1,0:T(8,128)S(1)}, f32[136,128]{1,0:T(8,128)S(1)}, u32[]{:S(2)}, u32[]{:S(2)}) collective-permute-start(f32[136,128]{1,0:T(8,128)S(1)} %add.16), channel_id=1, source_target_pairs={{0,12},{2,14},{4,8},{6,10},{8,4},{10,6},{12,0},{14,2},{1,13},{3,15... | collective-permute-start | bytes 208904 | tf_op jit(solution)/shard_map/ppermute | solution.py:366
  45.5 6.4 %collective-permute-start.20 = (f32[136,128]{1,0:T(8,128)S(1)}, f32[136,128]{1,0:T(8,128)S(1)}, u32[]{:S(2)}, u32[]{:S(2)}) collective-permute-start(f32[136,128]{1,0:T(8,128)S(1)} %add.16), channel_id=1, source_target_pairs={{0,8},{2,10},{4,12},{6,14},{8,0},{10,2},{12,4},{14,6},{1,9},{3,11}... | collective-permute-start | bytes 208904 | tf_op jit(solution)/shard_map/ppermute | solution.py:366
  45.5 6.4 %collective-permute-start.19 = (f32[136,128]{1,0:T(8,128)S(1)}, f32[136,128]{1,0:T(8,128)S(1)}, u32[]{:S(2)}, u32[]{:S(2)}) collective-permute-start(f32[136,128]{1,0:T(8,128)S(1)} %add.16), channel_id=1, source_target_pairs={{0,4},{2,6},{4,0},{6,2},{8,12},{10,14},{12,8},{14,10},{1,5},{3,7},... | collective-permute-start | bytes 208904 | tf_op jit(solution)/shard_map/ppermute | solution.py:366
  52.0 1.3 %collective-permute-start.22 = (f32[136,128]{1,0:T(8,128)S(1)}, f32[136,128]{1,0:T(8,128)S(1)}, u32[]{:S(2)}, u32[]{:S(2)}) collective-permute-start(f32[136,128]{1,0:T(8,128)S(1)} %add_add_fusion.mine), channel_id=1, source_target_pairs={{0,1},{1,0},{2,3},{3,2},{4,5},{5,4},{6,7},{7,6},{8,9},{9,8},{10,11... | collective-permute-start | bytes 208904 | tf_op jit(solution)/shard_map/ppermute | solution.py:60
  (2 other events, 15.7 us)

commit v9 on v8

--- a/solution.py
+++ b/solution.py
@@ -324,15 +324,19 @@
         inverse[...] = inverse[...] - dot(correction(error), full[0])
         return state[0] + 1, jnp.sum(error * error)
 
+    def write_basis(solved):
+        basis[...] = (dot3(halves(solved), halves(field[...])) * scale).T
+
+    def write_both():
+        solved = inverse[...] * along
+        upper = dot3(halves(solved), halves(matrix)) * (1.0 / scale)
+        factor[...] = jnp.where(row <= column, upper, 0.0)
+        write_basis(solved)
+
     first = refined((0, 0.0))
-    _, left = lax.while_loop(lambda state: (state[0] < REFINED) & (state[1] >= ENOUGH), refined, first)
-    solution_of = inverse[...] * along
-    inverse[...] = solution_of
-    upper = dot3(halves(solution_of), halves(matrix)) * (1.0 / scale)
-    factor[...] = jnp.where(row <= column, upper, 0.0)
-
-    @pl.when(jnp.logical_not(left < ENOUGH))
-    def _():
+    write_both()
+
+    def eliminated():
         inverse[...] = eye
         across = lax.broadcasted_iota(jnp.int32, (1, width), 1)
         down_at = lax.broadcasted_iota(jnp.int32, (width, 1), 0)
@@ -352,9 +356,13 @@
             return 0
 
         lax.fori_loop(0, width, eliminate, 0)
-
-    solved = halves(inverse[...])
-    basis[...] = (dot3(solved, halves(field[...])) * scale).T
+        write_basis(inverse[...])
+
+    @pl.when(jnp.logical_not(first[1] < ENOUGH))
+    def _():
+        _, left = lax.while_loop(lambda state: (state[0] < REFINED) & (state[1] >= ENOUGH), refined, first)
+        pl.when(left < ENOUGH)(write_both)
+        pl.when(jnp.logical_not(left < ENOUGH))(eliminated)
 
 
 def all_reduced(value):

time: 95.4 us -> 95.4 us (level)
  no operation moved by 1% of the time
where the time goes in v9:
time: 95.4 us; the launch traced here: 95.3 us
  Pallas kernels  52.5 us (55%)
  starting transfers between devices  26.5 us (28%)
  waiting for transfers between devices  14.7 us (15%)
  between operations  1.51 us (2%)
    pallas_call x1, Pallas kernels, on_device(): kernel_call(functools.partial(finish_kernel, scale, 2), (jax.ShapeDtypeSt...  41.9 us
    ppermute x4, starting transfers between devices, spread(): lax.ppermute(value, 'tile', [(i, (i + (steps, -steps)[i % 2]) % count) fo...  9.97 us
    ppermute x4, starting transfers between devices, swapped(): lax.ppermute(value, 'tile', [(i, i ^ 1) for i in range(lax.axis_size('til...  7.78 us
    ppermute x4, waiting for transfers between devices, exchanged(): return lax.ppermute(value, 'tile', [(i, i ^ jump) for i in range(count)])  6.9 us
    ppermute x4, starting transfers between devices, exchanged(): return lax.ppermute(value, 'tile', [(i, i ^ jump) for i in range(count)])  6.11 us
    ppermute x11, waiting for transfers between devices, shifted(): return lax.ppermute(value, axis, pairs)  3.33 us
    ppermute x4, waiting for transfers between devices, spread(): lax.ppermute(value, 'tile', [(i, (i + (steps, -steps)[i % 2]) % count) fo...  3.18 us
    pallas_call x1, Pallas kernels, on_device(): kernel_call(stage_kernel, pltpu.VMEM(jacobian.shape, BF16), [HBM], VMEM,...  2.79 us
  transfers between devices with their start and end apart: 23, of which 10 were waited for; matrix products, arithmetic and copies ran while one was open for 0% of the time, Pallas kernels for 9%

profile of v9, /device:TPU:0, one launch (start us, length us, event | category | flops | bytes accessed | tf_op | source)
XLA Modules:
  0.0 95.3 jit_solution(16571338601677208)
XLA Ops:
  1.2 4.7 %collective-permute-start.2 = (bf16[256,256]{1,0:T(8,128)(2,1)}, bf16[256,256]{1,0:T(8,128)(2,1)S(1)}, u32[]{:S(2)}, u32[]{:S(2)}) collective-permute-start(bf16[256,256]{1,0:T(8,128)(2,1)} %bitcast.3), channel_id=1, source_target_pairs={{0,12},{2,6},{4,0},{6,10},{8,4},{10,14},{12,8},{14,2},{1,13},{3,7}... | collective-permute-start | bytes 393224 | tf_op jit(solution)/shard_map/ppermute | solution.py:73
  5.8 1.0 %collective-permute-start = (bf16[256,256]{1,0:T(8,128)(2,1)}, bf16[256,256]{1,0:T(8,128)(2,1)S(1)}, u32[]{:S(2)}, u32[]{:S(2)}) collective-permute-start(bf16[256,256]{1,0:T(8,128)(2,1)} %bitcast.5), channel_id=1, source_target_pairs={{0,4},{2,14},{4,8},{6,2},{8,12},{10,6},{12,0},{14,10},{1,5},{3,15}... | collective-permute-start | bytes 393224 | tf_op jit(solution)/shard_map/ppermute | solution.py:73
  6.9 2.8 %shard_map.68.jac_near.jac = bf16[32,3,128,256]{3,2,1,0:T(8,128)(2,1)S(1)} custom-call(bf16[32,3,128,256]{3,2,1,0:T(8,128)(2,1)} %value.1), custom_call_target="tpu_custom_call" | custom-call | flops 1024 | bytes 1024 | tf_op jit(solution)/shard_map/pallas_call | solution.py:397
  10.0 2.1 %collective-permute-start.8 = (bf16[256,256]{1,0:T(8,128)(2,1)S(1)}, bf16[256,256]{1,0:T(8,128)(2,1)S(1)}, u32[]{:S(2)}, u32[]{:S(2)}) collective-permute-start(bf16[256,256]{1,0:T(8,128)(2,1)S(1)} %collective-permute-done.2.rest_1_), channel_id=1, source_target_pairs={{0,2},{2,0},{4,6},{6,4},{8,10},{10,8},{12,14},{14,12},{1,3},{3,1},... | collective-permute-start | bytes 393224 | tf_op jit(solution)/shard_map/ppermute | solution.py:68
  12.7 1.3 %shard_map.69.table = s32[262]{0:T(512)S(4)} custom-call(s32[3,32]{1,0:T(4,128)S(1)} %bitcast.9, s32[1]{0:T(128)S(6)} %copy.7.live), custom_call_target="tpu_custom_call" | custom-call | flops 1024 | bytes 1024 | tf_op jit(solution)/shard_map/pallas_call | solution.py:405
  14.9 1.3 %collective-permute-done.8.near = bf16[256,256]{1,0:T(8,128)(2,1)S(1)} collective-permute-done((bf16[256,256]{1,0:T(8,128)(2,1)S(1)}, bf16[256,256]{1,0:T(8,128)(2,1)S(1)}, u32[]{:S(2)}, u32[]{:S(2)}) %collective-permute-start.8) | collective-permute-done | bytes 131104 | tf_op jit(solution)/shard_map/ppermute | solution.py:68
  16.3 1.9 %shard_map.70 = (f32[16,128,256]{2,1,0:T(8,128)S(1)}, bf16[16,128,512]{2,1,0:T(8,128)(2,1)S(1)}) custom-call(s32[262]{0:T(512)S(4)} %shard_map.69.table, bf16[32,3,128,256]{3,2,1,0:T(8,128)(2,1)S(1)} %shard_map.68.jac_near.jac, bf16[32,3,128,256]{3,2,1,0:T(8,128)(2,1)S(1)} %collective-permute-done.4.jac_far, bf16[256,256]{1,0:T(8,128)(2,1)S(1)} %bitcast.7, ...), custom_call_target="tpu_custom_call" | custom-call | flops 1024 | bytes 1024 | tf_op jit(solution)/shard_map/pallas_call | solution.py:417
  18.2 1.3 %shard_map.71 = (bf16[16,256,128]{2,1,0:T(8,128)(2,1)S(1)}, f32[256,256]{1,0:T(8,128)S(1)}, s16[272,256]{1,0:T(8,128)(2,1)S(1)}) custom-call(s32[262]{0:T(512)S(4)} %shard_map.69.table, f32[16,128,256]{2,1,0:T(8,128)S(1)} %get-tuple-element.34.images, bf16[16,128,512]{2,1,0:T(8,128)(2,1)S(1)} %get-tuple-element.35.aside, ...), custom_call_target="tpu_custom_call" | custom-call | flops 1024 | bytes 1024 | tf_op jit(solution)/shard_map/pallas_call | solution.py:431
  20.1 0.8 shard_map.72
  21.8 1.8 %collective-permute-start.12 = (s16[272,256]{1,0:T(8,128)(2,1)S(1)}, s16[272,256]{1,0:T(8,128)(2,1)S(1)}, u32[]{:S(2)}, u32[]{:S(2)}) collective-permute-start(s16[272,256]{1,0:T(8,128)(2,1)S(1)} %shard_map.73), channel_id=1, source_target_pairs={{0,2},{2,0},{4,6},{6,4},{8,10},{10,8},{12,14},{14,12},{1,3},{3,1},... | collective-permute-start | bytes 417800 | tf_op jit(solution)/shard_map/ppermute | solution.py:68
  24.4 4.2 %collective-permute-start.15 = (s16[272,256]{1,0:T(8,128)(2,1)S(1)}, s16[272,256]{1,0:T(8,128)(2,1)S(1)}, u32[]{:S(2)}, u32[]{:S(2)}) collective-permute-start(s16[272,256]{1,0:T(8,128)(2,1)S(1)} %shard_map.78), channel_id=1, source_target_pairs={{0,12},{2,6},{4,0},{6,10},{8,4},{10,14},{12,8},{14,2},{1,13},{3,7}... | collective-permute-start | bytes 417800 | tf_op jit(solution)/shard_map/ppermute | solution.py:73
  28.6 1.0 %shard_map.75 = (f32[256,256]{1,0:T(8,128)S(1)}, s16[272,256]{1,0:T(8,128)(2,1)S(1)}) custom-call(s32[262]{0:T(512)S(4)} %shard_map.69.table, bf16[32,3,128,256]{3,2,1,0:T(8,128)(2,1)S(1)} %shard_map.68.jac_near.jac, bf16[33,256,128]{2,1,0:T(8,128)(2,1)S(1)} %shard_map.74.weighted), custom_call_target="tpu_custom_call" | custom-call | flops 1024 | bytes 1024 | tf_op jit(solution)/shard_map/pallas_call | solution.py:459
  29.8 4.0 %collective-permute-start.16 = (s16[272,256]{1,0:T(8,128)(2,1)S(1)}, s16[272,256]{1,0:T(8,128)(2,1)S(1)}, u32[]{:S(2)}, u32[]{:S(2)}) collective-permute-start(s16[272,256]{1,0:T(8,128)(2,1)S(1)} %get-tuple-element.50), channel_id=1, source_target_pairs={{0,2},{2,0},{4,6},{6,4},{8,10},{10,8},{12,14},{14,12},{1,3},{3,1},... | collective-permute-start | bytes 417800 | tf_op jit(solution)/shard_map/ppermute | solution.py:68
  33.7 0.6 shard_map.77.own
  34.4 2.8 %collective-permute-done.13.rest_0_ = s16[272,256]{1,0:T(8,128)(2,1)S(1)} collective-permute-done((s16[272,256]{1,0:T(8,128)(2,1)S(1)}, s16[272,256]{1,0:T(8,128)(2,1)S(1)}, u32[]{:S(2)}, u32[]{:S(2)}) %collective-permute-start.13) | collective-permute-done | bytes 139296 | tf_op jit(solution)/shard_map/ppermute | solution.py:73
  37.7 1.2 %collective-permute-done.17 = f32[136,128]{1,0:T(8,128)S(1)} collective-permute-done((f32[136,128]{1,0:T(8,128)S(1)}, f32[136,128]{1,0:T(8,128)S(1)}, u32[]{:S(2)}, u32[]{:S(2)}) %collective-permute-start.17) | collective-permute-done | bytes 69664 | tf_op jit(solution)/shard_map/ppermute | solution.py:60
  39.0 1.7 %collective-permute-start.18 = (f32[136,128]{1,0:T(8,128)S(1)}, f32[136,128]{1,0:T(8,128)S(1)}, u32[]{:S(2)}, u32[]{:S(2)}) collective-permute-start(f32[136,128]{1,0:T(8,128)S(1)} %add.15), channel_id=1, source_target_pairs={{0,2},{2,0},{4,6},{6,4},{8,10},{10,8},{12,14},{14,12},{1,3},{3,1},... | collective-permute-start | bytes 208904 | tf_op jit(solution)/shard_map/ppermute | solution.py:374
  40.6 2.7 %collective-permute-done.18 = f32[136,128]{1,0:T(8,128)S(1)} collective-permute-done((f32[136,128]{1,0:T(8,128)S(1)}, f32[136,128]{1,0:T(8,128)S(1)}, u32[]{:S(2)}, u32[]{:S(2)}) %collective-permute-start.18) | collective-permute-done | bytes 69664 | tf_op jit(solution)/shard_map/ppermute | solution.py:374
  43.3 2.2 %collective-permute-start.21 = (f32[136,128]{1,0:T(8,128)S(1)}, f32[136,128]{1,0:T(8,128)S(1)}, u32[]{:S(2)}, u32[]{:S(2)}) collective-permute-start(f32[136,128]{1,0:T(8,128)S(1)} %add.16), channel_id=1, source_target_pairs={{0,12},{2,14},{4,8},{6,10},{8,4},{10,6},{12,0},{14,2},{1,13},{3,15... | collective-permute-start | bytes 208904 | tf_op jit(solution)/shard_map/ppermute | solution.py:374
  45.5 2.3 %collective-permute-start.19 = (f32[136,128]{1,0:T(8,128)S(1)}, f32[136,128]{1,0:T(8,128)S(1)}, u32[]{:S(2)}, u32[]{:S(2)}) collective-permute-start(f32[136,128]{1,0:T(8,128)S(1)} %add.16), channel_id=1, source_target_pairs={{0,4},{2,6},{4,0},{6,2},{8,12},{10,14},{12,8},{14,10},{1,5},{3,7},... | collective-permute-start | bytes 208904 | tf_op jit(solution)/shard_map/ppermute | solution.py:374
  47.8 2.3 %collective-permute-done.21 = f32[136,128]{1,0:T(8,128)S(1)} collective-permute-done((f32[136,128]{1,0:T(8,128)S(1)}, f32[136,128]{1,0:T(8,128)S(1)}, u32[]{:S(2)}, u32[]{:S(2)}) %collective-permute-start.21) | collective-permute-done | bytes 69664 | tf_op jit(solution)/shard_map/ppermute | solution.py:374
  50.1 1.9 %collective-permute-done.20 = f32[136,128]{1,0:T(8,128)S(1)} collective-permute-done((f32[136,128]{1,0:T(8,128)S(1)}, f32[136,128]{1,0:T(8,128)S(1)}, u32[]{:S(2)}, u32[]{:S(2)}) %collective-permute-start.20) | collective-permute-done | bytes 69664 | tf_op jit(solution)/shard_map/ppermute | solution.py:374
  52.1 1.2 %collective-permute-done.22.other = f32[136,128]{1,0:T(8,128)S(1)} collective-permute-done((f32[136,128]{1,0:T(8,128)S(1)}, f32[136,128]{1,0:T(8,128)S(1)}, u32[]{:S(2)}, u32[]{:S(2)}) %collective-permute-start.22) | collective-permute-done | bytes 69664 | tf_op jit(solution)/shard_map/ppermute | solution.py:60
  53.3 41.9 %shard_map.80 = (f32[256,256]{1,0:T(8,128)}, f32[256,256]{1,0:T(8,128)}) custom-call(f32[136,128]{1,0:T(8,128)S(1)} %add_add_fusion.mine, f32[136,128]{1,0:T(8,128)S(1)} %collective-permute-done.22.other, f32[256,256]{1,0:T(8,128)S(1)} %get-tuple-element.53.field), custom_call_target="tpu_custom_call" | custom-call | flops 1024 | bytes 1024 | tf_op jit(solution)/shard_map/pallas_call | solution.py:482
  (44 shorter events, 4.8 us)
Async XLA Ops:
  0.6 15.6 %collective-permute-start.4 = (bf16[32,3,128,256]{3,2,1,0:T(8,128)(2,1)}, bf16[32,3,128,256]{3,2,1,0:T(8,128)(2,1)S(1)}, u32[]{:S(2)}, u32[]{:S(2)}) collective-permute-start(bf16[32,3,128,256]{3,2,1,0:T(8,128)(2,1)} %value.1), channel_id=1, source_target_pairs={{0,1},{1,0},{2,3},{3,2},{4,5},{5,4},{6,7},{7,6},{8,9},{9,8},{10,11... | collective-permute-start | bytes 18874376 | tf_op jit(solution)/shard_map/ppermute | solution.py:60
  1.1 13.0 %copy-start = (bf16[1,256,256]{2,1,0:T(8,128)(2,1)S(1)}, bf16[1,256,256]{2,1,0:T(8,128)(2,1)}, u32[]{:S(2)}) copy-start(bf16[1,256,256]{2,1,0:T(8,128)(2,1)} %param.9) | copy-start | bytes 393220
  1.2 8.9 %collective-permute-start.2 = (bf16[256,256]{1,0:T(8,128)(2,1)}, bf16[256,256]{1,0:T(8,128)(2,1)S(1)}, u32[]{:S(2)}, u32[]{:S(2)}) collective-permute-start(bf16[256,256]{1,0:T(8,128)(2,1)} %bitcast.3), channel_id=1, source_target_pairs={{0,12},{2,6},{4,0},{6,10},{8,4},{10,14},{12,8},{14,2},{1,13},{3,7}... | collective-permute-start | bytes 393224 | tf_op jit(solution)/shard_map/ppermute | solution.py:73
  5.8 8.3 %collective-permute-start.1 = (bf16[256,256]{1,0:T(8,128)(2,1)}, bf16[256,256]{1,0:T(8,128)(2,1)S(1)}, u32[]{:S(2)}, u32[]{:S(2)}) collective-permute-start(bf16[256,256]{1,0:T(8,128)(2,1)} %bitcast.4), channel_id=1, source_target_pairs={{0,2},{2,0},{4,6},{6,4},{8,10},{10,8},{12,14},{14,12},{1,3},{3,1},... | collective-permute-start | bytes 393224 | tf_op jit(solution)/shard_map/ppermute | solution.py:68
  5.8 8.6 %collective-permute-start = (bf16[256,256]{1,0:T(8,128)(2,1)}, bf16[256,256]{1,0:T(8,128)(2,1)S(1)}, u32[]{:S(2)}, u32[]{:S(2)}) collective-permute-start(bf16[256,256]{1,0:T(8,128)(2,1)} %bitcast.5), channel_id=1, source_target_pairs={{0,4},{2,14},{4,8},{6,2},{8,12},{10,6},{12,0},{14,10},{1,5},{3,15}... | collective-permute-start | bytes 393224 | tf_op jit(solution)/shard_map/ppermute | solution.py:73
  10.0 4.4 %collective-permute-start.3 = (bf16[256,256]{1,0:T(8,128)(2,1)S(1)}, bf16[256,256]{1,0:T(8,128)(2,1)S(1)}, u32[]{:S(2)}, u32[]{:S(2)}) collective-permute-start(bf16[256,256]{1,0:T(8,128)(2,1)S(1)} %collective-permute-done.2.rest_1_), channel_id=1, source_target_pairs={{0,1},{1,0},{2,3},{3,2},{4,5},{5,4},{6,7},{7,6},{8,9},{9,8},{10,11... | collective-permute-start | bytes 393224 | tf_op jit(solution)/shard_map/ppermute | solution.py:60
  10.0 6.2 %collective-permute-start.8 = (bf16[256,256]{1,0:T(8,128)(2,1)S(1)}, bf16[256,256]{1,0:T(8,128)(2,1)S(1)}, u32[]{:S(2)}, u32[]{:S(2)}) collective-permute-start(bf16[256,256]{1,0:T(8,128)(2,1)S(1)} %collective-permute-done.2.rest_1_), channel_id=1, source_target_pairs={{0,2},{2,0},{4,6},{6,4},{8,10},{10,8},{12,14},{14,12},{1,3},{3,1},... | collective-permute-start | bytes 393224 | tf_op jit(solution)/shard_map/ppermute | solution.py:68
  14.1 2.1 %collective-permute-start.5 = (bf16[256,256]{1,0:T(8,128)(2,1)S(1)}, bf16[256,256]{1,0:T(8,128)(2,1)S(1)}, u32[]{:S(2)}, u32[]{:S(2)}) collective-permute-start(bf16[256,256]{1,0:T(8,128)(2,1)S(1)} %bitcast.6), channel_id=1, source_target_pairs={{0,1},{1,0},{2,3},{3,2},{4,5},{5,4},{6,7},{7,6},{8,9},{9,8},{10,11... | collective-permute-start | bytes 393224 | tf_op jit(solution)/shard_map/ppermute | solution.py:60
  14.4 1.8 %collective-permute-start.6 = (bf16[256,256]{1,0:T(8,128)(2,1)S(1)}, bf16[256,256]{1,0:T(8,128)(2,1)S(1)}, u32[]{:S(2)}, u32[]{:S(2)}) collective-permute-start(bf16[256,256]{1,0:T(8,128)(2,1)S(1)} %collective-permute-done.rest_2_), channel_id=1, source_target_pairs={{0,1},{1,0},{2,3},{3,2},{4,5},{5,4},{6,7},{7,6},{8,9},{9,8},{10,11... | collective-permute-start | bytes 393224 | tf_op jit(solution)/shard_map/ppermute | solution.py:60
  14.7 1.5 %collective-permute-start.7 = (bf16[256,256]{1,0:T(8,128)(2,1)S(1)}, bf16[256,256]{1,0:T(8,128)(2,1)S(1)}, u32[]{:S(2)}, u32[]{:S(2)}) collective-permute-start(bf16[256,256]{1,0:T(8,128)(2,1)S(1)} %collective-permute-done.1.rest_3_), channel_id=1, source_target_pairs={{0,1},{1,0},{2,3},{3,2},{4,5},{5,4},{6,7},{7,6},{8,9},{9,8},{10,11... | collective-permute-start | bytes 393224 | tf_op jit(solution)/shard_map/ppermute | solution.py:60
  16.2 1.9 %collective-permute-start.9 = (bf16[256,256]{1,0:T(8,128)(2,1)S(1)}, bf16[256,256]{1,0:T(8,128)(2,1)S(1)}, u32[]{:S(2)}, u32[]{:S(2)}) collective-permute-start(bf16[256,256]{1,0:T(8,128)(2,1)S(1)} %collective-permute-done.8.near), channel_id=1, source_target_pairs={{0,1},{1,0},{2,3},{3,2},{4,5},{5,4},{6,7},{7,6},{8,9},{9,8},{10,11... | collective-permute-start | bytes 393224 | tf_op jit(solution)/shard_map/ppermute | solution.py:60
  19.5 1.6 %collective-permute-start.10 = (s16[272,256]{1,0:T(8,128)(2,1)S(1)}, s16[272,256]{1,0:T(8,128)(2,1)S(1)}, u32[]{:S(2)}, u32[]{:S(2)}) collective-permute-start(s16[272,256]{1,0:T(8,128)(2,1)S(1)} %get-tuple-element.37), channel_id=1, source_target_pairs={{0,1},{1,0},{2,3},{3,2},{4,5},{5,4},{6,7},{7,6},{8,9},{9,8},{10,11... | collective-permute-start | bytes 417800 | tf_op jit(solution)/shard_map/ppermute | solution.py:60
  21.2 3.0 %collective-permute-start.11 = (bf16[16,256,128]{2,1,0:T(8,128)(2,1)S(1)}, bf16[16,256,128]{2,1,0:T(8,128)(2,1)S(1)}, u32[]{:S(2)}, u32[]{:S(2)}) collective-permute-start(bf16[16,256,128]{2,1,0:T(8,128)(2,1)S(1)} %get-tuple-element.42.weighted.mine), channel_id=1, source_target_pairs={{0,1},{1,0},{2,3},{3,2},{4,5},{5,4},{6,7},{7,6},{8,9},{9,8},{10,11... | collective-permute-start | bytes 3145736 | tf_op jit(solution)/shard_map/ppermute | solution.py:60
  21.6 2.5 %collective-permute-start.14 = (s16[272,256]{1,0:T(8,128)(2,1)S(1)}, s16[272,256]{1,0:T(8,128)(2,1)S(1)}, u32[]{:S(2)}, u32[]{:S(2)}) collective-permute-start(s16[272,256]{1,0:T(8,128)(2,1)S(1)} %get-tuple-element.49), channel_id=1, source_target_pairs={{0,1},{1,0},{2,3},{3,2},{4,5},{5,4},{6,7},{7,6},{8,9},{9,8},{10,11... | collective-permute-start | bytes 417800 | tf_op jit(solution)/shard_map/ppermute | solution.py:60
  21.8 7.8 %collective-permute-start.12 = (s16[272,256]{1,0:T(8,128)(2,1)S(1)}, s16[272,256]{1,0:T(8,128)(2,1)S(1)}, u32[]{:S(2)}, u32[]{:S(2)}) collective-permute-start(s16[272,256]{1,0:T(8,128)(2,1)S(1)} %shard_map.73), channel_id=1, source_target_pairs={{0,2},{2,0},{4,6},{6,4},{8,10},{10,8},{12,14},{14,12},{1,3},{3,1},... | collective-permute-start | bytes 417800 | tf_op jit(solution)/shard_map/ppermute | solution.py:68
  24.4 9.9 %collective-permute-start.15 = (s16[272,256]{1,0:T(8,128)(2,1)S(1)}, s16[272,256]{1,0:T(8,128)(2,1)S(1)}, u32[]{:S(2)}, u32[]{:S(2)}) collective-permute-start(s16[272,256]{1,0:T(8,128)(2,1)S(1)} %shard_map.78), channel_id=1, source_target_pairs={{0,12},{2,6},{4,0},{6,10},{8,4},{10,14},{12,8},{14,2},{1,13},{3,7}... | collective-permute-start | bytes 417800 | tf_op jit(solution)/shard_map/ppermute | solution.py:73
  29.7 7.5 %collective-permute-start.13 = (s16[272,256]{1,0:T(8,128)(2,1)S(1)}, s16[272,256]{1,0:T(8,128)(2,1)S(1)}, u32[]{:S(2)}, u32[]{:S(2)}) collective-permute-start(s16[272,256]{1,0:T(8,128)(2,1)S(1)} %shard_map.76), channel_id=1, source_target_pairs={{0,4},{2,14},{4,8},{6,2},{8,12},{10,6},{12,0},{14,10},{1,5},{3,15}... | collective-permute-start | bytes 417800 | tf_op jit(solution)/shard_map/ppermute | solution.py:73
  29.8 7.4 %collective-permute-start.16 = (s16[272,256]{1,0:T(8,128)(2,1)S(1)}, s16[272,256]{1,0:T(8,128)(2,1)S(1)}, u32[]{:S(2)}, u32[]{:S(2)}) collective-permute-start(s16[272,256]{1,0:T(8,128)(2,1)S(1)} %get-tuple-element.50), channel_id=1, source_target_pairs={{0,2},{2,0},{4,6},{6,4},{8,10},{10,8},{12,14},{14,12},{1,3},{3,1},... | collective-permute-start | bytes 417800 | tf_op jit(solution)/shard_map/ppermute | solution.py:68
  37.6 1.3 %collective-permute-start.17 = (f32[136,128]{1,0:T(8,128)S(1)}, f32[136,128]{1,0:T(8,128)S(1)}, u32[]{:S(2)}, u32[]{:S(2)}) collective-permute-start(f32[136,128]{1,0:T(8,128)S(1)} %get-tuple-element.52), channel_id=1, source_target_pairs={{0,1},{1,0},{2,3},{3,2},{4,5},{5,4},{6,7},{7,6},{8,9},{9,8},{10,11... | collective-permute-start | bytes 208904 | tf_op jit(solution)/shard_map/ppermute | solution.py:60
  39.0 4.4 %collective-permute-start.18 = (f32[136,128]{1,0:T(8,128)S(1)}, f32[136,128]{1,0:T(8,128)S(1)}, u32[]{:S(2)}, u32[]{:S(2)}) collective-permute-start(f32[136,128]{1,0:T(8,128)S(1)} %add.15), channel_id=1, source_target_pairs={{0,2},{2,0},{4,6},{6,4},{8,10},{10,8},{12,14},{14,12},{1,3},{3,1},... | collective-permute-start | bytes 208904 | tf_op jit(solution)/shard_map/ppermute | solution.py:374
  43.3 6.8 %collective-permute-start.21 = (f32[136,128]{1,0:T(8,128)S(1)}, f32[136,128]{1,0:T(8,128)S(1)}, u32[]{:S(2)}, u32[]{:S(2)}) collective-permute-start(f32[136,128]{1,0:T(8,128)S(1)} %add.16), channel_id=1, source_target_pairs={{0,12},{2,14},{4,8},{6,10},{8,4},{10,6},{12,0},{14,2},{1,13},{3,15... | collective-permute-start | bytes 208904 | tf_op jit(solution)/shard_map/ppermute | solution.py:374
  45.5 6.4 %collective-permute-start.20 = (f32[136,128]{1,0:T(8,128)S(1)}, f32[136,128]{1,0:T(8,128)S(1)}, u32[]{:S(2)}, u32[]{:S(2)}) collective-permute-start(f32[136,128]{1,0:T(8,128)S(1)} %add.16), channel_id=1, source_target_pairs={{0,8},{2,10},{4,12},{6,14},{8,0},{10,2},{12,4},{14,6},{1,9},{3,11}... | collective-permute-start | bytes 208904 | tf_op jit(solution)/shard_map/ppermute | solution.py:374
  45.5 6.4 %collective-permute-start.19 = (f32[136,128]{1,0:T(8,128)S(1)}, f32[136,128]{1,0:T(8,128)S(1)}, u32[]{:S(2)}, u32[]{:S(2)}) collective-permute-start(f32[136,128]{1,0:T(8,128)S(1)} %add.16), channel_id=1, source_target_pairs={{0,4},{2,6},{4,0},{6,2},{8,12},{10,14},{12,8},{14,10},{1,5},{3,7},... | collective-permute-start | bytes 208904 | tf_op jit(solution)/shard_map/ppermute | solution.py:374
  52.0 1.3 %collective-permute-start.22 = (f32[136,128]{1,0:T(8,128)S(1)}, f32[136,128]{1,0:T(8,128)S(1)}, u32[]{:S(2)}, u32[]{:S(2)}) collective-permute-start(f32[136,128]{1,0:T(8,128)S(1)} %add_add_fusion.mine), channel_id=1, source_target_pairs={{0,1},{1,0},{2,3},{3,2},{4,5},{5,4},{6,7},{7,6},{8,9},{9,8},{10,11... | collective-permute-start | bytes 208904 | tf_op jit(solution)/shard_map/ppermute | solution.py:60
  (2 other events, 15.7 us)

commit v10 on v9

--- a/solution.py
+++ b/solution.py
@@ -154,7 +154,7 @@
         out[half + j] = other[j]
         return 0
 
-    lax.fori_loop(0, half, step, 0)
+    lax.fori_loop(0, half, step, 0, unroll=8)
     out[2 * half] = jnp.zeros(out.shape[1:], BF16)
 
 

time: 95.4 us -> 95.4 us (level)
  no operation moved by 1% of the time
where the time goes in v10:
time: 95.4 us; the launch traced here: 95.2 us
  Pallas kernels  52.6 us (55%)
  starting transfers between devices  26.4 us (28%)
  waiting for transfers between devices  14.7 us (15%)
  between operations  1.51 us (2%)
    pallas_call x1, Pallas kernels, on_device(): kernel_call(functools.partial(finish_kernel, scale, 2), (jax.ShapeDtypeSt...  41.9 us
    ppermute x4, starting transfers between devices, spread(): lax.ppermute(value, 'tile', [(i, (i + (steps, -steps)[i % 2]) % count) fo...  9.97 us
    ppermute x4, starting transfers between devices, swapped(): lax.ppermute(value, 'tile', [(i, i ^ 1) for i in range(lax.axis_size('til...  7.73 us
    ppermute x4, waiting for transfers between devices, exchanged(): return lax.ppermute(value, 'tile', [(i, i ^ jump) for i in range(count)])  6.88 us
    ppermute x4, starting transfers between devices, exchanged(): return lax.ppermute(value, 'tile', [(i, i ^ jump) for i in range(count)])  6.07 us
    ppermute x11, waiting for transfers between devices, shifted(): return lax.ppermute(value, axis, pairs)  3.33 us
    ppermute x4, waiting for transfers between devices, spread(): lax.ppermute(value, 'tile', [(i, (i + (steps, -steps)[i % 2]) % count) fo...  3.16 us
    pallas_call x1, Pallas kernels, on_device(): kernel_call(stage_kernel, pltpu.VMEM(jacobian.shape, BF16), [HBM], VMEM,...  2.79 us
  transfers between devices with their start and end apart: 23, of which 10 were waited for; matrix products, arithmetic and copies ran while one was open for 0% of the time, Pallas kernels for 9%

profile of v10, /device:TPU:0, one launch (start us, length us, event | category | flops | bytes accessed | tf_op | source)
XLA Modules:
  0.0 95.2 jit_solution(5214323051264654517)
XLA Ops:
  1.2 4.7 %collective-permute-start.2 = (bf16[256,256]{1,0:T(8,128)(2,1)}, bf16[256,256]{1,0:T(8,128)(2,1)S(1)}, u32[]{:S(2)}, u32[]{:S(2)}) collective-permute-start(bf16[256,256]{1,0:T(8,128)(2,1)} %bitcast.3), channel_id=1, source_target_pairs={{0,12},{2,6},{4,0},{6,10},{8,4},{10,14},{12,8},{14,2},{1,13},{3,7}... | collective-permute-start | bytes 393224 | tf_op jit(solution)/shard_map/ppermute | solution.py:73
  5.8 1.0 %collective-permute-start = (bf16[256,256]{1,0:T(8,128)(2,1)}, bf16[256,256]{1,0:T(8,128)(2,1)S(1)}, u32[]{:S(2)}, u32[]{:S(2)}) collective-permute-start(bf16[256,256]{1,0:T(8,128)(2,1)} %bitcast.5), channel_id=1, source_target_pairs={{0,4},{2,14},{4,8},{6,2},{8,12},{10,6},{12,0},{14,10},{1,5},{3,15}... | collective-permute-start | bytes 393224 | tf_op jit(solution)/shard_map/ppermute | solution.py:73
  6.9 2.8 %shard_map.68.jac_near.jac = bf16[32,3,128,256]{3,2,1,0:T(8,128)(2,1)S(1)} custom-call(bf16[32,3,128,256]{3,2,1,0:T(8,128)(2,1)} %value.1), custom_call_target="tpu_custom_call" | custom-call | flops 1024 | bytes 1024 | tf_op jit(solution)/shard_map/pallas_call | solution.py:397
  10.0 2.1 %collective-permute-start.8 = (bf16[256,256]{1,0:T(8,128)(2,1)S(1)}, bf16[256,256]{1,0:T(8,128)(2,1)S(1)}, u32[]{:S(2)}, u32[]{:S(2)}) collective-permute-start(bf16[256,256]{1,0:T(8,128)(2,1)S(1)} %collective-permute-done.2.rest_1_), channel_id=1, source_target_pairs={{0,2},{2,0},{4,6},{6,4},{8,10},{10,8},{12,14},{14,12},{1,3},{3,1},... | collective-permute-start | bytes 393224 | tf_op jit(solution)/shard_map/ppermute | solution.py:68
  12.7 1.3 %shard_map.69.table = s32[262]{0:T(512)S(4)} custom-call(s32[3,32]{1,0:T(4,128)S(1)} %bitcast.9, s32[1]{0:T(128)S(6)} %copy.7.live), custom_call_target="tpu_custom_call" | custom-call | flops 1024 | bytes 1024 | tf_op jit(solution)/shard_map/pallas_call | solution.py:405
  14.9 1.3 %collective-permute-done.8.near = bf16[256,256]{1,0:T(8,128)(2,1)S(1)} collective-permute-done((bf16[256,256]{1,0:T(8,128)(2,1)S(1)}, bf16[256,256]{1,0:T(8,128)(2,1)S(1)}, u32[]{:S(2)}, u32[]{:S(2)}) %collective-permute-start.8) | collective-permute-done | bytes 131104 | tf_op jit(solution)/shard_map/ppermute | solution.py:68
  16.3 1.9 %shard_map.70 = (f32[16,128,256]{2,1,0:T(8,128)S(1)}, bf16[16,128,512]{2,1,0:T(8,128)(2,1)S(1)}) custom-call(s32[262]{0:T(512)S(4)} %shard_map.69.table, bf16[32,3,128,256]{3,2,1,0:T(8,128)(2,1)S(1)} %shard_map.68.jac_near.jac, bf16[32,3,128,256]{3,2,1,0:T(8,128)(2,1)S(1)} %collective-permute-done.4.jac_far, bf16[256,256]{1,0:T(8,128)(2,1)S(1)} %bitcast.7, ...), custom_call_target="tpu_custom_call" | custom-call | flops 1024 | bytes 1024 | tf_op jit(solution)/shard_map/pallas_call | solution.py:417
  18.2 1.3 %shard_map.71 = (bf16[16,256,128]{2,1,0:T(8,128)(2,1)S(1)}, f32[256,256]{1,0:T(8,128)S(1)}, s16[272,256]{1,0:T(8,128)(2,1)S(1)}) custom-call(s32[262]{0:T(512)S(4)} %shard_map.69.table, f32[16,128,256]{2,1,0:T(8,128)S(1)} %get-tuple-element.34.images, bf16[16,128,512]{2,1,0:T(8,128)(2,1)S(1)} %get-tuple-element.35.aside, ...), custom_call_target="tpu_custom_call" | custom-call | flops 1024 | bytes 1024 | tf_op jit(solution)/shard_map/pallas_call | solution.py:431
  20.1 0.8 shard_map.72
  21.8 1.8 %collective-permute-start.12 = (s16[272,256]{1,0:T(8,128)(2,1)S(1)}, s16[272,256]{1,0:T(8,128)(2,1)S(1)}, u32[]{:S(2)}, u32[]{:S(2)}) collective-permute-start(s16[272,256]{1,0:T(8,128)(2,1)S(1)} %shard_map.73), channel_id=1, source_target_pairs={{0,2},{2,0},{4,6},{6,4},{8,10},{10,8},{12,14},{14,12},{1,3},{3,1},... | collective-permute-start | bytes 417800 | tf_op jit(solution)/shard_map/ppermute | solution.py:68
  24.4 4.2 %collective-permute-start.15 = (s16[272,256]{1,0:T(8,128)(2,1)S(1)}, s16[272,256]{1,0:T(8,128)(2,1)S(1)}, u32[]{:S(2)}, u32[]{:S(2)}) collective-permute-start(s16[272,256]{1,0:T(8,128)(2,1)S(1)} %shard_map.78), channel_id=1, source_target_pairs={{0,12},{2,6},{4,0},{6,10},{8,4},{10,14},{12,8},{14,2},{1,13},{3,7}... | collective-permute-start | bytes 417800 | tf_op jit(solution)/shard_map/ppermute | solution.py:73
  28.6 1.0 %shard_map.75 = (f32[256,256]{1,0:T(8,128)S(1)}, s16[272,256]{1,0:T(8,128)(2,1)S(1)}) custom-call(s32[262]{0:T(512)S(4)} %shard_map.69.table, bf16[32,3,128,256]{3,2,1,0:T(8,128)(2,1)S(1)} %shard_map.68.jac_near.jac, bf16[33,256,128]{2,1,0:T(8,128)(2,1)S(1)} %shard_map.74.weighted), custom_call_target="tpu_custom_call" | custom-call | flops 1024 | bytes 1024 | tf_op jit(solution)/shard_map/pallas_call | solution.py:459
  29.8 3.9 %collective-permute-start.16 = (s16[272,256]{1,0:T(8,128)(2,1)S(1)}, s16[272,256]{1,0:T(8,128)(2,1)S(1)}, u32[]{:S(2)}, u32[]{:S(2)}) collective-permute-start(s16[272,256]{1,0:T(8,128)(2,1)S(1)} %get-tuple-element.50), channel_id=1, source_target_pairs={{0,2},{2,0},{4,6},{6,4},{8,10},{10,8},{12,14},{14,12},{1,3},{3,1},... | collective-permute-start | bytes 417800 | tf_op jit(solution)/shard_map/ppermute | solution.py:68
  33.7 0.7 shard_map.77.own
  34.4 2.8 %collective-permute-done.13.rest_0_ = s16[272,256]{1,0:T(8,128)(2,1)S(1)} collective-permute-done((s16[272,256]{1,0:T(8,128)(2,1)S(1)}, s16[272,256]{1,0:T(8,128)(2,1)S(1)}, u32[]{:S(2)}, u32[]{:S(2)}) %collective-permute-start.13) | collective-permute-done | bytes 139296 | tf_op jit(solution)/shard_map/ppermute | solution.py:73
  37.7 1.2 %collective-permute-done.17 = f32[136,128]{1,0:T(8,128)S(1)} collective-permute-done((f32[136,128]{1,0:T(8,128)S(1)}, f32[136,128]{1,0:T(8,128)S(1)}, u32[]{:S(2)}, u32[]{:S(2)}) %collective-permute-start.17) | collective-permute-done | bytes 69664 | tf_op jit(solution)/shard_map/ppermute | solution.py:60
  39.0 1.6 %collective-permute-start.18 = (f32[136,128]{1,0:T(8,128)S(1)}, f32[136,128]{1,0:T(8,128)S(1)}, u32[]{:S(2)}, u32[]{:S(2)}) collective-permute-start(f32[136,128]{1,0:T(8,128)S(1)} %add.15), channel_id=1, source_target_pairs={{0,2},{2,0},{4,6},{6,4},{8,10},{10,8},{12,14},{14,12},{1,3},{3,1},... | collective-permute-start | bytes 208904 | tf_op jit(solution)/shard_map/ppermute | solution.py:374
  40.6 2.8 %collective-permute-done.18 = f32[136,128]{1,0:T(8,128)S(1)} collective-permute-done((f32[136,128]{1,0:T(8,128)S(1)}, f32[136,128]{1,0:T(8,128)S(1)}, u32[]{:S(2)}, u32[]{:S(2)}) %collective-permute-start.18) | collective-permute-done | bytes 69664 | tf_op jit(solution)/shard_map/ppermute | solution.py:374
  43.4 2.1 %collective-permute-start.21 = (f32[136,128]{1,0:T(8,128)S(1)}, f32[136,128]{1,0:T(8,128)S(1)}, u32[]{:S(2)}, u32[]{:S(2)}) collective-permute-start(f32[136,128]{1,0:T(8,128)S(1)} %add.16), channel_id=1, source_target_pairs={{0,12},{2,14},{4,8},{6,10},{8,4},{10,6},{12,0},{14,2},{1,13},{3,15... | collective-permute-start | bytes 208904 | tf_op jit(solution)/shard_map/ppermute | solution.py:374
  45.5 2.3 %collective-permute-start.19 = (f32[136,128]{1,0:T(8,128)S(1)}, f32[136,128]{1,0:T(8,128)S(1)}, u32[]{:S(2)}, u32[]{:S(2)}) collective-permute-start(f32[136,128]{1,0:T(8,128)S(1)} %add.16), channel_id=1, source_target_pairs={{0,4},{2,6},{4,0},{6,2},{8,12},{10,14},{12,8},{14,10},{1,5},{3,7},... | collective-permute-start | bytes 208904 | tf_op jit(solution)/shard_map/ppermute | solution.py:374
  47.8 2.4 %collective-permute-done.21 = f32[136,128]{1,0:T(8,128)S(1)} collective-permute-done((f32[136,128]{1,0:T(8,128)S(1)}, f32[136,128]{1,0:T(8,128)S(1)}, u32[]{:S(2)}, u32[]{:S(2)}) %collective-permute-start.21) | collective-permute-done | bytes 69664 | tf_op jit(solution)/shard_map/ppermute | solution.py:374
  50.2 1.8 %collective-permute-done.20 = f32[136,128]{1,0:T(8,128)S(1)} collective-permute-done((f32[136,128]{1,0:T(8,128)S(1)}, f32[136,128]{1,0:T(8,128)S(1)}, u32[]{:S(2)}, u32[]{:S(2)}) %collective-permute-start.20) | collective-permute-done | bytes 69664 | tf_op jit(solution)/shard_map/ppermute | solution.py:374
  52.1 1.2 %collective-permute-done.22.other = f32[136,128]{1,0:T(8,128)S(1)} collective-permute-done((f32[136,128]{1,0:T(8,128)S(1)}, f32[136,128]{1,0:T(8,128)S(1)}, u32[]{:S(2)}, u32[]{:S(2)}) %collective-permute-start.22) | collective-permute-done | bytes 69664 | tf_op jit(solution)/shard_map/ppermute | solution.py:60
  53.3 41.9 %shard_map.80 = (f32[256,256]{1,0:T(8,128)}, f32[256,256]{1,0:T(8,128)}) custom-call(f32[136,128]{1,0:T(8,128)S(1)} %add_add_fusion.mine, f32[136,128]{1,0:T(8,128)S(1)} %collective-permute-done.22.other, f32[256,256]{1,0:T(8,128)S(1)} %get-tuple-element.53.field), custom_call_target="tpu_custom_call" | custom-call | flops 1024 | bytes 1024 | tf_op jit(solution)/shard_map/pallas_call | solution.py:482
  (44 shorter events, 4.8 us)
Async XLA Ops:
  0.6 15.6 %collective-permute-start.4 = (bf16[32,3,128,256]{3,2,1,0:T(8,128)(2,1)}, bf16[32,3,128,256]{3,2,1,0:T(8,128)(2,1)S(1)}, u32[]{:S(2)}, u32[]{:S(2)}) collective-permute-start(bf16[32,3,128,256]{3,2,1,0:T(8,128)(2,1)} %value.1), channel_id=1, source_target_pairs={{0,1},{1,0},{2,3},{3,2},{4,5},{5,4},{6,7},{7,6},{8,9},{9,8},{10,11... | collective-permute-start | bytes 18874376 | tf_op jit(solution)/shard_map/ppermute | solution.py:60
  1.1 13.0 %copy-start = (bf16[1,256,256]{2,1,0:T(8,128)(2,1)S(1)}, bf16[1,256,256]{2,1,0:T(8,128)(2,1)}, u32[]{:S(2)}) copy-start(bf16[1,256,256]{2,1,0:T(8,128)(2,1)} %param.9) | copy-start | bytes 393220
  1.2 8.9 %collective-permute-start.2 = (bf16[256,256]{1,0:T(8,128)(2,1)}, bf16[256,256]{1,0:T(8,128)(2,1)S(1)}, u32[]{:S(2)}, u32[]{:S(2)}) collective-permute-start(bf16[256,256]{1,0:T(8,128)(2,1)} %bitcast.3), channel_id=1, source_target_pairs={{0,12},{2,6},{4,0},{6,10},{8,4},{10,14},{12,8},{14,2},{1,13},{3,7}... | collective-permute-start | bytes 393224 | tf_op jit(solution)/shard_map/ppermute | solution.py:73
  5.8 8.3 %collective-permute-start.1 = (bf16[256,256]{1,0:T(8,128)(2,1)}, bf16[256,256]{1,0:T(8,128)(2,1)S(1)}, u32[]{:S(2)}, u32[]{:S(2)}) collective-permute-start(bf16[256,256]{1,0:T(8,128)(2,1)} %bitcast.4), channel_id=1, source_target_pairs={{0,2},{2,0},{4,6},{6,4},{8,10},{10,8},{12,14},{14,12},{1,3},{3,1},... | collective-permute-start | bytes 393224 | tf_op jit(solution)/shard_map/ppermute | solution.py:68
  5.8 8.6 %collective-permute-start = (bf16[256,256]{1,0:T(8,128)(2,1)}, bf16[256,256]{1,0:T(8,128)(2,1)S(1)}, u32[]{:S(2)}, u32[]{:S(2)}) collective-permute-start(bf16[256,256]{1,0:T(8,128)(2,1)} %bitcast.5), channel_id=1, source_target_pairs={{0,4},{2,14},{4,8},{6,2},{8,12},{10,6},{12,0},{14,10},{1,5},{3,15}... | collective-permute-start | bytes 393224 | tf_op jit(solution)/shard_map/ppermute | solution.py:73
  10.0 4.4 %collective-permute-start.3 = (bf16[256,256]{1,0:T(8,128)(2,1)S(1)}, bf16[256,256]{1,0:T(8,128)(2,1)S(1)}, u32[]{:S(2)}, u32[]{:S(2)}) collective-permute-start(bf16[256,256]{1,0:T(8,128)(2,1)S(1)} %collective-permute-done.2.rest_1_), channel_id=1, source_target_pairs={{0,1},{1,0},{2,3},{3,2},{4,5},{5,4},{6,7},{7,6},{8,9},{9,8},{10,11... | collective-permute-start | bytes 393224 | tf_op jit(solution)/shard_map/ppermute | solution.py:60
  10.0 6.2 %collective-permute-start.8 = (bf16[256,256]{1,0:T(8,128)(2,1)S(1)}, bf16[256,256]{1,0:T(8,128)(2,1)S(1)}, u32[]{:S(2)}, u32[]{:S(2)}) collective-permute-start(bf16[256,256]{1,0:T(8,128)(2,1)S(1)} %collective-permute-done.2.rest_1_), channel_id=1, source_target_pairs={{0,2},{2,0},{4,6},{6,4},{8,10},{10,8},{12,14},{14,12},{1,3},{3,1},... | collective-permute-start | bytes 393224 | tf_op jit(solution)/shard_map/ppermute | solution.py:68
  14.1 2.1 %collective-permute-start.5 = (bf16[256,256]{1,0:T(8,128)(2,1)S(1)}, bf16[256,256]{1,0:T(8,128)(2,1)S(1)}, u32[]{:S(2)}, u32[]{:S(2)}) collective-permute-start(bf16[256,256]{1,0:T(8,128)(2,1)S(1)} %bitcast.6), channel_id=1, source_target_pairs={{0,1},{1,0},{2,3},{3,2},{4,5},{5,4},{6,7},{7,6},{8,9},{9,8},{10,11... | collective-permute-start | bytes 393224 | tf_op jit(solution)/shard_map/ppermute | solution.py:60
  14.4 1.8 %collective-permute-start.6 = (bf16[256,256]{1,0:T(8,128)(2,1)S(1)}, bf16[256,256]{1,0:T(8,128)(2,1)S(1)}, u32[]{:S(2)}, u32[]{:S(2)}) collective-permute-start(bf16[256,256]{1,0:T(8,128)(2,1)S(1)} %collective-permute-done.rest_2_), channel_id=1, source_target_pairs={{0,1},{1,0},{2,3},{3,2},{4,5},{5,4},{6,7},{7,6},{8,9},{9,8},{10,11... | collective-permute-start | bytes 393224 | tf_op jit(solution)/shard_map/ppermute | solution.py:60
  14.7 1.5 %collective-permute-start.7 = (bf16[256,256]{1,0:T(8,128)(2,1)S(1)}, bf16[256,256]{1,0:T(8,128)(2,1)S(1)}, u32[]{:S(2)}, u32[]{:S(2)}) collective-permute-start(bf16[256,256]{1,0:T(8,128)(2,1)S(1)} %collective-permute-done.1.rest_3_), channel_id=1, source_target_pairs={{0,1},{1,0},{2,3},{3,2},{4,5},{5,4},{6,7},{7,6},{8,9},{9,8},{10,11... | collective-permute-start | bytes 393224 | tf_op jit(solution)/shard_map/ppermute | solution.py:60
  16.2 1.9 %collective-permute-start.9 = (bf16[256,256]{1,0:T(8,128)(2,1)S(1)}, bf16[256,256]{1,0:T(8,128)(2,1)S(1)}, u32[]{:S(2)}, u32[]{:S(2)}) collective-permute-start(bf16[256,256]{1,0:T(8,128)(2,1)S(1)} %collective-permute-done.8.near), channel_id=1, source_target_pairs={{0,1},{1,0},{2,3},{3,2},{4,5},{5,4},{6,7},{7,6},{8,9},{9,8},{10,11... | collective-permute-start | bytes 393224 | tf_op jit(solution)/shard_map/ppermute | solution.py:60
  19.5 1.6 %collective-permute-start.10 = (s16[272,256]{1,0:T(8,128)(2,1)S(1)}, s16[272,256]{1,0:T(8,128)(2,1)S(1)}, u32[]{:S(2)}, u32[]{:S(2)}) collective-permute-start(s16[272,256]{1,0:T(8,128)(2,1)S(1)} %get-tuple-element.37), channel_id=1, source_target_pairs={{0,1},{1,0},{2,3},{3,2},{4,5},{5,4},{6,7},{7,6},{8,9},{9,8},{10,11... | collective-permute-start | bytes 417800 | tf_op jit(solution)/shard_map/ppermute | solution.py:60
  21.2 3.0 %collective-permute-start.11 = (bf16[16,256,128]{2,1,0:T(8,128)(2,1)S(1)}, bf16[16,256,128]{2,1,0:T(8,128)(2,1)S(1)}, u32[]{:S(2)}, u32[]{:S(2)}) collective-permute-start(bf16[16,256,128]{2,1,0:T(8,128)(2,1)S(1)} %get-tuple-element.42.weighted.mine), channel_id=1, source_target_pairs={{0,1},{1,0},{2,3},{3,2},{4,5},{5,4},{6,7},{7,6},{8,9},{9,8},{10,11... | collective-permute-start | bytes 3145736 | tf_op jit(solution)/shard_map/ppermute | solution.py:60
  21.6 2.5 %collective-permute-start.14 = (s16[272,256]{1,0:T(8,128)(2,1)S(1)}, s16[272,256]{1,0:T(8,128)(2,1)S(1)}, u32[]{:S(2)}, u32[]{:S(2)}) collective-permute-start(s16[272,256]{1,0:T(8,128)(2,1)S(1)} %get-tuple-element.49), channel_id=1, source_target_pairs={{0,1},{1,0},{2,3},{3,2},{4,5},{5,4},{6,7},{7,6},{8,9},{9,8},{10,11... | collective-permute-start | bytes 417800 | tf_op jit(solution)/shard_map/ppermute | solution.py:60
  21.8 7.9 %collective-permute-start.12 = (s16[272,256]{1,0:T(8,128)(2,1)S(1)}, s16[272,256]{1,0:T(8,128)(2,1)S(1)}, u32[]{:S(2)}, u32[]{:S(2)}) collective-permute-start(s16[272,256]{1,0:T(8,128)(2,1)S(1)} %shard_map.73), channel_id=1, source_target_pairs={{0,2},{2,0},{4,6},{6,4},{8,10},{10,8},{12,14},{14,12},{1,3},{3,1},... | collective-permute-start | bytes 417800 | tf_op jit(solution)/shard_map/ppermute | solution.py:68
  24.4 10.0 %collective-permute-start.15 = (s16[272,256]{1,0:T(8,128)(2,1)S(1)}, s16[272,256]{1,0:T(8,128)(2,1)S(1)}, u32[]{:S(2)}, u32[]{:S(2)}) collective-permute-start(s16[272,256]{1,0:T(8,128)(2,1)S(1)} %shard_map.78), channel_id=1, source_target_pairs={{0,12},{2,6},{4,0},{6,10},{8,4},{10,14},{12,8},{14,2},{1,13},{3,7}... | collective-permute-start | bytes 417800 | tf_op jit(solution)/shard_map/ppermute | solution.py:73
  29.7 7.5 %collective-permute-start.13 = (s16[272,256]{1,0:T(8,128)(2,1)S(1)}, s16[272,256]{1,0:T(8,128)(2,1)S(1)}, u32[]{:S(2)}, u32[]{:S(2)}) collective-permute-start(s16[272,256]{1,0:T(8,128)(2,1)S(1)} %shard_map.76), channel_id=1, source_target_pairs={{0,4},{2,14},{4,8},{6,2},{8,12},{10,6},{12,0},{14,10},{1,5},{3,15}... | collective-permute-start | bytes 417800 | tf_op jit(solution)/shard_map/ppermute | solution.py:73
  29.8 7.4 %collective-permute-start.16 = (s16[272,256]{1,0:T(8,128)(2,1)S(1)}, s16[272,256]{1,0:T(8,128)(2,1)S(1)}, u32[]{:S(2)}, u32[]{:S(2)}) collective-permute-start(s16[272,256]{1,0:T(8,128)(2,1)S(1)} %get-tuple-element.50), channel_id=1, source_target_pairs={{0,2},{2,0},{4,6},{6,4},{8,10},{10,8},{12,14},{14,12},{1,3},{3,1},... | collective-permute-start | bytes 417800 | tf_op jit(solution)/shard_map/ppermute | solution.py:68
  37.7 1.3 %collective-permute-start.17 = (f32[136,128]{1,0:T(8,128)S(1)}, f32[136,128]{1,0:T(8,128)S(1)}, u32[]{:S(2)}, u32[]{:S(2)}) collective-permute-start(f32[136,128]{1,0:T(8,128)S(1)} %get-tuple-element.52), channel_id=1, source_target_pairs={{0,1},{1,0},{2,3},{3,2},{4,5},{5,4},{6,7},{7,6},{8,9},{9,8},{10,11... | collective-permute-start | bytes 208904 | tf_op jit(solution)/shard_map/ppermute | solution.py:60
  39.0 4.4 %collective-permute-start.18 = (f32[136,128]{1,0:T(8,128)S(1)}, f32[136,128]{1,0:T(8,128)S(1)}, u32[]{:S(2)}, u32[]{:S(2)}) collective-permute-start(f32[136,128]{1,0:T(8,128)S(1)} %add.15), channel_id=1, source_target_pairs={{0,2},{2,0},{4,6},{6,4},{8,10},{10,8},{12,14},{14,12},{1,3},{3,1},... | collective-permute-start | bytes 208904 | tf_op jit(solution)/shard_map/ppermute | solution.py:374
  43.4 6.8 %collective-permute-start.21 = (f32[136,128]{1,0:T(8,128)S(1)}, f32[136,128]{1,0:T(8,128)S(1)}, u32[]{:S(2)}, u32[]{:S(2)}) collective-permute-start(f32[136,128]{1,0:T(8,128)S(1)} %add.16), channel_id=1, source_target_pairs={{0,12},{2,14},{4,8},{6,10},{8,4},{10,6},{12,0},{14,2},{1,13},{3,15... | collective-permute-start | bytes 208904 | tf_op jit(solution)/shard_map/ppermute | solution.py:374
  45.5 6.4 %collective-permute-start.20 = (f32[136,128]{1,0:T(8,128)S(1)}, f32[136,128]{1,0:T(8,128)S(1)}, u32[]{:S(2)}, u32[]{:S(2)}) collective-permute-start(f32[136,128]{1,0:T(8,128)S(1)} %add.16), channel_id=1, source_target_pairs={{0,8},{2,10},{4,12},{6,14},{8,0},{10,2},{12,4},{14,6},{1,9},{3,11}... | collective-permute-start | bytes 208904 | tf_op jit(solution)/shard_map/ppermute | solution.py:374
  45.5 6.4 %collective-permute-start.19 = (f32[136,128]{1,0:T(8,128)S(1)}, f32[136,128]{1,0:T(8,128)S(1)}, u32[]{:S(2)}, u32[]{:S(2)}) collective-permute-start(f32[136,128]{1,0:T(8,128)S(1)} %add.16), channel_id=1, source_target_pairs={{0,4},{2,6},{4,0},{6,2},{8,12},{10,14},{12,8},{14,10},{1,5},{3,7},... | collective-permute-start | bytes 208904 | tf_op jit(solution)/shard_map/ppermute | solution.py:374
  52.0 1.3 %collective-permute-start.22 = (f32[136,128]{1,0:T(8,128)S(1)}, f32[136,128]{1,0:T(8,128)S(1)}, u32[]{:S(2)}, u32[]{:S(2)}) collective-permute-start(f32[136,128]{1,0:T(8,128)S(1)} %add_add_fusion.mine), channel_id=1, source_target_pairs={{0,1},{1,0},{2,3},{3,2},{4,5},{5,4},{6,7},{7,6},{8,9},{9,8},{10,11... | collective-permute-start | bytes 208904 | tf_op jit(solution)/shard_map/ppermute | solution.py:60
  (2 other events, 15.7 us)
